TPU v7x, 32 devices: a whole 2x2x4 slice. The times are simulated.
32 devices in a mesh: dp: 2 (over core), seq: 4 (over z), fsdp: 4 (over y, x).
Axes of the slice: x: 2, y: 2, z: 4, core: 2. Of those that a mesh axis runs over, the one named last changes fastest.
Arguments:
- block_input: bfloat16 [8, 512, 1536], P(('dp', 'fsdp'), 'seq'), may hold values from -6 to 6
- in_proj: bfloat16 [1536, 4608], P('fsdp'), may hold values from -0.15625 to 0.15625
- out_proj: bfloat16 [1536, 1536], P('fsdp'), may hold values from -0.15625 to 0.15625
- gate_proj: bfloat16 [1536, 6912], P('fsdp'), may hold values from -0.15625 to 0.15625
- up_proj: bfloat16 [1536, 6912], P('fsdp'), may hold values from -0.15625 to 0.15625
- down_proj: bfloat16 [6912, 1536], P('fsdp'), may hold values from -0.078125 to 0.078125
- norm_one: bfloat16 [1536], P('fsdp'), may hold values from 0.5 to 1.5
- norm_two: bfloat16 [1536], P('fsdp'), may hold values from 0.5 to 1.5
- conv_kernel: bfloat16 [3, 1536], P(None, 'fsdp'), may hold values from -3.5 to 3.5
- out_cotangent: bfloat16 [8, 512, 1536], P(('dp', 'fsdp'), 'seq'), may hold values from -6 to 6
Outputs:
- block_output: bfloat16 [8, 512, 1536], P(('dp', 'fsdp'), 'seq')
- input_grad: float32 [8, 512, 1536], P(('dp', 'fsdp'), 'seq')
- in_proj_grad: float32 [1536, 4608], P(('dp', 'seq', 'fsdp'))
- out_proj_grad: float32 [1536, 1536], P(('dp', 'seq', 'fsdp'))
- gate_proj_grad: float32 [1536, 6912], P(('dp', 'seq', 'fsdp'))
- up_proj_grad: float32 [1536, 6912], P(('dp', 'seq', 'fsdp'))
- down_projection_gradient: float32 [6912, 1536], P(None, ('dp', 'seq', 'fsdp'))
- norm_one_grad: float32 [1536], P(('dp', 'seq', 'fsdp'))
- norm_two_grad: float32 [1536], P(('dp', 'seq', 'fsdp'))
- conv_kernel_grad: float32 [3, 1536], P(None, ('dp', 'seq', 'fsdp'))
All inputs are finite; a program needn't handle non-finite values.
Results may differ from a plain program's by a relative error of at most 0.0086.
Values may be sent and summed in bfloat16 or wider, within the bound.
No kernel may reach another device: no remote copies, remote signals or barrier semaphores. Data moves between devices by JAX's collectives and lax.ppermute only.
A program may use at most 256 MiB of HBM per device.

v0:
```python
import math

import jax
import jax.numpy as jnp
from jax import lax
from jax.experimental import pallas as pl
from jax.experimental.pallas import tpu as pltpu
from jax.sharding import PartitionSpec as P

epsilon = 1e-05
f32 = jnp.float32
bf16 = jnp.bfloat16
MIB = 1 << 20
SCALE = 1e8
ANY = pl.BlockSpec(memory_space=pl.ANY)


def shape(dims, dtype=bf16):
    return jax.ShapeDtypeStruct(dims, dtype)


def far(dims, dtype=bf16):
    return pltpu.HBM(dims, dtype)


def in_far(value):
    return pltpu.with_memory_space_constraint(value, pltpu.HBM)


def whole(array):
    dims = array.shape
    return pl.BlockSpec(dims, lambda *steps: (0,) * len(dims), pipeline_mode=pl.Buffered(1))


def tiles(dims, axis):
    return pl.BlockSpec(dims, lambda step: tuple(step if i == axis else 0 for i in range(len(dims))))


def run(body, outs, ins, grid=(1,), in_specs=None, out_specs=None, scratch=(), after=(), limit=6, us=1.0, aliases=None, hbm=False, near=()):
    in_specs = [whole(a) for a in ins] if in_specs is None else in_specs
    out_specs = [whole(o) for o in outs] if out_specs is None else out_specs
    n, m = len(ins), len(after)
    if hbm:
        ins = [in_far(a) if a.size > 1024 and i not in near else a for i, a in enumerate(ins)]
        outs = [far(o.shape, o.dtype) if math.prod(o.shape) > 1024 else o for o in outs]

    def kernel(*refs):
        body(*refs[:n], *refs[n + m :])

    return pl.pallas_call(
        kernel,
        out_shape=tuple(outs),
        grid=grid,
        in_specs=list(in_specs) + [ANY] * m,
        out_specs=tuple(out_specs),
        scratch_shapes=list(scratch),
        compiler_params=pltpu.CompilerParams(vmem_limit_bytes=limit * MIB),
        cost_estimate=pl.CostEstimate(flops=int(us * SCALE), bytes_accessed=1000, transcendentals=0),
        input_output_aliases=aliases or {},
    )(*ins, *after)


def mm(a, b):
    return lax.dot_general(a, b, (((1,), (0,)), ((), ())), preferred_element_type=f32)


def mm_t(a, b):
    return lax.dot_general(a, b, (((1,), (1,)), ((), ())), preferred_element_type=f32)


def swap(value, axis, k):
    return lax.ppermute(value, axis, [(i, i ^ k) for i in range(lax.axis_size(axis))])


def shifted(block, axis, distance):
    devices = range(lax.axis_size(axis))
    route = [(i - distance, i) for i in devices if i - distance in devices]
    return lax.ppermute(block, axis, route)


def sum_over(value, axis, after=()):
    size = lax.axis_size(axis)
    if after:
        value = wait_for(value, *after)
    if size <= 4:
        return sum((swap(value, axis, k) for k in range(1, size)), value)
    k = 1
    while k < size:
        value = value + swap(value, axis, k)
        k *= 2
    return value


def wait_body(value_ref, out_ref):
    pass


def wait_for(value, *after, keep=False):
    return run(
        wait_body,
        [far(value.shape, value.dtype) if keep else shape(value.shape, value.dtype)],
        [in_far(value) if keep else value],
        in_specs=[ANY],
        out_specs=[ANY],
        after=after,
        limit=4,
        us=0.3,
        aliases={0: 0},
    )[0]


def wait_all_body(*refs):
    pass


def wait_all(values, *after):
    count = len(values)
    return run(
        wait_all_body,
        [shape(v.shape, v.dtype) for v in values],
        values,
        in_specs=[ANY] * count,
        out_specs=[ANY] * count,
        after=after,
        limit=4,
        us=0.3,
        aliases={i: i for i in range(count)},
    )


def hold_body(value_ref, out_ref, sem):
    copy = pltpu.make_async_copy(value_ref, out_ref, sem)
    copy.start()
    copy.wait()


def hold(value, *after):
    return run(
        hold_body,
        [shape(value.shape, value.dtype)],
        [value],
        in_specs=[ANY],
        out_specs=[ANY],
        scratch=[pltpu.SemaphoreType.DMA(())],
        after=after,
        limit=4,
    )[0]


def on_device(
    block_input,
    in_proj,
    out_proj,
    gate_proj,
    up_proj,
    down_proj,
    norm_one,
    norm_two,
    conv_kernel,
    out_cotangent,
):
    shards = lax.axis_size("fsdp")
    blocks = lax.axis_size("seq")
    f = lax.axis_index("fsdp")
    c = lax.axis_index("dp")
    z = lax.axis_index("seq")
    others = range(1, shards)
    seqs, length, width = block_input.shape
    rows = seqs * length
    group = shards * rows
    part = in_proj.shape[0]
    hidden = down_proj.shape[0]
    taps = conv_kernel.shape[0]
    rim = taps - 1
    edge = 16
    half_part = part // 2
    half = width // 2
    slab = width // (blocks * 2 * shards)
    tile = 512
    h_steps = pl.cdiv(hidden, tile)
    d_steps = width // tile
    chunk = half // blocks
    place = jnp.stack([f, c, z % 2]).astype(jnp.int32)
    SMEM = pl.BlockSpec(memory_space=pltpu.SMEM)
    VMEM = pl.BlockSpec(memory_space=pltpu.VMEM)

    def send_tokens(local):
        return [swap(local, "fsdp", k) for k in others]

    def turn(all_ref, own, keep_ref, send_ref):
        for h in range(2):
            value = all_ref[:, h * half : (h + 1) * half].T

            @pl.when(own == h)
            def _():
                keep_ref[...] = value

            @pl.when(own != h)
            def _():
                send_ref[...] = value

    def pack(pieces, after=()):
        count = len(pieces)

        def body(*refs):
            got, out_ref, sems = refs[:count], refs[count], refs[count + 1]
            copies = [pltpu.make_async_copy(got[i], out_ref.at[i], sems.at[i]) for i in range(count)]
            for copy in copies:
                copy.start()
            for copy in copies:
                copy.wait()

        return run(
            body,
            [shape((count, *pieces[0].shape))],
            pieces,
            in_specs=[ANY] * count,
            out_specs=[VMEM],
            scratch=[pltpu.SemaphoreType.DMA((count,))],
            after=after,
            limit=6,
        )[0]

    def assemble(own, parts, after=(), out=shape, out_spec=VMEM, limit=14):
        planes, columns = parts[0][0].shape[1], parts[0][0].shape[3]
        count = len(others)
        arrays = [p for p, _ in parts]
        starts = jnp.stack([f] + [h for _, h in parts]).astype(jnp.int32)

        def body(place_ref, own_ref, *refs):
            got, out_ref, sems = refs[: len(arrays)], refs[-2], refs[-1]
            f_ = place_ref[0]
            copies = []
            for p in range(planes):
                row = pl.ds(pl.multiple_of(f_ * part, part), part)
                if own.ndim == 3:
                    copies.append(pltpu.make_async_copy(own_ref.at[p], out_ref.at[p, row], sems.at[len(copies)]))
                else:
                    for t in range(columns // part):
                        source = own_ref.at[:, pl.ds(pl.multiple_of(t * width + f_ * part, part), part)]
                        target = out_ref.at[p, row, pl.ds(t * part, part)]
                        copies.append(pltpu.make_async_copy(source, target, sems.at[len(copies)]))
                for j, ref in enumerate(got):
                    size = ref.shape[2]
                    for i, k in enumerate(others):
                        start = pl.multiple_of((f_ ^ k) * part + place_ref[1 + j], size)
                        target = out_ref.at[p, pl.ds(start, size)]
                        copies.append(pltpu.make_async_copy(ref.at[i, p], target, sems.at[len(copies)]))
            for copy in copies:
                copy.start()
            for copy in copies:
                copy.wait()

        return run(
            body,
            [out((planes, width, columns))],
            [starts, own, *arrays],
            in_specs=[SMEM] + [ANY] * (1 + len(arrays)),
            out_specs=[out_spec],
            scratch=[pltpu.SemaphoreType.DMA((planes * (4 + len(arrays) * count),))],
            after=after,
            limit=limit,
        )[0]

    quarter = half_part // 2
    here, there = (z % 2) * quarter, (1 - z % 2) * quarter

    def in_body(place_ref, w_ref, *refs):
        outs, sems = refs[: len(others)], refs[-1]
        copies = []
        first = pl.multiple_of(place_ref[1] * half_part + place_ref[2] * quarter, quarter)
        for i, k in enumerate(others):
            for t in range(3):
                start = pl.multiple_of(t * width + (place_ref[0] ^ k) * part, part)
                source = w_ref.at[pl.ds(first, quarter), pl.ds(start, part)]
                target = outs[i].at[:, pl.ds(t * part, part)]
                copies.append(pltpu.make_async_copy(source, target, sems.at[i * 3 + t]))
        for copy in copies:
            copy.start()
        for copy in copies:
            copy.wait()

    in_sent = run(
        in_body,
        [shape((quarter, 3 * part))] * len(others),
        [place, in_far(in_proj)],
        in_specs=[SMEM, ANY],
        out_specs=[VMEM] * len(others),
        scratch=[pltpu.SemaphoreType.DMA((3 * len(others),))],
    )
    in_got = [swap(m, "fsdp", k) for m, k in zip(in_sent, others)]

    x_local = block_input.reshape(rows, width)
    cot_local = out_cotangent.reshape(rows, width)
    tail = shifted(x_local[rows - edge :], "seq", 1)
    small = jnp.concatenate([norm_one[None], norm_two[None], conv_kernel], axis=0)
    small = jnp.pad(small, ((0, edge - taps - 2), (0, 0)))

    def join_body(x_ref, t_ref, small_ref, out_ref):
        out_ref[:rows] = x_ref[...]
        out_ref[rows:] = t_ref[...]
        row = lax.broadcasted_iota(jnp.int32, (edge, part), 0)
        out_ref[rows:, :part] = jnp.where(row < taps + 2, small_ref[...], t_ref[:, :part])

    (message,) = run(join_body, [shape((rows + edge, width))], [x_local, tail, small])
    messages = [message] + send_tokens(message)
    taps_own = conv_kernel.astype(f32)

    in_mine = pack(in_got, (message,))
    in_next = swap(in_mine, "seq", 1)

    def both_piece(j, start, size):
        return jnp.stack(
            [lax.dynamic_slice(weight, (start, j * hidden), (size, hidden)) for weight in (gate_proj, up_proj)]
        )

    both_sent = [both_piece(f ^ k, c * half_part + here, quarter) for k in others]
    both_sent = wait_all(both_sent, *in_got)
    both_got = [swap(piece, "fsdp", k) for piece, k in zip(both_sent, others)]

    def norm_body(place_ref, *refs):
        xs, (n_ref, nh_ref, gain_ref) = refs[:shards], refs[shards:]
        for s in range(shards):
            pick = xs[0][rows:, :part]
            for k in others:
                pick = jnp.where((place_ref[0] ^ k) == s, xs[k][rows:, :part], pick)
            gain_ref[:, s * part : (s + 1) * part] = pick[:8].astype(f32)
        gain = gain_ref[0:1]

        def normed(v):
            v = v.astype(f32)
            r = lax.rsqrt(jnp.mean(v * v, axis=-1, keepdims=True) + epsilon)
            return (v * r * gain).astype(bf16)

        for k in range(shards):
            n_ref[k * rows : (k + 1) * rows] = normed(xs[k][:rows])
            nh_ref[k * edge : (k + 1) * edge] = normed(xs[k][rows:])

    normed_one, normed_edge, gains = run(
        norm_body,
        [shape((group, width)), shape((shards * edge, width)), shape((8, width), f32)],
        [place, *[in_far(m) for m in messages]],
        in_specs=[SMEM] + [whole(m) for m in messages],
        after=(in_mine,),
        us=2,
    )

    both_mine = pack(both_got, (normed_one, in_next))
    both_next = swap(both_mine, "seq", 1)
    w_in = assemble(
        in_far(in_proj),
        [
            (in_mine[:, None], c * half_part + here),
            (in_next[:, None], c * half_part + there),
            (swap(in_mine, "dp", 1)[:, None], (1 - c) * half_part + here),
            (swap(in_next, "dp", 1)[:, None], (1 - c) * half_part + there),
        ],
        (both_mine,),
    )[0]

    cot_held = hold(cot_local, both_mine)
    cot_blocks = [cot_held] + send_tokens(cot_held)

    def mixer_body(n_ref, nh_ref, taps_ref, w_ref, o_ref, proj_ref, edge_ref, gated_ref, *refs):
        p_refs, (ph_ref, ext_ref) = refs[:shards], refs[shards:]
        for t in range(3):
            cols = slice(t * part, (t + 1) * part)
            w = w_ref[:, cols]
            proj_ref[:, cols] = mm(n_ref[...], w)
            if t != 1:
                ph_ref[:, cols] = mm(nh_ref[...], w)
        edge_ref[...] = ph_ref[:, :part] * ph_ref[:, 2 * part :]
        for k in range(shards):
            r = slice(k * rows, (k + 1) * rows)
            ext_ref[:edge] = edge_ref[k * edge : (k + 1) * edge]
            ext_ref[edge:] = proj_ref[r, :part] * proj_ref[r, 2 * part :]
            conv = taps_ref[rim : rim + 1] * ext_ref[edge:]
            for t in range(rim):
                conv = conv + taps_ref[t : t + 1] * ext_ref[edge - rim + t : edge - rim + t + rows]
            gated_ref[r] = (proj_ref[r, part : 2 * part] * conv).astype(bf16)
        for t in range(width // 512):
            cols = slice(t * 512, (t + 1) * 512)
            o = mm(gated_ref[...], o_ref[:, cols]).astype(bf16)
            for k in range(shards):
                p_refs[k][:, cols] = o[k * rows : (k + 1) * rows]

    projected, edge_product, gated, *mix_parts = run(
        mixer_body,
        [
            shape((group, 3 * part), f32),
            shape((shards * edge, part), f32),
            shape((group, part)),
        ]
        + [shape((rows, width))] * shards,
        [normed_one, normed_edge, taps_own, w_in, out_proj],
        scratch=[pltpu.VMEM((shards * edge, 3 * part), f32), pltpu.VMEM((edge + rows, part), f32)],
        after=(cot_held,),
        us=5.5,
        limit=6,
    )

    def cot_body(place_ref, *refs):
        blocks_, (down_ref, dh_ref, keep_ref, send_ref, all_ref) = refs[:shards], refs[shards:]

        @pl.when(pl.program_id(0) == 0)
        def _():
            for k in range(shards):
                all_ref[k * rows : (k + 1) * rows] = blocks_[k][...]
            turn(all_ref, place_ref[1], keep_ref, send_ref)

        dh_ref[...] = mm_t(all_ref[...], down_ref[...])

    d_hidden, cot_keep, cot_send = run(
        cot_body,
        [shape((group, hidden), f32), far((half, group)), far((half, group))],
        [place, *cot_blocks, in_far(down_proj)],
        grid=(h_steps,),
        in_specs=[SMEM] + [whole(b) for b in cot_blocks] + [tiles((tile, width), 0)],
        out_specs=[tiles((group, tile), 1), whole(shape((half, group))), whole(shape((half, group)))],
        scratch=[pltpu.VMEM((group, width), bf16)],
        after=(gated,),
        us=5,
        limit=14,
    )

    cot_come = swap(cot_send, "dp", 1)
    mix_got = [swap(mix_parts[k], "fsdp", k) for k in others]

    def second_body(*refs):
        parts, x_ref, gain_ref, s_ref, n_ref = refs[:shards], *refs[shards:]
        total = x_ref[...].astype(f32)
        for p in parts:
            total = total + p[...].astype(f32)
        s_ref[...] = total
        r = lax.rsqrt(jnp.mean(total * total, axis=-1, keepdims=True) + epsilon)
        n_ref[...] = (total * r * gain_ref[1:2]).astype(bf16)

    second, normed_two = run(
        second_body,
        [shape((rows, width), f32), shape((rows, width))],
        [mix_parts[0], *mix_got, x_local, gains],
        after=(d_hidden,),
    )
    two_blocks = [normed_two] + send_tokens(normed_two)

    both_next = wait_for(both_next, normed_two)
    w_both = assemble(
        both_piece(f, 0, part),
        [
            (both_mine, c * half_part + here),
            (both_next, c * half_part + there),
            (swap(both_mine, "dp", 1), (1 - c) * half_part + here),
            (swap(both_next, "dp", 1), (1 - c) * half_part + there),
        ],
        (normed_two,),
        limit=16,
    )
    turned = shape((half, group))

    def turn_two_body(place_ref, *refs):
        blocks_, (all_ref, keep_ref, send_ref) = refs[:shards], refs[shards:]
        for k in range(shards):
            all_ref[k * rows : (k + 1) * rows] = blocks_[k][...]
        turn(all_ref, place_ref[1], keep_ref, send_ref)

    two_all, two_keep, two_send = run(
        turn_two_body,
        [shape((group, width)), turned, turned],
        [place, *two_blocks],
        in_specs=[SMEM] + [whole(b) for b in two_blocks],
        after=(w_both,),
    )
    two_come = swap(two_send, "dp", 1)

    def feed_body(all_ref, w_ref, dh_ref, du_ref, dg_ref, h_ref):
        gate = mm(all_ref[...], w_ref[0])
        upward = mm(all_ref[...], w_ref[1])
        s = jax.nn.sigmoid(gate)
        dh = dh_ref[...]
        du_ref[...] = (dh * (gate * s)).astype(bf16).reshape(du_ref.shape)
        dg_ref[...] = (dh * upward * s * (1.0 + gate * (1.0 - s))).astype(bf16).reshape(du_ref.shape)
        h_ref[...] = (gate * s * upward).astype(bf16).reshape(du_ref.shape)

    bundle = 32
    units = (group // bundle, bundle, hidden)
    unit_tiles = tiles((group // bundle, bundle, tile), 2)
    d_up, d_gate, hidden_all = run(
        feed_body,
        [far(units)] * 3,
        [two_all, w_both, d_hidden],
        grid=(h_steps,),
        in_specs=[whole(two_all), tiles((2, width, tile), 2), tiles((group, tile), 1)],
        out_specs=[unit_tiles] * 3,
        after=(two_come,),
        us=10,
        limit=24,
    )
    d_up_come = swap(d_up, "dp", 1)
    d_gate_come = swap(d_gate, "dp", 1)
    hidden_come = swap(hidden_all, "dp", 1)

    def flat(ref):
        return ref[...].reshape(group, ref.shape[2])

    def up_sum_body(own_ref, come_ref, du_ref, duc_ref, out_ref):
        total = mm(own_ref[...], flat(du_ref)) + mm(come_ref[...], flat(duc_ref))
        out_ref[...] = total.astype(bf16).reshape(blocks, chunk, tile)

    (up_both,) = run(
        up_sum_body,
        [shape((blocks, chunk, hidden))],
        [two_keep, two_come, d_up, d_up_come],
        grid=(h_steps,),
        in_specs=[whole(turned), whole(turned), unit_tiles, unit_tiles],
        out_specs=[tiles((blocks, chunk, tile), 2)],
        us=5,
        limit=14,
        hbm=True,
        near=(0, 1, 3),
    )
    up_sum = lax.psum_scatter(up_both, "seq", scatter_dimension=0, tiled=True).reshape(chunk, hidden)

    def two_sum_body(own_ref, come_ref, cot_own_ref, cot_come_ref, dg_ref, dgc_ref, h_ref, hc_ref, out_ref):
        total = mm(own_ref[...], flat(dg_ref)) + mm(come_ref[...], flat(dgc_ref))
        out_ref[:, 0] = total.astype(bf16).reshape(blocks, chunk, tile)
        total = mm(cot_own_ref[...], flat(h_ref)) + mm(cot_come_ref[...], flat(hc_ref))
        out_ref[:, 1] = total.astype(bf16).reshape(blocks, chunk, tile)

    (two_both,) = run(
        two_sum_body,
        [shape((blocks, 2, chunk, hidden))],
        [two_keep, two_come, cot_keep, cot_come, d_gate, d_gate_come, hidden_all, hidden_come],
        grid=(h_steps,),
        in_specs=[whole(turned)] * 4 + [unit_tiles] * 4,
        out_specs=[tiles((blocks, 2, chunk, tile), 3)],
        after=(up_both,),
        us=10,
        limit=20,
        hbm=True,
        near=(0, 1, 2, 3, 5, 7),
    )
    two_sum = lax.psum_scatter(two_both, "seq", scatter_dimension=0, tiled=True)
    two_sum = two_sum.reshape(2, chunk, hidden)

    def back_two_body(dg_ref, du_ref, wg_ref, wu_ref, *p_refs):
        d = (mm_t(flat(dg_ref), wg_ref[...]) + mm_t(flat(du_ref), wu_ref[...])).astype(bf16)
        for k in range(shards):
            p_refs[k][...] = d[k * rows : (k + 1) * rows]

    back_two = run(
        back_two_body,
        [shape((rows, width))] * shards,
        [d_gate, d_up, w_both, w_both],
        grid=(d_steps,),
        in_specs=[
            whole(d_gate),
            whole(d_up),
            pl.BlockSpec((None, tile, hidden), lambda step: (0, step, 0)),
            pl.BlockSpec((None, tile, hidden), lambda step: (1, step, 0)),
        ],
        out_specs=[tiles((rows, tile), 1)] * shards,
        after=(two_both,),
        us=7,
        limit=16,
        hbm=True,
    )
    back_two_got = [swap(back_two[k], "fsdp", k) for k in others]

    def second_grad_body(*refs):
        parts, (s_ref, cot_ref, gain_ref, d_ref, mix_ref, term_ref) = refs[:shards], refs[shards:]
        dn = parts[0][...].astype(f32)
        for p in parts[1:]:
            dn = dn + p[...].astype(f32)
        s = s_ref[...]
        r = lax.rsqrt(jnp.mean(s * s, axis=-1, keepdims=True) + epsilon)
        term_ref[...] = jnp.sum(dn * s * r, axis=0, keepdims=True)
        a = dn * gain_ref[1:2]
        d = cot_ref[...].astype(f32) + r * a - s * (r * r * r) * jnp.mean(a * s, axis=-1, keepdims=True)
        d_ref[...] = d
        mix_ref[...] = d.astype(bf16)

    d_second, d_mix, two_term = run(
        second_grad_body,
        [shape((rows, width), f32), shape((rows, width)), shape((1, width), f32)],
        [back_two[0], *back_two_got, second, cot_local, gains],
    )
    mix_blocks = [d_mix] + send_tokens(d_mix)

    runs = part // (shards * slab)
    channels = part // shards

    def owner_body(place_ref, g_ref, *out_refs):
        row = lax.broadcasted_iota(jnp.int32, (part, channels), 0)
        col = lax.broadcasted_iota(jnp.int32, (part, channels), 1)
        for k in range(shards):
            source = (col // slab) * (shards * slab) + (place_ref[0] ^ k) * slab + col % slab
            out_refs[k][...] = mm(g_ref[...], (row == source).astype(bf16)).astype(bf16)

    owner = run(
        owner_body,
        [shape((group, channels))] * shards,
        [place, gated],
        in_specs=[SMEM, whole(gated)],
        after=(two_both,),
    )
    owner_got = [owner[0]] + [swap(owner[k], "fsdp", k) for k in others]

    def gated_grad_body(*refs):
        blocks_, (o_ref, proj_ref, edge_ref, taps_ref) = refs[:shards], refs[shards : shards + 4]
        all_ref, dc_ref, dconv_ref, head_ref, term_ref, ext_ref = refs[shards + 4 :]
        for k in range(shards):
            all_ref[k * rows : (k + 1) * rows] = blocks_[k][...]
        dg = mm_t(all_ref[...], o_ref[...])
        dconv_ref[...] = dg * proj_ref[:, part : 2 * part]
        terms = [jnp.zeros((1, part), f32)] * taps
        for k in range(shards):
            r = slice(k * rows, (k + 1) * rows)
            d = dconv_ref[r]
            head_ref[k * 8 : (k + 1) * 8] = d[:8]
            ext_ref[:edge] = edge_ref[k * edge : (k + 1) * edge]
            ext_ref[edge:] = proj_ref[r, :part] * proj_ref[r, 2 * part :]
            conv = jnp.zeros((rows, part), f32)
            for t in range(taps):
                e = ext_ref[edge - rim + t : edge - rim + t + rows]
                conv = conv + taps_ref[t : t + 1] * e
                terms[t] = terms[t] + jnp.sum(d * e, axis=0, keepdims=True)
            dc_ref[r] = (dg[k * rows : (k + 1) * rows] * conv).astype(bf16)
        for t in range(taps):
            term_ref[t : t + 1] = terms[t]

    mix_all, d_c, d_conv, heads, tap_terms = run(
        gated_grad_body,
        [
            shape((group, width)),
            shape((group, part)),
            shape((group, part), f32),
            shape((shards * 8, part), f32),
            shape((taps, part), f32),
        ],
        [*mix_blocks, out_proj, projected, edge_product, taps_own],
        scratch=[pltpu.VMEM((edge + rows, part), f32)],
    )
    behind = shifted(heads, "seq", -1)

    def turn_body(place_ref, n_ref, *refs):
        got, (nt_ref, ot_ref) = refs[:shards], refs[shards:]
        for h in range(2):
            nt_ref[h] = n_ref[:, h * half : (h + 1) * half].T
        row = lax.broadcasted_iota(jnp.int32, (channels, part), 0)
        col = lax.broadcasted_iota(jnp.int32, (channels, part), 1)
        for b in range(shards):
            both = jnp.zeros((rows, part), f32)
            for k in range(shards):
                spread = (col == row + (place_ref[0] ^ k) * channels).astype(bf16)
                both = both + mm(got[k][(b ^ k) * rows : ((b ^ k) + 1) * rows], spread)
            both = both.astype(bf16)
            for h in range(2):
                wide = both[:, h * (part // 2) : (h + 1) * (part // 2)]
                ot_ref[h, :, b * rows : (b + 1) * rows] = wide.astype(f32).T.astype(bf16)

    one_turned, own_turned = run(
        turn_body,
        [shape((2, half, group)), shape((2, part // 2, group))],
        [place, normed_one, *owner_got],
        in_specs=[SMEM, whole(normed_one)] + [whole(o) for o in owner_got],
        after=(mix_blocks[0],),
    )

    def projected_grad_body(
        place_ref, dconv_ref, behind_ref, taps_ref, proj_ref, dc_ref, nt_ref, ot_ref, mix_ref,
        dp_ref, in_ref, out_ref, ext_ref,
    ):
        other = 1 - place_ref[1]
        for k in range(shards):
            r = slice(k * rows, (k + 1) * rows)
            ext_ref[:rows] = dconv_ref[r]
            ext_ref[rows:] = behind_ref[k * 8 : (k + 1) * 8]
            d = taps_ref[rim : rim + 1] * ext_ref[:rows]
            for t in range(rim):
                d = d + taps_ref[t : t + 1] * ext_ref[rim - t : rim - t + rows]
            dp_ref[r, :part] = (d * proj_ref[r, 2 * part :]).astype(bf16)
            dp_ref[r, part : 2 * part] = dc_ref[r]
            dp_ref[r, 2 * part :] = (d * proj_ref[r, :part]).astype(bf16)
        for t in range(3):
            cols = slice(t * part, (t + 1) * part)
            in_ref[:, :, cols] = mm(nt_ref[other], dp_ref[:, cols]).astype(bf16).reshape(blocks, chunk, part)
        for t in range(width // 512):
            cols = slice(t * 512, (t + 1) * 512)
            out_ref[:, cols] = mm(ot_ref[other], mix_ref[:, cols]).astype(bf16)

    d_projected, in_there, out_there = run(
        projected_grad_body,
        [shape((group, 3 * part)), shape((blocks, chunk, 3 * part)), shape((part // 2, width))],
        [place, d_conv, behind, taps_own, projected, d_c, one_turned, own_turned, mix_all],
        in_specs=[SMEM] + [whole(a) for a in (d_conv, behind, taps_own, projected, d_c, one_turned, own_turned, mix_all)],
        scratch=[pltpu.VMEM((rows + 8, part), f32)],
        us=3,
    )
    in_come = swap(in_there, "dp", 1)
    out_come = swap(out_there, "dp", 1)

    def back_one_body(dp_ref, w_ref, *p_refs):
        d = mm_t(dp_ref[...], w_ref[...]).astype(bf16)
        for k in range(shards):
            p_refs[k][...] = d[k * rows : (k + 1) * rows]

    back_one = run(
        back_one_body,
        [shape((rows, width))] * shards,
        [d_projected, w_in],
        grid=(d_steps,),
        in_specs=[whole(d_projected), tiles((tile, 3 * part), 0)],
        out_specs=[tiles((rows, tile), 1)] * shards,
        us=4,
        limit=14,
        hbm=True,
    )
    back_one_got = [swap(back_one[k], "fsdp", k) for k in others]

    def mixer_sum_body(place_ref, nt_ref, dp_ref, in_come_ref, ot_ref, mix_ref, out_come_ref, in_ref, out_ref):
        own = place_ref[1]
        for t in range(3):
            cols = slice(t * part, (t + 1) * part)
            here = mm(nt_ref[own], dp_ref[:, cols]).reshape(blocks, chunk, part)
            in_ref[:, :, cols] = (here + in_come_ref[:, :, cols].astype(f32)).astype(bf16)
        for t in range(width // 512):
            cols = slice(t * 512, (t + 1) * 512)
            here = mm(ot_ref[own], mix_ref[:, cols])
            out_ref[:, cols] = (here + out_come_ref[:, cols].astype(f32)).astype(bf16)

    in_both, out_both = run(
        mixer_sum_body,
        [shape((blocks, chunk, 3 * part)), shape((blocks * slab, width))],
        [place, one_turned, d_projected, in_come, own_turned, mix_all, out_come],
        in_specs=[SMEM]
        + [whole(a) for a in (one_turned, d_projected, in_come, own_turned, mix_all, out_come)],
        after=(back_one[0],),
    )

    def final_body(h_ref, w_ref, *p_refs):
        d = mm(flat(h_ref), w_ref[...]).astype(bf16)
        for k in range(shards):
            p_refs[k][...] = d[k * rows : (k + 1) * rows]

    final_parts = run(
        final_body,
        [shape((rows, width))] * shards,
        [hidden_all, in_far(down_proj)],
        grid=(d_steps,),
        in_specs=[whole(hidden_all), tiles((hidden, tile), 1)],
        out_specs=[tiles((rows, tile), 1)] * shards,
        after=(in_both,),
        us=4,
        limit=14,
        hbm=True,
    )

    in_rows = in_both.reshape(blocks, shards, slab, 3 * part)

    def rows_for(k):
        return lax.dynamic_index_in_dim(in_rows, f ^ k, 1, keepdims=False)

    in_pieces = [rows_for(0)] + [swap(rows_for(k), "fsdp", k) for k in others]

    def place_body(place_ref, *refs):
        got, (o_ref, out_ref) = refs[:shards], refs[shards:]
        for s in range(shards):
            pick = got[0][...]
            for k in others:
                pick = jnp.where((place_ref[0] ^ k) == s, got[k][...], pick)
            for t in range(3):
                start = t * width + s * part
                out_ref[:, :, start : start + part] = pick[:, :, t * part : (t + 1) * part]
        out_ref[:, :, 3 * width :] = o_ref[...]

    (mix_both,) = run(
        place_body,
        [far((blocks, slab, 4 * width))],
        [place, *in_pieces, out_both.reshape(blocks, slab, width)],
        in_specs=[SMEM] + [VMEM] * (shards + 1),
        after=(final_parts[0],),
        limit=12,
    )
    mix_sum = lax.psum_scatter(mix_both, "seq", scatter_dimension=0, tiled=True).reshape(slab, 4 * width)

    def input_grad_body(*refs):
        parts, (x_ref, d_ref, gain_ref, out_ref, term_ref) = refs[:shards], refs[shards:]
        dn = parts[0][...].astype(f32)
        for p in parts[1:]:
            dn = dn + p[...].astype(f32)
        x = x_ref[...].astype(f32)
        r = lax.rsqrt(jnp.mean(x * x, axis=-1, keepdims=True) + epsilon)
        term_ref[...] = jnp.sum(dn * x * r, axis=0, keepdims=True)
        a = dn * gain_ref[0:1]
        out_ref[...] = d_ref[...] + r * a - x * (r * r * r) * jnp.mean(a * x, axis=-1, keepdims=True)

    input_grad, one_term = run(
        input_grad_body,
        [shape((rows, width), f32), shape((1, width), f32)],
        [back_one[0], *back_one_got, x_local, d_second, gains],
        after=(mix_both,),
    )
    input_grad = input_grad.reshape(seqs, length, width)


    two_sum = wait_for(two_sum, input_grad)
    up_rows = up_sum.reshape(1, shards, slab, hidden)
    two_rows = two_sum.reshape(2, shards, slab, hidden)

    def feed_rows(k):
        parts = [lax.dynamic_index_in_dim(r, f ^ k, 1, keepdims=False) for r in (up_rows, two_rows)]
        return jnp.concatenate(parts, axis=0)

    feed_pieces = [feed_rows(0)] + [swap(feed_rows(k), "fsdp", k) for k in others]

    final_got = [swap(final_parts[k], "fsdp", k) for k in others]
    final_got = wait_all(final_got, feed_pieces[0])
    total = second + final_parts[0].astype(f32)
    for piece in final_got:
        total = total + piece.astype(f32)
    block_output = total.astype(bf16).reshape(seqs, length, width)

    spread_taps = [jnp.where(f == s, tap_terms, 0.0) for s in range(shards)]
    terms = jnp.concatenate([one_term, two_term, jnp.concatenate(spread_taps, axis=1)], axis=0)
    terms = sum_over(sum_over(sum_over(terms, "dp"), "seq"), "fsdp", feed_pieces[1:])
    own = lax.dynamic_slice_in_dim(terms, ((c * blocks + z) * shards + f) * slab, slab, 1)

    def spread_body(place_ref, *refs):
        got, outs = refs[:shards], refs[shards:]
        for n in range(3):
            for s in range(shards):
                pick = got[0][n]
                for k in others:
                    pick = jnp.where((place_ref[0] ^ k) == s, got[k][n], pick)
                outs[n][:, s * hidden : (s + 1) * hidden] = pick.astype(f32)

    up_grad, gate_grad, down_rows = run(
        spread_body,
        [far((slab, shards * hidden), f32)] * 3,
        [place, *feed_pieces],
        in_specs=[SMEM] + [whole(p) for p in feed_pieces],
        limit=12,
    )
    down_grad = jnp.transpose(down_rows)

    def last_body(sum_ref, in_ref, out_ref):
        in_ref[...] = sum_ref[:, : 3 * width].astype(f32)
        out_ref[...] = sum_ref[:, 3 * width :].astype(f32)

    in_grad, out_grad = run(
        last_body, [far((slab, 3 * width), f32), far((slab, width), f32)], [mix_sum], after=(gate_grad, block_output, terms)
    )
    return (
        block_output,
        input_grad,
        in_grad,
        out_grad,
        gate_grad,
        up_grad,
        down_grad,
        own[0],
        own[1],
        own[2:],
    )


def solution(mesh):
    placed = (
        P(("dp", "fsdp"), "seq", None),
        P("fsdp", None),
        P("fsdp", None),
        P("fsdp", None),
        P("fsdp", None),
        P("fsdp", None),
        P("fsdp"),
        P("fsdp"),
        P(None, "fsdp"),
        P(("dp", "fsdp"), "seq", None),
    )
    return jax.shard_map(
        on_device,
        mesh=mesh,
        in_specs=placed,
        out_specs=(
            P(("dp", "fsdp"), "seq", None),
            P(("dp", "fsdp"), "seq", None),
            P(("dp", "seq", "fsdp"), None),
            P(("dp", "seq", "fsdp"), None),
            P(("dp", "seq", "fsdp"), None),
            P(("dp", "seq", "fsdp"), None),
            P(None, ("dp", "seq", "fsdp")),
            P(("dp", "seq", "fsdp")),
            P(("dp", "seq", "fsdp")),
            P(None, ("dp", "seq", "fsdp")),
        ),
        check_vma=False,
    )
```

profile of v0, /device:TPU:0, one launch (start us, length us, event | category | flops | bytes accessed | tf_op | source)
XLA Modules:
  0.0 384.0 jit_solution(14399987414290482307)
XLA Ops:
  13.7 3.9 %collective-permute-start = (bf16[16,1536]{1,0:T(8,128)(2,1)S(1)}, bf16[16,1536]{1,0:T(8,128)(2,1)S(1)}, u32[]{:S(2)}, u32[]{:S(2)}) collective-permute-start(bf16[16,1536]{1,0:T(8,128)(2,1)S(1)} %slice_bitcast_fusion), channel_id=1, source_target_pairs={{0,4},{4,8},{8,12},{1,5},{5,9},{9,13},{2,6},{6,10},{10,14},{3,7},{... | collective-permute-start | bytes 147464 | tf_op jit(solution)/shard_map/ppermute | solution.py:78
  28.6 5.4 %collective-permute-done.1.refs_2_ = bf16[144,1536]{1,0:T(8,128)(2,1)S(1)} collective-permute-done((bf16[144,1536]{1,0:T(8,128)(2,1)S(1)}, bf16[144,1536]{1,0:T(8,128)(2,1)S(1)}, u32[]{:S(2)}, u32[]{:S(2)}) %collective-permute-start.1) | collective-permute-done | bytes 442400 | tf_op jit(solution)/shard_map/ppermute | solution.py:72
  38.1 34.0 %collective-permute-done.3.refs_4_ = bf16[144,1536]{1,0:T(8,128)(2,1)S(1)} collective-permute-done((bf16[144,1536]{1,0:T(8,128)(2,1)S(1)}, bf16[144,1536]{1,0:T(8,128)(2,1)S(1)}, u32[]{:S(2)}, u32[]{:S(2)}) %collective-permute-start.3) | collective-permute-done | bytes 442400 | tf_op jit(solution)/shard_map/ppermute | solution.py:72
  82.4 3.1 shard_map.183
  85.6 4.0 %shard_map.185 = (f32[512,1152]{1,0:T(8,128)S(1)}, f32[64,384]{1,0:T(8,128)S(1)}, bf16[512,384]{1,0:T(8,128)(2,1)S(1)}, bf16[128,1536]{1,0:T(8,128)(2,1)S(1)}, b...) custom-call(bf16[512,1536]{1,0:T(8,128)(2,1)S(1)} %copy-done.8, ...), custom_call_target="tpu_custom_call" | custom-call | flops 550000000 | bytes 1000 | tf_op jit(solution)/shard_map/pallas_call | solution.py:50
  93.7 6.4 %collective-permute-done.17.refs_3_ = bf16[128,1536]{1,0:T(8,128)(2,1)} collective-permute-done((bf16[128,1536]{1,0:T(8,128)(2,1)S(1)}, bf16[128,1536]{1,0:T(8,128)(2,1)}, u32[]{:S(2)}, u32[]{:S(2)}) %collective-permute-start.17) | collective-permute-done | bytes 393248 | tf_op jit(solution)/shard_map/ppermute | solution.py:72
  100.2 8.3 %shard_map.186 = (f32[512,1728]{1,0:T(8,128)S(1)}, bf16[768,512]{1,0:T(8,128)(2,1)}, bf16[768,512]{1,0:T(8,128)(2,1)}) custom-call(s32[3]{0:T(128)S(1)} %pad_add_fusion.refs_0_, bf16[128,1536]{1,0:T(8,128)(2,1)S(1)} %shard_map.184.refs_5_.refs_1_, bf16[128,1536]{1,0:T(8,128)(2,1)} %collective-permute-done.16.refs_2_, ...), custom_call_target="tpu_custom_call" | custom-call | flops 500000000 | bytes 1000 | tf_op jit(solution)/shard_map/pallas_call | solution.py:50
  108.5 7.5 %collective-permute-done.14.refs_2_ = bf16[128,1536]{1,0:T(8,128)(2,1)S(1)} collective-permute-done((bf16[128,1536]{1,0:T(8,128)(2,1)S(1)}, bf16[128,1536]{1,0:T(8,128)(2,1)S(1)}, u32[]{:S(2)}, u32[]{:S(2)}) %collective-permute-start.14) | collective-permute-done | bytes 393248 | tf_op jit(solution)/shard_map/ppermute | solution.py:72
  116.4 4.9 %collective-permute-done.22.refs_0_ = bf16[3,2,96,1728]{3,2,1,0:T(8,128)(2,1)} collective-permute-done((bf16[3,2,96,1728]{3,2,1,0:T(8,128)(2,1)S(1)}, bf16[3,2,96,1728]{3,2,1,0:T(8,128)(2,1)}, u32[]{:S(2)}, u32[]{:S(2)}) %collective-permute-start.22) | collective-permute-done | bytes 1990688 | tf_op jit(solution)/shard_map/ppermute | solution.py:72
  128.1 4.3 %shard_map.189.refs_5_.refs_1_.refs_2_.refs_3_ = bf16[2,1536,1728]{2,1,0:T(8,128)(2,1)S(1)} custom-call(s32[5]{0:T(128)S(1)} %stack.78.refs_0_, bf16[2,384,1728]{2,1,0:T(8,128)(2,1)S(1)} %pad_maximum_fusion.refs_1_, bf16[3,2,96,1728]{3,2,1,0:T(8,128)(2,1)S(1)} %shard_map.182.refs_6_.refs_1_.refs_2_, bf16[3,2,96,1728]{3,2,1,0:T(8,128)(2,1)} %shard_map.188.refs_3_, ...), custom_call_target="tpu_custom_call" | custom-call | flops 100000000 | bytes 1000 | tf_op jit(solution)/shard_map/pallas_call | solution.py:50
  133.2 9.1 %collective-permute-done.20.refs_3_ = bf16[128,1536]{1,0:T(8,128)(2,1)S(1)} collective-permute-done((bf16[128,1536]{1,0:T(8,128)(2,1)S(1)}, bf16[128,1536]{1,0:T(8,128)(2,1)S(1)}, u32[]{:S(2)}, u32[]{:S(2)}) %collective-permute-start.20) | collective-permute-done | bytes 393248 | tf_op jit(solution)/shard_map/ppermute | solution.py:72
  146.0 10.7 %shard_map.191 = (bf16[16,32,1728]{2,1,0:T(8,128)(2,1)}, bf16[16,32,1728]{2,1,0:T(8,128)(2,1)}, bf16[16,32,1728]{2,1,0:T(8,128)(2,1)}) custom-call(bf16[512,1536]{1,0:T(8,128)(2,1)S(1)} %get-tuple-element.95.refs_0_, bf16[2,1536,1728]{2,1,0:T(8,128)(2,1)S(1)} %shard_map.189.refs_5_.refs_1_.refs_2_.refs_3_, f32[512,1728]{1,0:T(8,128)S(1)} %copy-done.6, ...), custom_call_target="tpu_custom_call" | custom-call | flops 1000000000 | bytes 1000 | tf_op jit(solution)/shard_map/pallas_call | solution.py:50
  156.9 3.9 %collective-permute-done.29.refs_3_ = bf16[16,32,1728]{2,1,0:T(8,128)(2,1)S(1)} collective-permute-done((bf16[16,32,1728]{2,1,0:T(8,128)(2,1)}, bf16[16,32,1728]{2,1,0:T(8,128)(2,1)S(1)}, u32[]{:S(2)}, u32[]{:S(2)}) %collective-permute-start.29) | collective-permute-done | bytes 1769504 | tf_op jit(solution)/shard_map/ppermute | solution.py:72
  160.7 6.1 %shard_map.192.refs_8_ = bf16[4,192,1728]{2,1,0:T(8,128)(2,1)} custom-call(bf16[768,512]{1,0:T(8,128)(2,1)S(1)} %get-tuple-element.98.refs_0_, bf16[768,512]{1,0:T(8,128)(2,1)S(1)} %collective-permute-done.25.refs_3_.refs_1_, bf16[16,32,1728]{2,1,0:T(8,128)(2,1)} %get-tuple-element.102.refs_2_.refs_1_, bf16[16,32,1728]{2,1,0:T(8,128)(2,1)S(1)} %collective-permute-done.29.refs_3_), custom_call_target="tpu_custom_call" | custom-call | flops 500000000 | bytes 1000 | tf_op jit(solution)/shard_map/pallas_call | solution.py:50
  167.7 7.1 %collective-permute-done.26.refs_3_ = bf16[768,512]{1,0:T(8,128)(2,1)S(1)} collective-permute-done((bf16[768,512]{1,0:T(8,128)(2,1)}, bf16[768,512]{1,0:T(8,128)(2,1)S(1)}, u32[]{:S(2)}, u32[]{:S(2)}) %collective-permute-start.26) | collective-permute-done | bytes 786464 | tf_op jit(solution)/shard_map/ppermute | solution.py:72
  177.0 9.6 %shard_map.193.refs_2_.refs_4_ = bf16[4,2,192,1728]{3,2,1,0:T(8,128)(2,1)} custom-call(bf16[768,512]{1,0:T(8,128)(2,1)S(1)} %copy-done.22, bf16[768,512]{1,0:T(8,128)(2,1)S(1)} %collective-permute-done.25.refs_3_.refs_1_, bf16[768,512]{1,0:T(8,128)(2,1)S(1)} %copy-done.36, bf16[768,512]{1,0:T(8,128)(2,1)S(1)} %collective-permute-done.26.refs_3_, ...), custom_call_target="tpu_custom_call" | custom-call | flops 1000000000 | bytes 1000 | tf_op jit(solution)/shard_map/pallas_call | solution.py:50
  189.4 10.3 %shard_map.195 = (bf16[128,1536]{1,0:T(8,128)(2,1)}, bf16[128,1536]{1,0:T(8,128)(2,1)}, bf16[128,1536]{1,0:T(8,128)(2,1)}, bf16[128,1536]{1,0:T(8,128)(2,1)}) custom-call(bf16[16,32,1728]{2,1,0:T(8,128)(2,1)} %get-tuple-element.101.refs_4_.refs_0_, bf16[16,32,1728]{2,1,0:T(8,128)(2,1)} %get-tuple-element.102.refs_2_.refs_1_, bf16[2,1536,1728]{2,1,0:T(8,128)(2,1)} %copy-done, ...), custom_call_target="tpu_custom_call" | custom-call | flops 700000000 | bytes 1000 | tf_op jit(solution)/shard_map/pallas_call | solution.py:50
  203.2 8.7 %collective-permute-done.33.refs_1_ = bf16[128,1536]{1,0:T(8,128)(2,1)S(1)} collective-permute-done((bf16[128,1536]{1,0:T(8,128)(2,1)}, bf16[128,1536]{1,0:T(8,128)(2,1)S(1)}, u32[]{:S(2)}, u32[]{:S(2)}) %collective-permute-start.33) | collective-permute-done | bytes 393248 | tf_op jit(solution)/shard_map/ppermute | solution.py:72
  211.9 8.1 %collective-permute-done.34.refs_2_ = bf16[128,1536]{1,0:T(8,128)(2,1)S(1)} collective-permute-done((bf16[128,1536]{1,0:T(8,128)(2,1)}, bf16[128,1536]{1,0:T(8,128)(2,1)S(1)}, u32[]{:S(2)}, u32[]{:S(2)}) %collective-permute-start.34) | collective-permute-done | bytes 393248 | tf_op jit(solution)/shard_map/ppermute | solution.py:72
  230.0 5.4 %collective-permute-done.36.refs_1_ = bf16[128,1536]{1,0:T(8,128)(2,1)S(1)} collective-permute-done((bf16[128,1536]{1,0:T(8,128)(2,1)S(1)}, bf16[128,1536]{1,0:T(8,128)(2,1)S(1)}, u32[]{:S(2)}, u32[]{:S(2)}) %collective-permute-start.36) | collective-permute-done | bytes 393248 | tf_op jit(solution)/shard_map/ppermute | solution.py:72
  236.8 7.8 %collective-permute-done.37.refs_2_ = bf16[128,1536]{1,0:T(8,128)(2,1)S(1)} collective-permute-done((bf16[128,1536]{1,0:T(8,128)(2,1)S(1)}, bf16[128,1536]{1,0:T(8,128)(2,1)S(1)}, u32[]{:S(2)}, u32[]{:S(2)}) %collective-permute-start.37) | collective-permute-done | bytes 393248 | tf_op jit(solution)/shard_map/ppermute | solution.py:72
  249.8 4.7 %collective-permute-done.39.refs_2_ = f32[32,384]{1,0:T(8,128)S(1)} collective-permute-done((f32[32,384]{1,0:T(8,128)S(1)}, f32[32,384]{1,0:T(8,128)S(1)}, u32[]{:S(2)}, u32[]{:S(2)}) %collective-permute-start.39) | collective-permute-done | bytes 49184 | tf_op jit(solution)/shard_map/ppermute | solution.py:78
  254.4 3.7 shard_map.199
  259.7 5.6 %shard_map.200 = (bf16[128,1536]{1,0:T(8,128)(2,1)}, bf16[128,1536]{1,0:T(8,128)(2,1)}, bf16[128,1536]{1,0:T(8,128)(2,1)}, bf16[128,1536]{1,0:T(8,128)(2,1)}) custom-call(bf16[512,1152]{1,0:T(8,128)(2,1)} %copy-done.16, bf16[1536,1152]{1,0:T(8,128)(2,1)} %bitcast.89), custom_call_target="tpu_custom_call" | custom-call | flops 400000000 | bytes 1000 | tf_op jit(solution)/shard_map/pallas_call | solution.py:50
  266.4 3.3 shard_map.201
  273.4 6.6 %shard_map.202 = (bf16[128,1536]{1,0:T(8,128)(2,1)}, bf16[128,1536]{1,0:T(8,128)(2,1)}, bf16[128,1536]{1,0:T(8,128)(2,1)}, bf16[128,1536]{1,0:T(8,128)(2,1)}) custom-call(bf16[16,32,1728]{2,1,0:T(8,128)(2,1)} %get-tuple-element.97.refs_6_.refs_0_, bf16[1728,1536]{1,0:T(8,128)(2,1)} %refs_1_.5, bf16[4,192,1152]{2,1,0:T(8,128)(2,1)S(1)} %get-tuple-element.124.refs_2_), custom_call_target="tpu_custom_call" | custom-call | flops 400000000 | bytes 1000 | tf_op jit(solution)/shard_map/pallas_call | solution.py:50
  283.0 9.6 %collective-permute-done.49.refs_3_ = bf16[4,48,1152]{2,1,0:T(8,128)(2,1)S(1)} collective-permute-done((bf16[4,48,1152]{2,1,0:T(8,128)(2,1)S(1)}, bf16[4,48,1152]{2,1,0:T(8,128)(2,1)S(1)}, u32[]{:S(2)}, u32[]{:S(2)}) %collective-permute-start.49) | collective-permute-done | bytes 442400 | tf_op jit(solution)/shard_map/ppermute | solution.py:72
  299.6 8.9 %collective-permute-done.45.refs_1_ = bf16[128,1536]{1,0:T(8,128)(2,1)} collective-permute-done((bf16[128,1536]{1,0:T(8,128)(2,1)}, bf16[128,1536]{1,0:T(8,128)(2,1)}, u32[]{:S(2)}, u32[]{:S(2)}) %collective-permute-start.45) | collective-permute-done | bytes 393248 | tf_op jit(solution)/shard_map/ppermute | solution.py:72
  308.5 7.3 %collective-permute-done.46.refs_2_ = bf16[128,1536]{1,0:T(8,128)(2,1)} collective-permute-done((bf16[128,1536]{1,0:T(8,128)(2,1)}, bf16[128,1536]{1,0:T(8,128)(2,1)}, u32[]{:S(2)}, u32[]{:S(2)}) %collective-permute-start.46) | collective-permute-done | bytes 393248 | tf_op jit(solution)/shard_map/ppermute | solution.py:72
  337.8 7.8 %collective-permute-done.44.refs_2_ = bf16[128,1536]{1,0:T(8,128)(2,1)S(1)} collective-permute-done((bf16[128,1536]{1,0:T(8,128)(2,1)S(1)}, bf16[128,1536]{1,0:T(8,128)(2,1)S(1)}, u32[]{:S(2)}, u32[]{:S(2)}) %collective-permute-start.44) | collective-permute-done | bytes 393248 | tf_op jit(solution)/shard_map/ppermute | solution.py:72
  345.6 11.0 %collective-permute-done.53.refs_4_.refs_3_ = bf16[3,48,1728]{2,1,0:T(8,128)(2,1)S(1)} collective-permute-done((bf16[3,48,1728]{2,1,0:T(8,128)(2,1)S(1)}, bf16[3,48,1728]{2,1,0:T(8,128)(2,1)S(1)}, u32[]{:S(2)}, u32[]{:S(2)}) %collective-permute-start.53) | collective-permute-done | bytes 497696 | tf_op jit(solution)/shard_map/ppermute | solution.py:72
  356.6 8.9 %collective-permute-done.52.refs_3_.refs_2_ = bf16[3,48,1728]{2,1,0:T(8,128)(2,1)S(1)} collective-permute-done((bf16[3,48,1728]{2,1,0:T(8,128)(2,1)S(1)}, bf16[3,48,1728]{2,1,0:T(8,128)(2,1)S(1)}, u32[]{:S(2)}, u32[]{:S(2)}) %collective-permute-start.52) | collective-permute-done | bytes 497696 | tf_op jit(solution)/shard_map/ppermute | solution.py:72
  (283 shorter events, 123.3 us)
Async XLA Ops:
  7.2 319.1 %reduce-scatter.4.cloned.1.call-start = ((), (), s32[]{:S(2)}) async-start(), calls=%async_computation.3 | async-start | bytes 3440640 | tf_op jit(solution)/shard_map/reduce_scatter | solution.py:521
  9.1 15.0 %collective-permute-start.4 = (bf16[96,1152]{1,0:T(8,128)(2,1)S(1)}, bf16[96,1152]{1,0:T(8,128)(2,1)S(1)}, u32[]{:S(2)}, u32[]{:S(2)}) collective-permute-start(bf16[96,1152]{1,0:T(8,128)(2,1)S(1)} %get-tuple-element.78), channel_id=1, source_target_pairs={{0,1},{1,0},{2,3},{3,2},{4,5},{5,4},{6,7},{7,6},{8,9},{9,8},{10,11... | collective-permute-start | bytes 663560 | tf_op jit(solution)/shard_map/ppermute | solution.py:72
  24.2 50.9 %collective-permute-start.10 = (bf16[2,96,1728]{2,1,0:T(8,128)(2,1)S(1)}, bf16[2,96,1728]{2,1,0:T(8,128)(2,1)S(1)}, u32[]{:S(2)}, u32[]{:S(2)}) collective-permute-start(bf16[2,96,1728]{2,1,0:T(8,128)(2,1)S(1)} %get-tuple-element.83), channel_id=1, source_target_pairs={{0,1},{1,0},{2,3},{3,2},{4,5},{5,4},{6,7},{7,6},{8,9},{9,8},{10,11... | collective-permute-start | bytes 1990664 | tf_op jit(solution)/shard_map/ppermute | solution.py:72
  25.3 49.8 %collective-permute-start.11 = (bf16[2,96,1728]{2,1,0:T(8,128)(2,1)S(1)}, bf16[2,96,1728]{2,1,0:T(8,128)(2,1)S(1)}, u32[]{:S(2)}, u32[]{:S(2)}) collective-permute-start(bf16[2,96,1728]{2,1,0:T(8,128)(2,1)S(1)} %get-tuple-element.84), channel_id=1, source_target_pairs={{0,2},{1,3},{2,0},{3,1},{4,6},{5,7},{6,4},{7,5},{8,10},{9,11},{10,... | collective-permute-start | bytes 1990664 | tf_op jit(solution)/shard_map/ppermute | solution.py:72
  25.9 49.2 %collective-permute-start.12 = (bf16[2,96,1728]{2,1,0:T(8,128)(2,1)S(1)}, bf16[2,96,1728]{2,1,0:T(8,128)(2,1)S(1)}, u32[]{:S(2)}, u32[]{:S(2)}) collective-permute-start(bf16[2,96,1728]{2,1,0:T(8,128)(2,1)S(1)} %get-tuple-element.85), channel_id=1, source_target_pairs={{0,3},{1,2},{2,1},{3,0},{4,7},{5,6},{6,5},{7,4},{8,11},{9,10},{10,... | collective-permute-start | bytes 1990664 | tf_op jit(solution)/shard_map/ppermute | solution.py:72
  34.0 41.1 %collective-permute-start.7 = (bf16[3,96,1152]{2,1,0:T(8,128)(2,1)S(1)}, bf16[3,96,1152]{2,1,0:T(8,128)(2,1)}, u32[]{:S(2)}, u32[]{:S(2)}) collective-permute-start(bf16[3,96,1152]{2,1,0:T(8,128)(2,1)S(1)} %shard_map.179.refs_5_), channel_id=1, source_target_pairs={{0,4},{4,0},{8,12},{12,8},{1,5},{5,1},{9,13},{13,9},{2,6},{6,2},{1... | collective-permute-start | bytes 1990664 | tf_op jit(solution)/shard_map/ppermute | solution.py:72
  35.6 36.5 %collective-permute-start.3 = (bf16[144,1536]{1,0:T(8,128)(2,1)S(1)}, bf16[144,1536]{1,0:T(8,128)(2,1)S(1)}, u32[]{:S(2)}, u32[]{:S(2)}) collective-permute-start(bf16[144,1536]{1,0:T(8,128)(2,1)S(1)} %shard_map.177.refs_3_.refs_1_), channel_id=1, source_target_pairs={{0,3},{1,2},{2,1},{3,0},{4,7},{5,6},{6,5},{7,4},{8,11},{9,10},{10,... | collective-permute-start | bytes 1327112 | tf_op jit(solution)/shard_map/ppermute | solution.py:72
  76.2 45.1 %collective-permute-start.22 = (bf16[3,2,96,1728]{3,2,1,0:T(8,128)(2,1)S(1)}, bf16[3,2,96,1728]{3,2,1,0:T(8,128)(2,1)}, u32[]{:S(2)}, u32[]{:S(2)}) collective-permute-start(bf16[3,2,96,1728]{3,2,1,0:T(8,128)(2,1)S(1)} %shard_map.182.refs_6_.refs_1_.refs_2_), channel_id=1, source_target_pairs={{0,4},{4,0},{8,12},{12,8},{1,5},{5,1},{9,13},{13,9},{2,6},{6,2},{1... | collective-permute-start | bytes 5971976 | tf_op jit(solution)/shard_map/ppermute | solution.py:72
  79.9 20.2 %collective-permute-start.17 = (bf16[128,1536]{1,0:T(8,128)(2,1)S(1)}, bf16[128,1536]{1,0:T(8,128)(2,1)}, u32[]{:S(2)}, u32[]{:S(2)}) collective-permute-start(bf16[128,1536]{1,0:T(8,128)(2,1)S(1)} %shard_map.184.refs_5_.refs_1_), channel_id=1, source_target_pairs={{0,2},{1,3},{2,0},{3,1},{4,6},{5,7},{6,4},{7,5},{8,10},{9,11},{10,... | collective-permute-start | bytes 1179656 | tf_op jit(solution)/shard_map/ppermute | solution.py:72
  81.0 19.2 %collective-permute-start.18 = (bf16[128,1536]{1,0:T(8,128)(2,1)S(1)}, bf16[128,1536]{1,0:T(8,128)(2,1)S(1)}, u32[]{:S(2)}, u32[]{:S(2)}) collective-permute-start(bf16[128,1536]{1,0:T(8,128)(2,1)S(1)} %shard_map.184.refs_5_.refs_1_), channel_id=1, source_target_pairs={{0,3},{1,2},{2,1},{3,0},{4,7},{5,6},{6,5},{7,4},{8,11},{9,10},{10,... | collective-permute-start | bytes 1179656 | tf_op jit(solution)/shard_map/ppermute | solution.py:72
  91.7 16.8 %collective-permute-start.13 = (bf16[128,1536]{1,0:T(8,128)(2,1)S(1)}, bf16[128,1536]{1,0:T(8,128)(2,1)S(1)}, u32[]{:S(2)}, u32[]{:S(2)}) collective-permute-start(bf16[128,1536]{1,0:T(8,128)(2,1)S(1)} %get-tuple-element.87), channel_id=1, source_target_pairs={{0,1},{1,0},{2,3},{3,2},{4,5},{5,4},{6,7},{7,6},{8,9},{9,8},{10,11... | collective-permute-start | bytes 1179656 | tf_op jit(solution)/shard_map/ppermute | solution.py:72
  92.8 23.2 %collective-permute-start.14 = (bf16[128,1536]{1,0:T(8,128)(2,1)S(1)}, bf16[128,1536]{1,0:T(8,128)(2,1)S(1)}, u32[]{:S(2)}, u32[]{:S(2)}) collective-permute-start(bf16[128,1536]{1,0:T(8,128)(2,1)S(1)} %get-tuple-element.88), channel_id=1, source_target_pairs={{0,2},{1,3},{2,0},{3,1},{4,6},{5,7},{6,4},{7,5},{8,10},{9,11},{10,... | collective-permute-start | bytes 1179656 | tf_op jit(solution)/shard_map/ppermute | solution.py:72
  100.2 15.8 %collective-permute-start.15 = (bf16[128,1536]{1,0:T(8,128)(2,1)S(1)}, bf16[128,1536]{1,0:T(8,128)(2,1)S(1)}, u32[]{:S(2)}, u32[]{:S(2)}) collective-permute-start(bf16[128,1536]{1,0:T(8,128)(2,1)S(1)} %get-tuple-element.89), channel_id=1, source_target_pairs={{0,3},{1,2},{2,1},{3,0},{4,7},{5,6},{6,5},{7,4},{8,11},{9,10},{10,... | collective-permute-start | bytes 1179656 | tf_op jit(solution)/shard_map/ppermute | solution.py:72
  100.2 27.9 %collective-permute-start.23 = (bf16[3,2,96,1728]{3,2,1,0:T(8,128)(2,1)S(1)}, bf16[3,2,96,1728]{3,2,1,0:T(8,128)(2,1)}, u32[]{:S(2)}, u32[]{:S(2)}) collective-permute-start(bf16[3,2,96,1728]{3,2,1,0:T(8,128)(2,1)S(1)} %shard_map.182.refs_6_.refs_1_.refs_2_), channel_id=1, source_target_pairs={{0,16},{16,0},{1,17},{17,1},{2,18},{18,2},{3,19},{19,3},{4,20},{20... | collective-permute-start | bytes 5971976 | tf_op jit(solution)/shard_map/ppermute | solution.py:72
  122.6 19.7 %collective-permute-start.20 = (bf16[128,1536]{1,0:T(8,128)(2,1)S(1)}, bf16[128,1536]{1,0:T(8,128)(2,1)S(1)}, u32[]{:S(2)}, u32[]{:S(2)}) collective-permute-start(bf16[128,1536]{1,0:T(8,128)(2,1)S(1)} %get-tuple-element.94.refs_1_.refs_6_), channel_id=1, source_target_pairs={{0,2},{1,3},{2,0},{3,1},{4,6},{5,7},{6,4},{7,5},{8,10},{9,11},{10,... | collective-permute-start | bytes 1179656 | tf_op jit(solution)/shard_map/ppermute | solution.py:72
  123.3 19.0 %collective-permute-start.21 = (bf16[128,1536]{1,0:T(8,128)(2,1)S(1)}, bf16[128,1536]{1,0:T(8,128)(2,1)S(1)}, u32[]{:S(2)}, u32[]{:S(2)}) collective-permute-start(bf16[128,1536]{1,0:T(8,128)(2,1)S(1)} %get-tuple-element.94.refs_1_.refs_6_), channel_id=1, source_target_pairs={{0,3},{1,2},{2,1},{3,0},{4,7},{5,6},{6,5},{7,4},{8,11},{9,10},{10,... | collective-permute-start | bytes 1179656 | tf_op jit(solution)/shard_map/ppermute | solution.py:72
  166.9 160.7 %reduce-scatter.6.cloned.1.call-start = ((), (), s32[]{:S(2)}) async-start(), calls=%async_computation.4 | async-start | bytes 6881280 | tf_op jit(solution)/shard_map/reduce_scatter | solution.py:542
  186.7 187.3 %reduce-scatter.8.cloned.1.call-start = ((), (), s32[]{:S(2)}) async-start(), calls=%async_computation.5 | async-start | bytes 2949120 | tf_op jit(solution)/shard_map/reduce_scatter | solution.py:784
  200.4 19.6 %collective-permute-start.34 = (bf16[128,1536]{1,0:T(8,128)(2,1)}, bf16[128,1536]{1,0:T(8,128)(2,1)S(1)}, u32[]{:S(2)}, u32[]{:S(2)}) collective-permute-start(bf16[128,1536]{1,0:T(8,128)(2,1)} %get-tuple-element.109), channel_id=1, source_target_pairs={{0,2},{1,3},{2,0},{3,1},{4,6},{5,7},{6,4},{7,5},{8,10},{9,11},{10,... | collective-permute-start | bytes 1179656 | tf_op jit(solution)/shard_map/ppermute | solution.py:72
  201.6 18.4 %collective-permute-start.35 = (bf16[128,1536]{1,0:T(8,128)(2,1)}, bf16[128,1536]{1,0:T(8,128)(2,1)S(1)}, u32[]{:S(2)}, u32[]{:S(2)}) collective-permute-start(bf16[128,1536]{1,0:T(8,128)(2,1)} %get-tuple-element.110), channel_id=1, source_target_pairs={{0,3},{1,2},{2,1},{3,0},{4,7},{5,6},{6,5},{7,4},{8,11},{9,10},{10,... | collective-permute-start | bytes 1179656 | tf_op jit(solution)/shard_map/ppermute | solution.py:72
  224.6 20.0 %collective-permute-start.37 = (bf16[128,1536]{1,0:T(8,128)(2,1)S(1)}, bf16[128,1536]{1,0:T(8,128)(2,1)S(1)}, u32[]{:S(2)}, u32[]{:S(2)}) collective-permute-start(bf16[128,1536]{1,0:T(8,128)(2,1)S(1)} %get-tuple-element.111.refs_6_.refs_0_), channel_id=1, source_target_pairs={{0,2},{1,3},{2,0},{3,1},{4,6},{5,7},{6,4},{7,5},{8,10},{9,11},{10,... | collective-permute-start | bytes 1179656 | tf_op jit(solution)/shard_map/ppermute | solution.py:72
  225.3 19.3 %collective-permute-start.38 = (bf16[128,1536]{1,0:T(8,128)(2,1)S(1)}, bf16[128,1536]{1,0:T(8,128)(2,1)S(1)}, u32[]{:S(2)}, u32[]{:S(2)}) collective-permute-start(bf16[128,1536]{1,0:T(8,128)(2,1)S(1)} %get-tuple-element.111.refs_6_.refs_0_), channel_id=1, source_target_pairs={{0,3},{1,2},{2,1},{3,0},{4,7},{5,6},{6,5},{7,4},{8,11},{9,10},{10,... | collective-permute-start | bytes 1179656 | tf_op jit(solution)/shard_map/ppermute | solution.py:72
  227.9 19.8 %collective-permute-start.30 = (bf16[512,96]{1,0:T(8,128)(2,1)S(1)}, bf16[512,96]{1,0:T(8,128)(2,1)S(1)}, u32[]{:S(2)}, u32[]{:S(2)}) collective-permute-start(bf16[512,96]{1,0:T(8,128)(2,1)S(1)} %get-tuple-element.104), channel_id=1, source_target_pairs={{0,1},{1,0},{2,3},{3,2},{4,5},{5,4},{6,7},{7,6},{8,9},{9,8},{10,11... | collective-permute-start | bytes 294920 | tf_op jit(solution)/shard_map/ppermute | solution.py:72
  229.3 19.0 %collective-permute-start.31 = (bf16[512,96]{1,0:T(8,128)(2,1)S(1)}, bf16[512,96]{1,0:T(8,128)(2,1)S(1)}, u32[]{:S(2)}, u32[]{:S(2)}) collective-permute-start(bf16[512,96]{1,0:T(8,128)(2,1)S(1)} %get-tuple-element.105), channel_id=1, source_target_pairs={{0,2},{1,3},{2,0},{3,1},{4,6},{5,7},{6,4},{7,5},{8,10},{9,11},{10,... | collective-permute-start | bytes 294920 | tf_op jit(solution)/shard_map/ppermute | solution.py:72
  271.4 21.2 %collective-permute-start.49 = (bf16[4,48,1152]{2,1,0:T(8,128)(2,1)S(1)}, bf16[4,48,1152]{2,1,0:T(8,128)(2,1)S(1)}, u32[]{:S(2)}, u32[]{:S(2)}) collective-permute-start(bf16[4,48,1152]{2,1,0:T(8,128)(2,1)S(1)} %get-tuple-element.153), channel_id=1, source_target_pairs={{0,2},{1,3},{2,0},{3,1},{4,6},{5,7},{6,4},{7,5},{8,10},{9,11},{10,... | collective-permute-start | bytes 1327112 | tf_op jit(solution)/shard_map/ppermute | solution.py:72
  272.9 19.7 %collective-permute-start.50 = (bf16[4,48,1152]{2,1,0:T(8,128)(2,1)S(1)}, bf16[4,48,1152]{2,1,0:T(8,128)(2,1)S(1)}, u32[]{:S(2)}, u32[]{:S(2)}) collective-permute-start(bf16[4,48,1152]{2,1,0:T(8,128)(2,1)S(1)} %get-tuple-element.152), channel_id=1, source_target_pairs={{0,3},{1,2},{2,1},{3,0},{4,7},{5,6},{6,5},{7,4},{8,11},{9,10},{10,... | collective-permute-start | bytes 1327112 | tf_op jit(solution)/shard_map/ppermute | solution.py:72
  297.3 18.5 %collective-permute-start.46 = (bf16[128,1536]{1,0:T(8,128)(2,1)}, bf16[128,1536]{1,0:T(8,128)(2,1)}, u32[]{:S(2)}, u32[]{:S(2)}) collective-permute-start(bf16[128,1536]{1,0:T(8,128)(2,1)} %get-tuple-element.130), channel_id=1, source_target_pairs={{0,2},{1,3},{2,0},{3,1},{4,6},{5,7},{6,4},{7,5},{8,10},{9,11},{10,... | collective-permute-start | bytes 1179656 | tf_op jit(solution)/shard_map/ppermute | solution.py:72
  298.2 17.7 %collective-permute-start.47 = (bf16[128,1536]{1,0:T(8,128)(2,1)}, bf16[128,1536]{1,0:T(8,128)(2,1)}, u32[]{:S(2)}, u32[]{:S(2)}) collective-permute-start(bf16[128,1536]{1,0:T(8,128)(2,1)} %get-tuple-element.131), channel_id=1, source_target_pairs={{0,3},{1,2},{2,1},{3,0},{4,7},{5,6},{6,5},{7,4},{8,11},{9,10},{10,... | collective-permute-start | bytes 1179656 | tf_op jit(solution)/shard_map/ppermute | solution.py:72
  320.7 17.0 %collective-permute-start.43 = (bf16[128,1536]{1,0:T(8,128)(2,1)}, bf16[128,1536]{1,0:T(8,128)(2,1)S(1)}, u32[]{:S(2)}, u32[]{:S(2)}) collective-permute-start(bf16[128,1536]{1,0:T(8,128)(2,1)} %get-tuple-element.127), channel_id=1, source_target_pairs={{0,2},{1,3},{2,0},{3,1},{4,6},{5,7},{6,4},{7,5},{8,10},{9,11},{10,... | collective-permute-start | bytes 1179656 | tf_op jit(solution)/shard_map/ppermute | solution.py:72
  334.2 22.4 %collective-permute-start.53 = (bf16[3,48,1728]{2,1,0:T(8,128)(2,1)S(1)}, bf16[3,48,1728]{2,1,0:T(8,128)(2,1)S(1)}, u32[]{:S(2)}, u32[]{:S(2)}) collective-permute-start(bf16[3,48,1728]{2,1,0:T(8,128)(2,1)S(1)} %pad_maximum_fusion.7), channel_id=1, source_target_pairs={{0,3},{1,2},{2,1},{3,0},{4,7},{5,6},{6,5},{7,4},{8,11},{9,10},{10,... | collective-permute-start | bytes 1493000 | tf_op jit(solution)/shard_map/ppermute | solution.py:72
  335.4 30.1 %collective-permute-start.52 = (bf16[3,48,1728]{2,1,0:T(8,128)(2,1)S(1)}, bf16[3,48,1728]{2,1,0:T(8,128)(2,1)S(1)}, u32[]{:S(2)}, u32[]{:S(2)}) collective-permute-start(bf16[3,48,1728]{2,1,0:T(8,128)(2,1)S(1)} %pad_maximum_fusion.6), channel_id=1, source_target_pairs={{0,2},{1,3},{2,0},{3,1},{4,6},{5,7},{6,4},{7,5},{8,10},{9,11},{10,... | collective-permute-start | bytes 1493000 | tf_op jit(solution)/shard_map/ppermute | solution.py:72
  336.3 29.2 %collective-permute-start.51 = (bf16[3,48,1728]{2,1,0:T(8,128)(2,1)S(1)}, bf16[3,48,1728]{2,1,0:T(8,128)(2,1)S(1)}, u32[]{:S(2)}, u32[]{:S(2)}) collective-permute-start(bf16[3,48,1728]{2,1,0:T(8,128)(2,1)S(1)} %pad_maximum_fusion.5), channel_id=1, source_target_pairs={{0,1},{1,0},{2,3},{3,2},{4,5},{5,4},{6,7},{7,6},{8,9},{9,8},{10,11... | collective-permute-start | bytes 1493000 | tf_op jit(solution)/shard_map/ppermute | solution.py:72
  (93 other events, 914.2 us)
Sparse Core Ops, SparseCore 0:
  167.0 54.7 reduce-scatter.3
  224.1 98.8 reduce-scatter.5
  325.3 48.5 reduce-scatter.7
where the time goes:
time: 385 us; the launch traced here: 384 us
  waiting for transfers between devices  174 us (45%)
  Pallas kernels  97.5 us (25%)
  starting transfers between devices  66 us (17%)
  local copies, waits for them, and re-layouts  30.4 us (8%)
  between operations  14.6 us (4%)
    ppermute x59, waiting for transfers between devices, swap(): lax.ppermute(value, axis, [(i, i ^ k) for i in range(lax.axis_size(axis))])  170 us
    pallas_call x33, Pallas kernels, run(): pl.pallas_call(kernel, out_shape=tuple(outs), grid=grid, in_specs=list(in...  97.5 us
    ppermute x59, starting transfers between devices, swap(): lax.ppermute(value, axis, [(i, i ^ k) for i in range(lax.axis_size(axis))])  60.5 us
    unnamed x122, local copies, waits for them, and re-layouts  20.4 us
  transfers between devices with their start and end apart: 64, of which 26 were waited for; matrix products, arithmetic and copies ran while one was open for 3% of the time, Pallas kernels for 20%

commit v1 on v0

--- a/solution.py
+++ b/solution.py
@@ -318,6 +318,9 @@
     both_sent = wait_all(both_sent, *in_got)
     both_got = [swap(piece, "fsdp", k) for piece, k in zip(both_sent, others)]
 
+    both_mine = pack(both_got, (in_next,))
+    both_next = swap(both_mine, "seq", 1)
+
     def norm_body(place_ref, *refs):
         xs, (n_ref, nh_ref, gain_ref) = refs[:shards], refs[shards:]
         for s in range(shards):
@@ -341,12 +344,10 @@
         [shape((group, width)), shape((shards * edge, width)), shape((8, width), f32)],
         [place, *[in_far(m) for m in messages]],
         in_specs=[SMEM] + [whole(m) for m in messages],
-        after=(in_mine,),
+        after=(both_mine,),
         us=2,
     )
 
-    both_mine = pack(both_got, (normed_one, in_next))
-    both_next = swap(both_mine, "seq", 1)
     w_in = assemble(
         in_far(in_proj),
         [
@@ -491,10 +492,10 @@
         grid=(h_steps,),
         in_specs=[whole(two_all), tiles((2, width, tile), 2), tiles((group, tile), 1)],
         out_specs=[unit_tiles] * 3,
-        after=(two_come,),
         us=10,
         limit=24,
     )
+    d_up = wait_for(d_up, two_come, keep=True)
     d_up_come = swap(d_up, "dp", 1)
     d_gate_come = swap(d_gate, "dp", 1)
     hidden_come = swap(hidden_all, "dp", 1)
@@ -848,7 +849,7 @@
         out_ref[...] = sum_ref[:, 3 * width :].astype(f32)
 
     in_grad, out_grad = run(
-        last_body, [far((slab, 3 * width), f32), far((slab, width), f32)], [mix_sum], after=(gate_grad, block_output, terms)
+        last_body, [far((slab, 3 * width), f32), far((slab, width), f32)], [in_far(mix_sum)], after=(gate_grad, block_output, terms)
     )
     return (
         block_output,

time: 385 us -> 375 us (0.974)
  waiting for transfers between devices: 174 us -> 161 us
    ppermute x59, waiting for transfers between devices: 170 us -> 157 us  [swap(): lax.ppermute(value, axis, [(i, i ^ k) for i in range(lax.axis_size(axis))])]
    pallas_call x33 -> x34, Pallas kernels: 97.5 us -> 99.1 us  [run(): pl.pallas_call(kernel, out_shape=tuple(outs), grid=grid, in_specs=list(in...]
    unnamed x122 -> x112, local copies, waits for them, and re-layouts: 20.4 us -> 21.6 us
  transfers between devices with their start and end apart: 64 -> 64, of which waited for: 26 -> 27; matrix products, arithmetic and copies ran while one was open for 3% -> 3% of each run, Pallas kernels for 20% -> 23%
where the time goes in v1:
time: 375 us; the launch traced here: 374 us
  waiting for transfers between devices  161 us (43%)
  Pallas kernels  99.1 us (26%)
  starting transfers between devices  66.1 us (18%)
  local copies, waits for them, and re-layouts  31.7 us (8%)
  between operations  14.6 us (4%)
    ppermute x59, waiting for transfers between devices, swap(): lax.ppermute(value, axis, [(i, i ^ k) for i in range(lax.axis_size(axis))])  157 us
    pallas_call x34, Pallas kernels, run(): pl.pallas_call(kernel, out_shape=tuple(outs), grid=grid, in_specs=list(in...  99.1 us
    ppermute x59, starting transfers between devices, swap(): lax.ppermute(value, axis, [(i, i ^ k) for i in range(lax.axis_size(axis))])  60.6 us
    unnamed x112, local copies, waits for them, and re-layouts  21.6 us
  transfers between devices with their start and end apart: 64, of which 27 were waited for; matrix products, arithmetic and copies ran while one was open for 3% of the time, Pallas kernels for 23%

profile of v1, /device:TPU:0, one launch (start us, length us, event | category | flops | bytes accessed | tf_op | source)
XLA Modules:
  0.0 373.6 jit_solution(7958503965192985970)
XLA Ops:
  13.7 3.9 %collective-permute-start = (bf16[16,1536]{1,0:T(8,128)(2,1)S(1)}, bf16[16,1536]{1,0:T(8,128)(2,1)S(1)}, u32[]{:S(2)}, u32[]{:S(2)}) collective-permute-start(bf16[16,1536]{1,0:T(8,128)(2,1)S(1)} %slice_bitcast_fusion), channel_id=1, source_target_pairs={{0,4},{4,8},{8,12},{1,5},{5,9},{9,13},{2,6},{6,10},{10,14},{3,7},{... | collective-permute-start | bytes 147464 | tf_op jit(solution)/shard_map/ppermute | solution.py:78
  30.6 11.5 %collective-permute-done.7.refs_0_ = bf16[2,96,1728]{2,1,0:T(8,128)(2,1)S(1)} collective-permute-done((bf16[2,96,1728]{2,1,0:T(8,128)(2,1)S(1)}, bf16[2,96,1728]{2,1,0:T(8,128)(2,1)S(1)}, u32[]{:S(2)}, u32[]{:S(2)}) %collective-permute-start.7) | collective-permute-done | bytes 663584 | tf_op jit(solution)/shard_map/ppermute | solution.py:72
  42.2 13.6 %collective-permute-done.8.refs_1_ = bf16[2,96,1728]{2,1,0:T(8,128)(2,1)S(1)} collective-permute-done((bf16[2,96,1728]{2,1,0:T(8,128)(2,1)S(1)}, bf16[2,96,1728]{2,1,0:T(8,128)(2,1)S(1)}, u32[]{:S(2)}, u32[]{:S(2)}) %collective-permute-start.8) | collective-permute-done | bytes 663584 | tf_op jit(solution)/shard_map/ppermute | solution.py:72
  61.7 9.4 %collective-permute-done.1.refs_2_ = bf16[144,1536]{1,0:T(8,128)(2,1)S(1)} collective-permute-done((bf16[144,1536]{1,0:T(8,128)(2,1)S(1)}, bf16[144,1536]{1,0:T(8,128)(2,1)S(1)}, u32[]{:S(2)}, u32[]{:S(2)}) %collective-permute-start.1) | collective-permute-done | bytes 442400 | tf_op jit(solution)/shard_map/ppermute | solution.py:72
  72.0 5.5 %collective-permute-done.2.refs_3_ = bf16[144,1536]{1,0:T(8,128)(2,1)S(1)} collective-permute-done((bf16[144,1536]{1,0:T(8,128)(2,1)S(1)}, bf16[144,1536]{1,0:T(8,128)(2,1)S(1)}, u32[]{:S(2)}, u32[]{:S(2)}) %collective-permute-start.2) | collective-permute-done | bytes 442400 | tf_op jit(solution)/shard_map/ppermute | solution.py:72
  88.7 4.0 %shard_map.185 = (f32[512,1152]{1,0:T(8,128)S(1)}, f32[64,384]{1,0:T(8,128)S(1)}, bf16[512,384]{1,0:T(8,128)(2,1)S(1)}, bf16[128,1536]{1,0:T(8,128)(2,1)S(1)}, b...) custom-call(bf16[512,1536]{1,0:T(8,128)(2,1)S(1)} %get-tuple-element.84.refs_0_.refs_1_, ...), custom_call_target="tpu_custom_call" | custom-call | flops 550000000 | bytes 1000 | tf_op jit(solution)/shard_map/pallas_call | solution.py:50
  99.0 8.3 %shard_map.186 = (f32[512,1728]{1,0:T(8,128)S(1)}, bf16[768,512]{1,0:T(8,128)(2,1)}, bf16[768,512]{1,0:T(8,128)(2,1)}) custom-call(s32[3]{0:T(128)S(1)} %pad_add_fusion.refs_0_, bf16[128,1536]{1,0:T(8,128)(2,1)S(1)} %shard_map.184.refs_5_.refs_1_, bf16[128,1536]{1,0:T(8,128)(2,1)} %collective-permute-done.16.refs_2_, ...), custom_call_target="tpu_custom_call" | custom-call | flops 500000000 | bytes 1000 | tf_op jit(solution)/shard_map/pallas_call | solution.py:50
  107.3 4.6 %collective-permute-done.14.refs_2_ = bf16[128,1536]{1,0:T(8,128)(2,1)S(1)} collective-permute-done((bf16[128,1536]{1,0:T(8,128)(2,1)S(1)}, bf16[128,1536]{1,0:T(8,128)(2,1)S(1)}, u32[]{:S(2)}, u32[]{:S(2)}) %collective-permute-start.14) | collective-permute-done | bytes 393248 | tf_op jit(solution)/shard_map/ppermute | solution.py:72
  116.7 3.0 dynamic-slice_bitcast_fusion
  120.0 4.3 %shard_map.189.refs_5_.refs_1_.refs_2_.refs_3_ = bf16[2,1536,1728]{2,1,0:T(8,128)(2,1)S(1)} custom-call(s32[5]{0:T(128)S(1)} %stack.87.refs_0_, bf16[2,384,1728]{2,1,0:T(8,128)(2,1)S(1)} %pad_maximum_fusion.refs_1_, bf16[3,2,96,1728]{3,2,1,0:T(8,128)(2,1)S(1)} %shard_map.181.refs_5_.refs_6_.refs_1_.refs_2_, bf16[3,2,96,1728]{3,2,1,0:T(8,128)(2,1)} %shard_map.188.refs_3_, ...), custom_call_target="tpu_custom_call" | custom-call | flops 100000000 | bytes 1000 | tf_op jit(solution)/shard_map/pallas_call | solution.py:50
  125.2 9.7 %collective-permute-done.20.refs_3_ = bf16[128,1536]{1,0:T(8,128)(2,1)S(1)} collective-permute-done((bf16[128,1536]{1,0:T(8,128)(2,1)S(1)}, bf16[128,1536]{1,0:T(8,128)(2,1)S(1)}, u32[]{:S(2)}, u32[]{:S(2)}) %collective-permute-start.20) | collective-permute-done | bytes 393248 | tf_op jit(solution)/shard_map/ppermute | solution.py:72
  136.9 10.6 %shard_map.191 = (bf16[16,32,1728]{2,1,0:T(8,128)(2,1)}, bf16[16,32,1728]{2,1,0:T(8,128)(2,1)}, bf16[16,32,1728]{2,1,0:T(8,128)(2,1)}) custom-call(bf16[512,1536]{1,0:T(8,128)(2,1)S(1)} %get-tuple-element.95.refs_0_, bf16[2,1536,1728]{2,1,0:T(8,128)(2,1)S(1)} %shard_map.189.refs_5_.refs_1_.refs_2_.refs_3_, f32[512,1728]{1,0:T(8,128)S(1)} %copy-done.6), custom_call_target="tpu_custom_call" | custom-call | flops 1000000000 | bytes 1000 | tf_op jit(solution)/shard_map/pallas_call | solution.py:50
  147.6 4.0 %collective-permute-done.29.refs_3_ = bf16[16,32,1728]{2,1,0:T(8,128)(2,1)S(1)} collective-permute-done((bf16[16,32,1728]{2,1,0:T(8,128)(2,1)}, bf16[16,32,1728]{2,1,0:T(8,128)(2,1)S(1)}, u32[]{:S(2)}, u32[]{:S(2)}) %collective-permute-start.29) | collective-permute-done | bytes 1769504 | tf_op jit(solution)/shard_map/ppermute | solution.py:72
  151.5 6.1 %shard_map.193.refs_8_ = bf16[4,192,1728]{2,1,0:T(8,128)(2,1)} custom-call(bf16[768,512]{1,0:T(8,128)(2,1)S(1)} %get-tuple-element.97.refs_0_, bf16[768,512]{1,0:T(8,128)(2,1)S(1)} %collective-permute-done.25.refs_1_, bf16[16,32,1728]{2,1,0:T(8,128)(2,1)} %shard_map.192.refs_2_.refs_1_, bf16[16,32,1728]{2,1,0:T(8,128)(2,1)S(1)} %collective-permute-done.29.refs_3_), custom_call_target="tpu_custom_call" | custom-call | flops 500000000 | bytes 1000 | tf_op jit(solution)/shard_map/pallas_call | solution.py:50
  158.5 7.1 %collective-permute-done.26.refs_3_ = bf16[768,512]{1,0:T(8,128)(2,1)S(1)} collective-permute-done((bf16[768,512]{1,0:T(8,128)(2,1)}, bf16[768,512]{1,0:T(8,128)(2,1)S(1)}, u32[]{:S(2)}, u32[]{:S(2)}) %collective-permute-start.26) | collective-permute-done | bytes 786464 | tf_op jit(solution)/shard_map/ppermute | solution.py:72
  167.8 9.6 %shard_map.194.refs_2_.refs_4_ = bf16[4,2,192,1728]{3,2,1,0:T(8,128)(2,1)} custom-call(bf16[768,512]{1,0:T(8,128)(2,1)S(1)} %copy-done.21, bf16[768,512]{1,0:T(8,128)(2,1)S(1)} %collective-permute-done.25.refs_1_, bf16[768,512]{1,0:T(8,128)(2,1)S(1)} %copy-done.35, bf16[768,512]{1,0:T(8,128)(2,1)S(1)} %collective-permute-done.26.refs_3_, ...), custom_call_target="tpu_custom_call" | custom-call | flops 1000000000 | bytes 1000 | tf_op jit(solution)/shard_map/pallas_call | solution.py:50
  180.1 10.3 %shard_map.196 = (bf16[128,1536]{1,0:T(8,128)(2,1)}, bf16[128,1536]{1,0:T(8,128)(2,1)}, bf16[128,1536]{1,0:T(8,128)(2,1)}, bf16[128,1536]{1,0:T(8,128)(2,1)}) custom-call(bf16[16,32,1728]{2,1,0:T(8,128)(2,1)} %get-tuple-element.101.refs_4_.refs_0_, bf16[16,32,1728]{2,1,0:T(8,128)(2,1)} %shard_map.192.refs_2_.refs_1_, bf16[2,1536,1728]{2,1,0:T(8,128)(2,1)} %copy-done, ...), custom_call_target="tpu_custom_call" | custom-call | flops 700000000 | bytes 1000 | tf_op jit(solution)/shard_map/pallas_call | solution.py:50
  194.0 8.7 %collective-permute-done.33.refs_1_ = bf16[128,1536]{1,0:T(8,128)(2,1)S(1)} collective-permute-done((bf16[128,1536]{1,0:T(8,128)(2,1)}, bf16[128,1536]{1,0:T(8,128)(2,1)S(1)}, u32[]{:S(2)}, u32[]{:S(2)}) %collective-permute-start.33) | collective-permute-done | bytes 393248 | tf_op jit(solution)/shard_map/ppermute | solution.py:72
  202.9 7.6 %collective-permute-done.35.refs_3_ = bf16[128,1536]{1,0:T(8,128)(2,1)S(1)} collective-permute-done((bf16[128,1536]{1,0:T(8,128)(2,1)}, bf16[128,1536]{1,0:T(8,128)(2,1)S(1)}, u32[]{:S(2)}, u32[]{:S(2)}) %collective-permute-start.35) | collective-permute-done | bytes 393248 | tf_op jit(solution)/shard_map/ppermute | solution.py:72
  220.9 5.1 %collective-permute-done.36.refs_1_ = bf16[128,1536]{1,0:T(8,128)(2,1)S(1)} collective-permute-done((bf16[128,1536]{1,0:T(8,128)(2,1)S(1)}, bf16[128,1536]{1,0:T(8,128)(2,1)S(1)}, u32[]{:S(2)}, u32[]{:S(2)}) %collective-permute-start.36) | collective-permute-done | bytes 393248 | tf_op jit(solution)/shard_map/ppermute | solution.py:72
  227.7 6.9 %collective-permute-done.37.refs_2_ = bf16[128,1536]{1,0:T(8,128)(2,1)S(1)} collective-permute-done((bf16[128,1536]{1,0:T(8,128)(2,1)S(1)}, bf16[128,1536]{1,0:T(8,128)(2,1)S(1)}, u32[]{:S(2)}, u32[]{:S(2)}) %collective-permute-start.37) | collective-permute-done | bytes 393248 | tf_op jit(solution)/shard_map/ppermute | solution.py:72
  240.5 3.5 collective-permute-done.39.refs_2_
  244.0 3.7 shard_map.200
  249.3 5.7 %shard_map.201 = (bf16[128,1536]{1,0:T(8,128)(2,1)}, bf16[128,1536]{1,0:T(8,128)(2,1)}, bf16[128,1536]{1,0:T(8,128)(2,1)}, bf16[128,1536]{1,0:T(8,128)(2,1)}) custom-call(bf16[512,1152]{1,0:T(8,128)(2,1)} %copy-done.15, bf16[1536,1152]{1,0:T(8,128)(2,1)} %bitcast.89), custom_call_target="tpu_custom_call" | custom-call | flops 400000000 | bytes 1000 | tf_op jit(solution)/shard_map/pallas_call | solution.py:50
  256.0 3.4 shard_map.202
  263.1 6.7 %shard_map.203 = (bf16[128,1536]{1,0:T(8,128)(2,1)}, bf16[128,1536]{1,0:T(8,128)(2,1)}, bf16[128,1536]{1,0:T(8,128)(2,1)}, bf16[128,1536]{1,0:T(8,128)(2,1)}) custom-call(bf16[16,32,1728]{2,1,0:T(8,128)(2,1)} %get-tuple-element.96.refs_6_.refs_0_, bf16[1728,1536]{1,0:T(8,128)(2,1)} %refs_1_.5, bf16[4,192,1152]{2,1,0:T(8,128)(2,1)S(1)} %get-tuple-element.124.refs_2_), custom_call_target="tpu_custom_call" | custom-call | flops 400000000 | bytes 1000 | tf_op jit(solution)/shard_map/pallas_call | solution.py:50
  272.7 9.8 %collective-permute-done.49.refs_3_ = bf16[4,48,1152]{2,1,0:T(8,128)(2,1)S(1)} collective-permute-done((bf16[4,48,1152]{2,1,0:T(8,128)(2,1)S(1)}, bf16[4,48,1152]{2,1,0:T(8,128)(2,1)S(1)}, u32[]{:S(2)}, u32[]{:S(2)}) %collective-permute-start.49) | collective-permute-done | bytes 442400 | tf_op jit(solution)/shard_map/ppermute | solution.py:72
  289.5 8.9 %collective-permute-done.45.refs_1_ = bf16[128,1536]{1,0:T(8,128)(2,1)} collective-permute-done((bf16[128,1536]{1,0:T(8,128)(2,1)}, bf16[128,1536]{1,0:T(8,128)(2,1)}, u32[]{:S(2)}, u32[]{:S(2)}) %collective-permute-start.45) | collective-permute-done | bytes 393248 | tf_op jit(solution)/shard_map/ppermute | solution.py:72
  298.4 7.1 %collective-permute-done.46.refs_2_ = bf16[128,1536]{1,0:T(8,128)(2,1)} collective-permute-done((bf16[128,1536]{1,0:T(8,128)(2,1)}, bf16[128,1536]{1,0:T(8,128)(2,1)}, u32[]{:S(2)}, u32[]{:S(2)}) %collective-permute-start.46) | collective-permute-done | bytes 393248 | tf_op jit(solution)/shard_map/ppermute | solution.py:72
  327.5 7.8 %collective-permute-done.44.refs_2_ = bf16[128,1536]{1,0:T(8,128)(2,1)S(1)} collective-permute-done((bf16[128,1536]{1,0:T(8,128)(2,1)S(1)}, bf16[128,1536]{1,0:T(8,128)(2,1)S(1)}, u32[]{:S(2)}, u32[]{:S(2)}) %collective-permute-start.44) | collective-permute-done | bytes 393248 | tf_op jit(solution)/shard_map/ppermute | solution.py:72
  335.3 11.0 %collective-permute-done.53.refs_4_.refs_3_ = bf16[3,48,1728]{2,1,0:T(8,128)(2,1)S(1)} collective-permute-done((bf16[3,48,1728]{2,1,0:T(8,128)(2,1)S(1)}, bf16[3,48,1728]{2,1,0:T(8,128)(2,1)S(1)}, u32[]{:S(2)}, u32[]{:S(2)}) %collective-permute-start.53) | collective-permute-done | bytes 497696 | tf_op jit(solution)/shard_map/ppermute | solution.py:72
  346.3 8.9 %collective-permute-done.52.refs_3_.refs_2_ = bf16[3,48,1728]{2,1,0:T(8,128)(2,1)S(1)} collective-permute-done((bf16[3,48,1728]{2,1,0:T(8,128)(2,1)S(1)}, bf16[3,48,1728]{2,1,0:T(8,128)(2,1)S(1)}, u32[]{:S(2)}, u32[]{:S(2)}) %collective-permute-start.52) | collective-permute-done | bytes 497696 | tf_op jit(solution)/shard_map/ppermute | solution.py:72
  (274 shorter events, 128.8 us)
Async XLA Ops:
  7.2 308.9 %reduce-scatter.4.cloned.1.call-start = ((), (), s32[]{:S(2)}) async-start(), calls=%async_computation.3 | async-start | bytes 3440640 | tf_op jit(solution)/shard_map/reduce_scatter | solution.py:522
  23.8 18.4 %collective-permute-start.7 = (bf16[2,96,1728]{2,1,0:T(8,128)(2,1)S(1)}, bf16[2,96,1728]{2,1,0:T(8,128)(2,1)S(1)}, u32[]{:S(2)}, u32[]{:S(2)}) collective-permute-start(bf16[2,96,1728]{2,1,0:T(8,128)(2,1)S(1)} %get-tuple-element.81), channel_id=1, source_target_pairs={{0,1},{1,0},{2,3},{3,2},{4,5},{5,4},{6,7},{7,6},{8,9},{9,8},{10,11... | collective-permute-start | bytes 1990664 | tf_op jit(solution)/shard_map/ppermute | solution.py:72
  25.0 30.8 %collective-permute-start.8 = (bf16[2,96,1728]{2,1,0:T(8,128)(2,1)S(1)}, bf16[2,96,1728]{2,1,0:T(8,128)(2,1)S(1)}, u32[]{:S(2)}, u32[]{:S(2)}) collective-permute-start(bf16[2,96,1728]{2,1,0:T(8,128)(2,1)S(1)} %get-tuple-element.82), channel_id=1, source_target_pairs={{0,2},{1,3},{2,0},{3,1},{4,6},{5,7},{6,4},{7,5},{8,10},{9,11},{10,... | collective-permute-start | bytes 1990664 | tf_op jit(solution)/shard_map/ppermute | solution.py:72
  25.8 29.9 %collective-permute-start.9 = (bf16[2,96,1728]{2,1,0:T(8,128)(2,1)S(1)}, bf16[2,96,1728]{2,1,0:T(8,128)(2,1)S(1)}, u32[]{:S(2)}, u32[]{:S(2)}) collective-permute-start(bf16[2,96,1728]{2,1,0:T(8,128)(2,1)S(1)} %get-tuple-element.83), channel_id=1, source_target_pairs={{0,3},{1,2},{2,1},{3,0},{4,7},{5,6},{6,5},{7,4},{8,11},{9,10},{10,... | collective-permute-start | bytes 1990664 | tf_op jit(solution)/shard_map/ppermute | solution.py:72
  29.0 26.8 %collective-permute-start.10 = (bf16[3,96,1152]{2,1,0:T(8,128)(2,1)}, bf16[3,96,1152]{2,1,0:T(8,128)(2,1)}, u32[]{:S(2)}, u32[]{:S(2)}) collective-permute-start(bf16[3,96,1152]{2,1,0:T(8,128)(2,1)} %shard_map.180), channel_id=1, source_target_pairs={{0,4},{4,0},{8,12},{12,8},{1,5},{5,1},{9,13},{13,9},{2,6},{6,2},{1... | collective-permute-start | bytes 1990664 | tf_op jit(solution)/shard_map/ppermute | solution.py:72
  56.6 55.8 %collective-permute-start.22 = (bf16[3,2,96,1728]{3,2,1,0:T(8,128)(2,1)S(1)}, bf16[3,2,96,1728]{3,2,1,0:T(8,128)(2,1)}, u32[]{:S(2)}, u32[]{:S(2)}) collective-permute-start(bf16[3,2,96,1728]{3,2,1,0:T(8,128)(2,1)S(1)} %shard_map.181.refs_5_.refs_6_.refs_1_.refs_2_), channel_id=1, source_target_pairs={{0,4},{4,0},{8,12},{12,8},{1,5},{5,1},{9,13},{13,9},{2,6},{6,2},{1... | collective-permute-start | bytes 5971976 | tf_op jit(solution)/shard_map/ppermute | solution.py:72
  58.8 18.8 %collective-permute-start.2 = (bf16[144,1536]{1,0:T(8,128)(2,1)S(1)}, bf16[144,1536]{1,0:T(8,128)(2,1)S(1)}, u32[]{:S(2)}, u32[]{:S(2)}) collective-permute-start(bf16[144,1536]{1,0:T(8,128)(2,1)S(1)} %shard_map.177.refs_3_.refs_1_), channel_id=1, source_target_pairs={{0,2},{1,3},{2,0},{3,1},{4,6},{5,7},{6,4},{7,5},{8,10},{9,11},{10,... | collective-permute-start | bytes 1327112 | tf_op jit(solution)/shard_map/ppermute | solution.py:72
  59.9 19.5 %collective-permute-start.3 = (bf16[144,1536]{1,0:T(8,128)(2,1)S(1)}, bf16[144,1536]{1,0:T(8,128)(2,1)S(1)}, u32[]{:S(2)}, u32[]{:S(2)}) collective-permute-start(bf16[144,1536]{1,0:T(8,128)(2,1)S(1)} %shard_map.177.refs_3_.refs_1_), channel_id=1, source_target_pairs={{0,3},{1,2},{2,1},{3,0},{4,7},{5,6},{6,5},{7,4},{8,11},{9,10},{10,... | collective-permute-start | bytes 1327112 | tf_op jit(solution)/shard_map/ppermute | solution.py:72
  61.7 22.1 %collective-permute-start.11 = (bf16[3,96,1152]{2,1,0:T(8,128)(2,1)}, bf16[3,96,1152]{2,1,0:T(8,128)(2,1)}, u32[]{:S(2)}, u32[]{:S(2)}) collective-permute-start(bf16[3,96,1152]{2,1,0:T(8,128)(2,1)} %shard_map.180), channel_id=1, source_target_pairs={{0,16},{16,0},{1,17},{17,1},{2,18},{18,2},{3,19},{19,3},{4,20},{20... | collective-permute-start | bytes 1990664 | tf_op jit(solution)/shard_map/ppermute | solution.py:72
  77.5 17.3 %collective-permute-start.16 = (bf16[128,1536]{1,0:T(8,128)(2,1)S(1)}, bf16[128,1536]{1,0:T(8,128)(2,1)}, u32[]{:S(2)}, u32[]{:S(2)}) collective-permute-start(bf16[128,1536]{1,0:T(8,128)(2,1)S(1)} %shard_map.184.refs_5_.refs_1_), channel_id=1, source_target_pairs={{0,1},{1,0},{2,3},{3,2},{4,5},{5,4},{6,7},{7,6},{8,9},{9,8},{10,11... | collective-permute-start | bytes 1179656 | tf_op jit(solution)/shard_map/ppermute | solution.py:72
  80.2 15.9 %collective-permute-start.17 = (bf16[128,1536]{1,0:T(8,128)(2,1)S(1)}, bf16[128,1536]{1,0:T(8,128)(2,1)}, u32[]{:S(2)}, u32[]{:S(2)}) collective-permute-start(bf16[128,1536]{1,0:T(8,128)(2,1)S(1)} %shard_map.184.refs_5_.refs_1_), channel_id=1, source_target_pairs={{0,2},{1,3},{2,0},{3,1},{4,6},{5,7},{6,4},{7,5},{8,10},{9,11},{10,... | collective-permute-start | bytes 1179656 | tf_op jit(solution)/shard_map/ppermute | solution.py:72
  83.8 15.2 %collective-permute-start.18 = (bf16[128,1536]{1,0:T(8,128)(2,1)S(1)}, bf16[128,1536]{1,0:T(8,128)(2,1)S(1)}, u32[]{:S(2)}, u32[]{:S(2)}) collective-permute-start(bf16[128,1536]{1,0:T(8,128)(2,1)S(1)} %shard_map.184.refs_5_.refs_1_), channel_id=1, source_target_pairs={{0,3},{1,2},{2,1},{3,0},{4,7},{5,6},{6,5},{7,4},{8,11},{9,10},{10,... | collective-permute-start | bytes 1179656 | tf_op jit(solution)/shard_map/ppermute | solution.py:72
  94.8 17.1 %collective-permute-start.14 = (bf16[128,1536]{1,0:T(8,128)(2,1)S(1)}, bf16[128,1536]{1,0:T(8,128)(2,1)S(1)}, u32[]{:S(2)}, u32[]{:S(2)}) collective-permute-start(bf16[128,1536]{1,0:T(8,128)(2,1)S(1)} %get-tuple-element.88), channel_id=1, source_target_pairs={{0,2},{1,3},{2,0},{3,1},{4,6},{5,7},{6,4},{7,5},{8,10},{9,11},{10,... | collective-permute-start | bytes 1179656 | tf_op jit(solution)/shard_map/ppermute | solution.py:72
  96.1 15.8 %collective-permute-start.15 = (bf16[128,1536]{1,0:T(8,128)(2,1)S(1)}, bf16[128,1536]{1,0:T(8,128)(2,1)S(1)}, u32[]{:S(2)}, u32[]{:S(2)}) collective-permute-start(bf16[128,1536]{1,0:T(8,128)(2,1)S(1)} %get-tuple-element.89), channel_id=1, source_target_pairs={{0,3},{1,2},{2,1},{3,0},{4,7},{5,6},{6,5},{7,4},{8,11},{9,10},{10,... | collective-permute-start | bytes 1179656 | tf_op jit(solution)/shard_map/ppermute | solution.py:72
  99.0 21.0 %collective-permute-start.23 = (bf16[3,2,96,1728]{3,2,1,0:T(8,128)(2,1)S(1)}, bf16[3,2,96,1728]{3,2,1,0:T(8,128)(2,1)}, u32[]{:S(2)}, u32[]{:S(2)}) collective-permute-start(bf16[3,2,96,1728]{3,2,1,0:T(8,128)(2,1)S(1)} %shard_map.181.refs_5_.refs_6_.refs_1_.refs_2_), channel_id=1, source_target_pairs={{0,16},{16,0},{1,17},{17,1},{2,18},{18,2},{3,19},{19,3},{4,20},{20... | collective-permute-start | bytes 5971976 | tf_op jit(solution)/shard_map/ppermute | solution.py:72
  115.2 19.7 %collective-permute-start.20 = (bf16[128,1536]{1,0:T(8,128)(2,1)S(1)}, bf16[128,1536]{1,0:T(8,128)(2,1)S(1)}, u32[]{:S(2)}, u32[]{:S(2)}) collective-permute-start(bf16[128,1536]{1,0:T(8,128)(2,1)S(1)} %get-tuple-element.94.refs_1_.refs_6_), channel_id=1, source_target_pairs={{0,2},{1,3},{2,0},{3,1},{4,6},{5,7},{6,4},{7,5},{8,10},{9,11},{10,... | collective-permute-start | bytes 1179656 | tf_op jit(solution)/shard_map/ppermute | solution.py:72
  116.0 18.9 %collective-permute-start.21 = (bf16[128,1536]{1,0:T(8,128)(2,1)S(1)}, bf16[128,1536]{1,0:T(8,128)(2,1)S(1)}, u32[]{:S(2)}, u32[]{:S(2)}) collective-permute-start(bf16[128,1536]{1,0:T(8,128)(2,1)S(1)} %get-tuple-element.94.refs_1_.refs_6_), channel_id=1, source_target_pairs={{0,3},{1,2},{2,1},{3,0},{4,7},{5,6},{6,5},{7,4},{8,11},{9,10},{10,... | collective-permute-start | bytes 1179656 | tf_op jit(solution)/shard_map/ppermute | solution.py:72
  157.7 159.6 %reduce-scatter.6.cloned.1.call-start = ((), (), s32[]{:S(2)}) async-start(), calls=%async_computation.4 | async-start | bytes 6881280 | tf_op jit(solution)/shard_map/reduce_scatter | solution.py:543
  177.5 186.2 %reduce-scatter.8.cloned.1.call-start = ((), (), s32[]{:S(2)}) async-start(), calls=%async_computation.5 | async-start | bytes 2949120 | tf_op jit(solution)/shard_map/reduce_scatter | solution.py:785
  192.2 18.3 %collective-permute-start.35 = (bf16[128,1536]{1,0:T(8,128)(2,1)}, bf16[128,1536]{1,0:T(8,128)(2,1)S(1)}, u32[]{:S(2)}, u32[]{:S(2)}) collective-permute-start(bf16[128,1536]{1,0:T(8,128)(2,1)} %get-tuple-element.110), channel_id=1, source_target_pairs={{0,3},{1,2},{2,1},{3,0},{4,7},{5,6},{6,5},{7,4},{8,11},{9,10},{10,... | collective-permute-start | bytes 1179656 | tf_op jit(solution)/shard_map/ppermute | solution.py:72
  215.4 19.2 %collective-permute-start.37 = (bf16[128,1536]{1,0:T(8,128)(2,1)S(1)}, bf16[128,1536]{1,0:T(8,128)(2,1)S(1)}, u32[]{:S(2)}, u32[]{:S(2)}) collective-permute-start(bf16[128,1536]{1,0:T(8,128)(2,1)S(1)} %get-tuple-element.111.refs_6_.refs_0_), channel_id=1, source_target_pairs={{0,2},{1,3},{2,0},{3,1},{4,6},{5,7},{6,4},{7,5},{8,10},{9,11},{10,... | collective-permute-start | bytes 1179656 | tf_op jit(solution)/shard_map/ppermute | solution.py:72
  216.2 18.9 %collective-permute-start.38 = (bf16[128,1536]{1,0:T(8,128)(2,1)S(1)}, bf16[128,1536]{1,0:T(8,128)(2,1)S(1)}, u32[]{:S(2)}, u32[]{:S(2)}) collective-permute-start(bf16[128,1536]{1,0:T(8,128)(2,1)S(1)} %get-tuple-element.111.refs_6_.refs_0_), channel_id=1, source_target_pairs={{0,3},{1,2},{2,1},{3,0},{4,7},{5,6},{6,5},{7,4},{8,11},{9,10},{10,... | collective-permute-start | bytes 1179656 | tf_op jit(solution)/shard_map/ppermute | solution.py:72
  218.5 19.7 %collective-permute-start.30 = (bf16[512,96]{1,0:T(8,128)(2,1)S(1)}, bf16[512,96]{1,0:T(8,128)(2,1)S(1)}, u32[]{:S(2)}, u32[]{:S(2)}) collective-permute-start(bf16[512,96]{1,0:T(8,128)(2,1)S(1)} %get-tuple-element.104), channel_id=1, source_target_pairs={{0,1},{1,0},{2,3},{3,2},{4,5},{5,4},{6,7},{7,6},{8,9},{9,8},{10,11... | collective-permute-start | bytes 294920 | tf_op jit(solution)/shard_map/ppermute | solution.py:72
  220.1 18.2 %collective-permute-start.31 = (bf16[512,96]{1,0:T(8,128)(2,1)S(1)}, bf16[512,96]{1,0:T(8,128)(2,1)S(1)}, u32[]{:S(2)}, u32[]{:S(2)}) collective-permute-start(bf16[512,96]{1,0:T(8,128)(2,1)S(1)} %get-tuple-element.105), channel_id=1, source_target_pairs={{0,2},{1,3},{2,0},{3,1},{4,6},{5,7},{6,4},{7,5},{8,10},{9,11},{10,... | collective-permute-start | bytes 294920 | tf_op jit(solution)/shard_map/ppermute | solution.py:72
  261.2 21.2 %collective-permute-start.49 = (bf16[4,48,1152]{2,1,0:T(8,128)(2,1)S(1)}, bf16[4,48,1152]{2,1,0:T(8,128)(2,1)S(1)}, u32[]{:S(2)}, u32[]{:S(2)}) collective-permute-start(bf16[4,48,1152]{2,1,0:T(8,128)(2,1)S(1)} %get-tuple-element.153), channel_id=1, source_target_pairs={{0,2},{1,3},{2,0},{3,1},{4,6},{5,7},{6,4},{7,5},{8,10},{9,11},{10,... | collective-permute-start | bytes 1327112 | tf_op jit(solution)/shard_map/ppermute | solution.py:72
  262.5 20.0 %collective-permute-start.50 = (bf16[4,48,1152]{2,1,0:T(8,128)(2,1)S(1)}, bf16[4,48,1152]{2,1,0:T(8,128)(2,1)S(1)}, u32[]{:S(2)}, u32[]{:S(2)}) collective-permute-start(bf16[4,48,1152]{2,1,0:T(8,128)(2,1)S(1)} %get-tuple-element.152), channel_id=1, source_target_pairs={{0,3},{1,2},{2,1},{3,0},{4,7},{5,6},{6,5},{7,4},{8,11},{9,10},{10,... | collective-permute-start | bytes 1327112 | tf_op jit(solution)/shard_map/ppermute | solution.py:72
  287.0 18.5 %collective-permute-start.46 = (bf16[128,1536]{1,0:T(8,128)(2,1)}, bf16[128,1536]{1,0:T(8,128)(2,1)}, u32[]{:S(2)}, u32[]{:S(2)}) collective-permute-start(bf16[128,1536]{1,0:T(8,128)(2,1)} %get-tuple-element.130), channel_id=1, source_target_pairs={{0,2},{1,3},{2,0},{3,1},{4,6},{5,7},{6,4},{7,5},{8,10},{9,11},{10,... | collective-permute-start | bytes 1179656 | tf_op jit(solution)/shard_map/ppermute | solution.py:72
  287.7 17.8 %collective-permute-start.47 = (bf16[128,1536]{1,0:T(8,128)(2,1)}, bf16[128,1536]{1,0:T(8,128)(2,1)}, u32[]{:S(2)}, u32[]{:S(2)}) collective-permute-start(bf16[128,1536]{1,0:T(8,128)(2,1)} %get-tuple-element.131), channel_id=1, source_target_pairs={{0,3},{1,2},{2,1},{3,0},{4,7},{5,6},{6,5},{7,4},{8,11},{9,10},{10,... | collective-permute-start | bytes 1179656 | tf_op jit(solution)/shard_map/ppermute | solution.py:72
  310.3 17.2 %collective-permute-start.43 = (bf16[128,1536]{1,0:T(8,128)(2,1)}, bf16[128,1536]{1,0:T(8,128)(2,1)S(1)}, u32[]{:S(2)}, u32[]{:S(2)}) collective-permute-start(bf16[128,1536]{1,0:T(8,128)(2,1)} %get-tuple-element.127), channel_id=1, source_target_pairs={{0,2},{1,3},{2,0},{3,1},{4,6},{5,7},{6,4},{7,5},{8,10},{9,11},{10,... | collective-permute-start | bytes 1179656 | tf_op jit(solution)/shard_map/ppermute | solution.py:72
  323.9 22.4 %collective-permute-start.53 = (bf16[3,48,1728]{2,1,0:T(8,128)(2,1)S(1)}, bf16[3,48,1728]{2,1,0:T(8,128)(2,1)S(1)}, u32[]{:S(2)}, u32[]{:S(2)}) collective-permute-start(bf16[3,48,1728]{2,1,0:T(8,128)(2,1)S(1)} %pad_maximum_fusion.7), channel_id=1, source_target_pairs={{0,3},{1,2},{2,1},{3,0},{4,7},{5,6},{6,5},{7,4},{8,11},{9,10},{10,... | collective-permute-start | bytes 1493000 | tf_op jit(solution)/shard_map/ppermute | solution.py:72
  325.2 30.0 %collective-permute-start.52 = (bf16[3,48,1728]{2,1,0:T(8,128)(2,1)S(1)}, bf16[3,48,1728]{2,1,0:T(8,128)(2,1)S(1)}, u32[]{:S(2)}, u32[]{:S(2)}) collective-permute-start(bf16[3,48,1728]{2,1,0:T(8,128)(2,1)S(1)} %pad_maximum_fusion.6), channel_id=1, source_target_pairs={{0,2},{1,3},{2,0},{3,1},{4,6},{5,7},{6,4},{7,5},{8,10},{9,11},{10,... | collective-permute-start | bytes 1493000 | tf_op jit(solution)/shard_map/ppermute | solution.py:72
  325.9 29.3 %collective-permute-start.51 = (bf16[3,48,1728]{2,1,0:T(8,128)(2,1)S(1)}, bf16[3,48,1728]{2,1,0:T(8,128)(2,1)S(1)}, u32[]{:S(2)}, u32[]{:S(2)}) collective-permute-start(bf16[3,48,1728]{2,1,0:T(8,128)(2,1)S(1)} %pad_maximum_fusion.5), channel_id=1, source_target_pairs={{0,1},{1,0},{2,3},{3,2},{4,5},{5,4},{6,7},{7,6},{8,9},{9,8},{10,11... | collective-permute-start | bytes 1493000 | tf_op jit(solution)/shard_map/ppermute | solution.py:72
  (88 other events, 894.9 us)
Sparse Core Ops, SparseCore 0:
  157.8 53.0 reduce-scatter.3
  213.3 98.8 reduce-scatter.5
  314.4 48.5 reduce-scatter.7

commit v2 on v1

--- a/solution.py
+++ b/solution.py
@@ -255,7 +255,7 @@
             body,
             [out((planes, width, columns))],
             [starts, own, *arrays],
-            in_specs=[SMEM] + [ANY] * (1 + len(arrays)),
+            in_specs=[SMEM] + [VMEM] * (1 + len(arrays)),
             out_specs=[out_spec],
             scratch=[pltpu.SemaphoreType.DMA((planes * (4 + len(arrays) * count),))],
             after=after,
@@ -362,14 +362,16 @@
     cot_held = hold(cot_local, both_mine)
     cot_blocks = [cot_held] + send_tokens(cot_held)
 
-    def mixer_body(n_ref, nh_ref, taps_ref, w_ref, o_ref, proj_ref, edge_ref, gated_ref, *refs):
-        p_refs, (ph_ref, ext_ref) = refs[:shards], refs[shards:]
+    def mixer_body(n_ref, nh_ref, taps_ref, w_ref, o_ref, far_ref, edge_ref, gated_ref, *refs):
+        p_refs, (ph_ref, ext_ref, proj_ref, sem) = refs[:shards], refs[shards:]
         for t in range(3):
             cols = slice(t * part, (t + 1) * part)
             w = w_ref[:, cols]
             proj_ref[:, cols] = mm(n_ref[...], w)
             if t != 1:
                 ph_ref[:, cols] = mm(nh_ref[...], w)
+        leave = pltpu.make_async_copy(proj_ref, far_ref, sem)
+        leave.start()
         edge_ref[...] = ph_ref[:, :part] * ph_ref[:, 2 * part :]
         for k in range(shards):
             r = slice(k * rows, (k + 1) * rows)
@@ -384,20 +386,28 @@
             o = mm(gated_ref[...], o_ref[:, cols]).astype(bf16)
             for k in range(shards):
                 p_refs[k][:, cols] = o[k * rows : (k + 1) * rows]
+        leave.wait()
 
     projected, edge_product, gated, *mix_parts = run(
         mixer_body,
         [
-            shape((group, 3 * part), f32),
+            far((group, 3 * part), f32),
             shape((shards * edge, part), f32),
             shape((group, part)),
         ]
         + [shape((rows, width))] * shards,
         [normed_one, normed_edge, taps_own, w_in, out_proj],
-        scratch=[pltpu.VMEM((shards * edge, 3 * part), f32), pltpu.VMEM((edge + rows, part), f32)],
+        out_specs=[ANY, whole(shape((shards * edge, part))), whole(shape((group, part)))]
+        + [whole(shape((rows, width)))] * shards,
+        scratch=[
+            pltpu.VMEM((shards * edge, 3 * part), f32),
+            pltpu.VMEM((edge + rows, part), f32),
+            pltpu.VMEM((group, 3 * part), f32),
+            pltpu.SemaphoreType.DMA(()),
+        ],
         after=(cot_held,),
         us=5.5,
-        limit=6,
+        limit=10,
     )
 
     def cot_body(place_ref, *refs):
@@ -454,8 +464,11 @@
             (swap(both_next, "dp", 1), (1 - c) * half_part + there),
         ],
         (normed_two,),
-        limit=16,
-    )
+        out=far,
+        out_spec=ANY,
+        limit=20,
+    )
+    w_both = in_far(w_both)
     turned = shape((half, group))
 
     def turn_two_body(place_ref, *refs):
@@ -473,32 +486,32 @@
     )
     two_come = swap(two_send, "dp", 1)
 
-    def feed_body(all_ref, w_ref, dh_ref, du_ref, dg_ref, h_ref):
-        gate = mm(all_ref[...], w_ref[0])
-        upward = mm(all_ref[...], w_ref[1])
-        s = jax.nn.sigmoid(gate)
-        dh = dh_ref[...]
-        du_ref[...] = (dh * (gate * s)).astype(bf16).reshape(du_ref.shape)
-        dg_ref[...] = (dh * upward * s * (1.0 + gate * (1.0 - s))).astype(bf16).reshape(du_ref.shape)
-        h_ref[...] = (gate * s * upward).astype(bf16).reshape(du_ref.shape)
-
     bundle = 32
     units = (group // bundle, bundle, hidden)
     unit_tiles = tiles((group // bundle, bundle, tile), 2)
-    d_up, d_gate, hidden_all = run(
-        feed_body,
-        [far(units)] * 3,
+    def gate_body(all_ref, w_ref, dh_ref, g_ref, du_ref):
+        gate_ = mm(all_ref[...], w_ref[...])
+        g_ref[...] = gate_
+        du = dh_ref[...] * (gate_ * jax.nn.sigmoid(gate_))
+        du_ref[...] = du.astype(bf16).reshape(du_ref.shape)
+
+    gate, d_up = run(
+        gate_body,
+        [far((group, hidden), f32), far(units)],
         [two_all, w_both, d_hidden],
         grid=(h_steps,),
-        in_specs=[whole(two_all), tiles((2, width, tile), 2), tiles((group, tile), 1)],
-        out_specs=[unit_tiles] * 3,
-        us=10,
-        limit=24,
-    )
+        in_specs=[
+            whole(two_all),
+            pl.BlockSpec((None, width, tile), lambda step: (0, 0, step)),
+            tiles((group, tile), 1),
+        ],
+        out_specs=[tiles((group, tile), 1), unit_tiles],
+        us=6,
+        limit=16,
+    )
+    gate = in_far(gate)
     d_up = wait_for(d_up, two_come, keep=True)
     d_up_come = swap(d_up, "dp", 1)
-    d_gate_come = swap(d_gate, "dp", 1)
-    hidden_come = swap(hidden_all, "dp", 1)
 
     def flat(ref):
         return ref[...].reshape(group, ref.shape[2])
@@ -521,27 +534,32 @@
     )
     up_sum = lax.psum_scatter(up_both, "seq", scatter_dimension=0, tiled=True).reshape(chunk, hidden)
 
-    def two_sum_body(own_ref, come_ref, cot_own_ref, cot_come_ref, dg_ref, dgc_ref, h_ref, hc_ref, out_ref):
-        total = mm(own_ref[...], flat(dg_ref)) + mm(come_ref[...], flat(dgc_ref))
-        out_ref[:, 0] = total.astype(bf16).reshape(blocks, chunk, tile)
-        total = mm(cot_own_ref[...], flat(h_ref)) + mm(cot_come_ref[...], flat(hc_ref))
-        out_ref[:, 1] = total.astype(bf16).reshape(blocks, chunk, tile)
-
-    (two_both,) = run(
-        two_sum_body,
-        [shape((blocks, 2, chunk, hidden))],
-        [two_keep, two_come, cot_keep, cot_come, d_gate, d_gate_come, hidden_all, hidden_come],
+    def up_body(all_ref, w_ref, g_ref, dh_ref, dg_ref, h_ref):
+        upward = mm(all_ref[...], w_ref[...])
+        gate_ = g_ref[...]
+        s = jax.nn.sigmoid(gate_)
+        dg = dh_ref[...] * upward * s * (1.0 + gate_ * (1.0 - s))
+        dg_ref[...] = dg.astype(bf16).reshape(dg_ref.shape)
+        h_ref[...] = (gate_ * s * upward).astype(bf16).reshape(h_ref.shape)
+
+    d_gate, hidden_all = run(
+        up_body,
+        [far(units)] * 2,
+        [two_all, w_both, gate, d_hidden],
         grid=(h_steps,),
-        in_specs=[whole(turned)] * 4 + [unit_tiles] * 4,
-        out_specs=[tiles((blocks, 2, chunk, tile), 3)],
-        after=(up_both,),
-        us=10,
-        limit=20,
-        hbm=True,
-        near=(0, 1, 2, 3, 5, 7),
-    )
-    two_sum = lax.psum_scatter(two_both, "seq", scatter_dimension=0, tiled=True)
-    two_sum = two_sum.reshape(2, chunk, hidden)
+        in_specs=[
+            whole(two_all),
+            pl.BlockSpec((None, width, tile), lambda step: (1, 0, step)),
+            tiles((group, tile), 1),
+            tiles((group, tile), 1),
+        ],
+        out_specs=[unit_tiles] * 2,
+        after=(in_far(up_both),),
+        us=7,
+        limit=18,
+    )
+    d_gate_come = swap(d_gate, "dp", 1)
+    hidden_come = swap(hidden_all, "dp", 1)
 
     def back_two_body(dg_ref, du_ref, wg_ref, wu_ref, *p_refs):
         d = (mm_t(flat(dg_ref), wg_ref[...]) + mm_t(flat(du_ref), wu_ref[...])).astype(bf16)
@@ -560,12 +578,51 @@
             pl.BlockSpec((None, tile, hidden), lambda step: (1, step, 0)),
         ],
         out_specs=[tiles((rows, tile), 1)] * shards,
-        after=(two_both,),
         us=7,
         limit=16,
         hbm=True,
     )
     back_two_got = [swap(back_two[k], "fsdp", k) for k in others]
+
+    main = hidden // 128 * 128
+    rest = hidden - main
+    last_main = main - (h_steps - 1) * tile
+
+    def two_sum_body(own_ref, come_ref, cot_own_ref, cot_come_ref, dg_ref, dgc_ref, h_ref, hc_ref, out_ref):
+        step = pl.program_id(0)
+        gate_ = mm(own_ref[...], flat(dg_ref)) + mm(come_ref[...], flat(dgc_ref))
+        gate_ = gate_.reshape(blocks, chunk, tile)
+        down_ = mm(cot_own_ref[...], flat(h_ref)) + mm(cot_come_ref[...], flat(hc_ref))
+        down_ = down_.reshape(blocks, chunk, tile)
+
+        @pl.when(step < h_steps - 1)
+        def _():
+            at = pl.multiple_of(step * tile, 128)
+            out_ref[:, :, pl.ds(at, tile)] = gate_.astype(bf16)
+            out_ref[:, :, pl.ds(main + at, tile)] = down_.astype(bf16)
+
+        @pl.when(step == h_steps - 1)
+        def _():
+            out_ref[:, :, main - last_main : main] = gate_[:, :, :last_main].astype(bf16)
+            out_ref[:, :, 2 * main - last_main : 2 * main] = down_[:, :, :last_main].astype(bf16)
+            rests = [v[:, :, last_main : last_main + rest] for v in (gate_, down_)]
+            out_ref[:, :, 2 * main :] = jnp.concatenate(rests, axis=2).astype(bf16)
+
+    (two_both,) = run(
+        two_sum_body,
+        [shape((blocks, chunk, 2 * hidden))],
+        [two_keep, two_come, cot_keep, cot_come, d_gate, d_gate_come, hidden_all, hidden_come],
+        grid=(h_steps,),
+        in_specs=[whole(turned)] * 4 + [unit_tiles] * 4,
+        out_specs=[whole(shape((blocks, chunk, 2 * hidden)))],
+        after=(in_far(back_two[0]),),
+        us=10,
+        limit=24,
+        hbm=True,
+        near=(0, 1, 2, 3, 5, 7),
+    )
+    two_sum = lax.psum_scatter(two_both, "seq", scatter_dimension=0, tiled=True)
+    two_sum = two_sum.reshape(chunk, 2 * hidden)
 
     def second_grad_body(*refs):
         parts, (s_ref, cot_ref, gain_ref, d_ref, mix_ref, term_ref) = refs[:shards], refs[shards:]
@@ -602,7 +659,7 @@
         [shape((group, channels))] * shards,
         [place, gated],
         in_specs=[SMEM, whole(gated)],
-        after=(two_both,),
+        after=(in_far(two_both),),
     )
     owner_got = [owner[0]] + [swap(owner[k], "fsdp", k) for k in others]
 
@@ -735,7 +792,7 @@
         [place, one_turned, d_projected, in_come, own_turned, mix_all, out_come],
         in_specs=[SMEM]
         + [whole(a) for a in (one_turned, d_projected, in_come, own_turned, mix_all, out_come)],
-        after=(back_one[0],),
+        after=(in_far(back_one[0]),),
     )
 
     def final_body(h_ref, w_ref, *p_refs):
@@ -779,7 +836,7 @@
         [far((blocks, slab, 4 * width))],
         [place, *in_pieces, out_both.reshape(blocks, slab, width)],
         in_specs=[SMEM] + [VMEM] * (shards + 1),
-        after=(final_parts[0],),
+        after=(in_far(final_parts[0]),),
         limit=12,
     )
     mix_sum = lax.psum_scatter(mix_both, "seq", scatter_dimension=0, tiled=True).reshape(slab, 4 * width)
@@ -799,18 +856,18 @@
         input_grad_body,
         [shape((rows, width), f32), shape((1, width), f32)],
         [back_one[0], *back_one_got, x_local, d_second, gains],
-        after=(mix_both,),
+        after=(in_far(mix_both),),
     )
     input_grad = input_grad.reshape(seqs, length, width)
 
 
-    two_sum = wait_for(two_sum, input_grad)
-    up_rows = up_sum.reshape(1, shards, slab, hidden)
-    two_rows = two_sum.reshape(2, shards, slab, hidden)
+    two_sum = wait_for(two_sum, one_term)
+    up_rows = up_sum.reshape(shards, slab, hidden)
+    two_rows = two_sum.reshape(shards, slab, 2 * hidden)
 
     def feed_rows(k):
-        parts = [lax.dynamic_index_in_dim(r, f ^ k, 1, keepdims=False) for r in (up_rows, two_rows)]
-        return jnp.concatenate(parts, axis=0)
+        parts = [lax.dynamic_index_in_dim(r, f ^ k, 0, keepdims=False) for r in (two_rows, up_rows)]
+        return jnp.concatenate(parts, axis=1)
 
     feed_pieces = [feed_rows(0)] + [swap(feed_rows(k), "fsdp", k) for k in others]
 
@@ -823,17 +880,25 @@
 
     spread_taps = [jnp.where(f == s, tap_terms, 0.0) for s in range(shards)]
     terms = jnp.concatenate([one_term, two_term, jnp.concatenate(spread_taps, axis=1)], axis=0)
-    terms = sum_over(sum_over(sum_over(terms, "dp"), "seq"), "fsdp", feed_pieces[1:])
+    terms = sum_over(sum_over(sum_over(terms, "dp", feed_pieces[:1]), "seq"), "fsdp", feed_pieces[1:])
     own = lax.dynamic_slice_in_dim(terms, ((c * blocks + z) * shards + f) * slab, slab, 1)
 
     def spread_body(place_ref, *refs):
-        got, outs = refs[:shards], refs[shards:]
-        for n in range(3):
-            for s in range(shards):
-                pick = got[0][n]
-                for k in others:
-                    pick = jnp.where((place_ref[0] ^ k) == s, got[k][n], pick)
-                outs[n][:, s * hidden : (s + 1) * hidden] = pick.astype(f32)
+        got, (up_ref, gate_ref, down_ref) = refs[:shards], refs[shards:]
+
+        def pick(s, start, size):
+            value = got[0][:, start : start + size]
+            for k in others:
+                value = jnp.where((place_ref[0] ^ k) == s, got[k][:, start : start + size], value)
+            return value.astype(f32)
+
+        for s in range(shards):
+            at = s * hidden
+            up_ref[:, at : at + hidden] = pick(s, 2 * hidden, hidden)
+            gate_ref[:, at : at + main] = pick(s, 0, main)
+            down_ref[:, at : at + main] = pick(s, main, main)
+            gate_ref[:, at + main : at + hidden] = pick(s, 2 * main, rest)
+            down_ref[:, at + main : at + hidden] = pick(s, 2 * main + rest, rest)
 
     up_grad, gate_grad, down_rows = run(
         spread_body,
@@ -849,7 +914,7 @@
         out_ref[...] = sum_ref[:, 3 * width :].astype(f32)
 
     in_grad, out_grad = run(
-        last_body, [far((slab, 3 * width), f32), far((slab, width), f32)], [in_far(mix_sum)], after=(gate_grad, block_output, terms)
+        last_body, [far((slab, 3 * width), f32), far((slab, width), f32)], [in_far(mix_sum)], after=(in_far(gate_grad), in_far(block_output), own)
     )
     return (
         block_output,

time: 375 us -> 371 us (0.989)
  waiting for transfers between devices: 161 us -> 137 us
  Pallas kernels: 99.1 us -> 115 us
  other arithmetic: 1.09 us -> 6.67 us
    ppermute x59, waiting for transfers between devices: 157 us -> 125 us  [swap(): lax.ppermute(value, axis, [(i, i ^ k) for i in range(lax.axis_size(axis))])]
    pallas_call x34 -> x36, Pallas kernels: 99.1 us -> 115 us  [run(): pl.pallas_call(kernel, out_shape=tuple(outs), grid=grid, in_specs=list(in...]
    reduce_scatter x1, waiting for transfers between devices: 0.01 us -> 5.89 us  [on_device(): lax.psum_scatter(mix_both, 'seq', scatter_dimension=0, tiled=True)]
    unnamed x112 -> x130, local copies, waits for them, and re-layouts: 21.6 us -> 18.8 us
  transfers between devices with their start and end apart: 64 -> 64, of which waited for: 27 -> 23; matrix products, arithmetic and copies ran while one was open for 3% -> 5% of each run, Pallas kernels for 23% -> 28%
where the time goes in v2:
time: 371 us; the launch traced here: 370 us
  waiting for transfers between devices  137 us (37%)
  Pallas kernels  115 us (31%)
  starting transfers between devices  66.1 us (18%)
  local copies, waits for them, and re-layouts  30.3 us (8%)
  between operations  14.6 us (4%)
  other arithmetic  6.67 us (2%)
    ppermute x59, waiting for transfers between devices, swap(): lax.ppermute(value, axis, [(i, i ^ k) for i in range(lax.axis_size(axis))])  125 us
    pallas_call x36, Pallas kernels, run(): pl.pallas_call(kernel, out_shape=tuple(outs), grid=grid, in_specs=list(in...  115 us
    ppermute x59, starting transfers between devices, swap(): lax.ppermute(value, axis, [(i, i ^ k) for i in range(lax.axis_size(axis))])  60.5 us
    unnamed x130, local copies, waits for them, and re-layouts  18.8 us
  transfers between devices with their start and end apart: 64, of which 23 were waited for; matrix products, arithmetic and copies ran while one was open for 5% of the time, Pallas kernels for 28%

profile of v2, /device:TPU:0, one launch (start us, length us, event | category | flops | bytes accessed | tf_op | source)
XLA Modules:
  0.0 369.6 jit_solution(16469373892073887013)
XLA Ops:
  14.4 3.9 %collective-permute-start = (bf16[16,1536]{1,0:T(8,128)(2,1)S(1)}, bf16[16,1536]{1,0:T(8,128)(2,1)S(1)}, u32[]{:S(2)}, u32[]{:S(2)}) collective-permute-start(bf16[16,1536]{1,0:T(8,128)(2,1)S(1)} %slice_bitcast_fusion), channel_id=1, source_target_pairs={{0,4},{4,8},{8,12},{1,5},{5,9},{9,13},{2,6},{6,10},{10,14},{3,7},{... | collective-permute-start | bytes 147464 | tf_op jit(solution)/shard_map/ppermute | solution.py:78
  31.3 11.5 %collective-permute-done.7.refs_0_ = bf16[2,96,1728]{2,1,0:T(8,128)(2,1)S(1)} collective-permute-done((bf16[2,96,1728]{2,1,0:T(8,128)(2,1)S(1)}, bf16[2,96,1728]{2,1,0:T(8,128)(2,1)S(1)}, u32[]{:S(2)}, u32[]{:S(2)}) %collective-permute-start.7) | collective-permute-done | bytes 663584 | tf_op jit(solution)/shard_map/ppermute | solution.py:72
  42.8 13.8 %collective-permute-done.8.refs_1_ = bf16[2,96,1728]{2,1,0:T(8,128)(2,1)S(1)} collective-permute-done((bf16[2,96,1728]{2,1,0:T(8,128)(2,1)S(1)}, bf16[2,96,1728]{2,1,0:T(8,128)(2,1)S(1)}, u32[]{:S(2)}, u32[]{:S(2)}) %collective-permute-start.8) | collective-permute-done | bytes 663584 | tf_op jit(solution)/shard_map/ppermute | solution.py:72
  62.6 9.6 %collective-permute-done.1.refs_2_ = bf16[144,1536]{1,0:T(8,128)(2,1)S(1)} collective-permute-done((bf16[144,1536]{1,0:T(8,128)(2,1)S(1)}, bf16[144,1536]{1,0:T(8,128)(2,1)S(1)}, u32[]{:S(2)}, u32[]{:S(2)}) %collective-permute-start.1) | collective-permute-done | bytes 442400 | tf_op jit(solution)/shard_map/ppermute | solution.py:72
  73.7 4.7 %collective-permute-done.2.refs_3_ = bf16[144,1536]{1,0:T(8,128)(2,1)S(1)} collective-permute-done((bf16[144,1536]{1,0:T(8,128)(2,1)S(1)}, bf16[144,1536]{1,0:T(8,128)(2,1)S(1)}, u32[]{:S(2)}, u32[]{:S(2)}) %collective-permute-start.2) | collective-permute-done | bytes 442400 | tf_op jit(solution)/shard_map/ppermute | solution.py:72
  86.2 6.4 %shard_map.183 = bf16[1,1536,1152]{2,1,0:T(8,128)(2,1)S(1)} custom-call(s32[5]{0:T(128)S(1)} %stack.87.refs_0_, bf16[384,4608]{1,0:T(8,128)(2,1)} %refs_1_.4, bf16[3,1,96,1152]{3,2,1,0:T(8,128)(2,1)} %bitcast.15.refs_2_, bf16[3,1,96,1152]{3,2,1,0:T(8,128)(2,1)S(1)} %bitcast.88, bf16[3,1,96,1152]{3,2,1,0:T(8,128)(2,1)} %bitcast.18.refs_4_, ...), custom_call_target="tpu_custom_call" | custom-call | flops 100000000 | bytes 1000 | tf_op jit(solution)/shard_map/pallas_call | solution.py:50
  92.6 4.3 %shard_map.185 = (f32[512,1152]{1,0:T(8,128)}, f32[64,384]{1,0:T(8,128)S(1)}, bf16[512,384]{1,0:T(8,128)(2,1)S(1)}, bf16[128,1536]{1,0:T(8,128)(2,1)S(1)}, bf16[...) custom-call(bf16[512,1536]{1,0:T(8,128)(2,1)S(1)} %get-tuple-element.85.refs_0_.refs_1_, ...), custom_call_target="tpu_custom_call" | custom-call | flops 550000000 | bytes 1000 | tf_op jit(solution)/shard_map/pallas_call | solution.py:50
  101.0 8.4 %shard_map.186 = (f32[512,1728]{1,0:T(8,128)S(1)}, bf16[768,512]{1,0:T(8,128)(2,1)}, bf16[768,512]{1,0:T(8,128)(2,1)}) custom-call(s32[3]{0:T(128)S(1)} %pad_add_fusion.refs_0_, bf16[128,1536]{1,0:T(8,128)(2,1)} %shard_map.184.refs_5_.refs_1_, bf16[128,1536]{1,0:T(8,128)(2,1)} %collective-permute-done.16.refs_2_, ...), custom_call_target="tpu_custom_call" | custom-call | flops 500000000 | bytes 1000 | tf_op jit(solution)/shard_map/pallas_call | solution.py:50
  109.5 3.2 collective-permute-done.14.refs_2_
  121.7 7.2 %shard_map.189.refs_5_.refs_1_.refs_2_.refs_3_ = bf16[2,1536,1728]{2,1,0:T(8,128)(2,1)} custom-call(s32[5]{0:T(128)S(1)} %stack.87.refs_0_, bf16[2,384,1728]{2,1,0:T(8,128)(2,1)S(1)} %pad_maximum_fusion.refs_1_, bf16[3,2,96,1728]{3,2,1,0:T(8,128)(2,1)S(1)} %shard_map.181.refs_5_.refs_6_.refs_1_.refs_2_, bf16[3,2,96,1728]{3,2,1,0:T(8,128)(2,1)} %shard_map.188.refs_3_, ...), custom_call_target="tpu_custom_call" | custom-call | flops 100000000 | bytes 1000 | tf_op jit(solution)/shard_map/pallas_call | solution.py:50
  128.9 6.9 %collective-permute-done.20.refs_3_ = bf16[128,1536]{1,0:T(8,128)(2,1)S(1)} collective-permute-done((bf16[128,1536]{1,0:T(8,128)(2,1)}, bf16[128,1536]{1,0:T(8,128)(2,1)S(1)}, u32[]{:S(2)}, u32[]{:S(2)}) %collective-permute-start.20) | collective-permute-done | bytes 393248 | tf_op jit(solution)/shard_map/ppermute | solution.py:72
  137.9 7.5 %shard_map.191 = (f32[512,1728]{1,0:T(8,128)}, bf16[16,32,1728]{2,1,0:T(8,128)(2,1)}) custom-call(bf16[512,1536]{1,0:T(8,128)(2,1)S(1)} %get-tuple-element.96.refs_0_, bf16[2,1536,1728]{2,1,0:T(8,128)(2,1)} %shard_map.189.refs_5_.refs_1_.refs_2_.refs_3_, f32[512,1728]{1,0:T(8,128)S(1)} %copy-done.1), custom_call_target="tpu_custom_call" | custom-call | flops 600000000 | bytes 1000 | tf_op jit(solution)/shard_map/pallas_call | solution.py:50
  145.4 4.0 %collective-permute-done.26.refs_3_ = bf16[16,32,1728]{2,1,0:T(8,128)(2,1)S(1)} collective-permute-done((bf16[16,32,1728]{2,1,0:T(8,128)(2,1)}, bf16[16,32,1728]{2,1,0:T(8,128)(2,1)S(1)}, u32[]{:S(2)}, u32[]{:S(2)}) %collective-permute-start.26) | collective-permute-done | bytes 1769504 | tf_op jit(solution)/shard_map/ppermute | solution.py:72
  149.4 6.1 %shard_map.193.refs_4_ = bf16[4,192,1728]{2,1,0:T(8,128)(2,1)} custom-call(bf16[768,512]{1,0:T(8,128)(2,1)S(1)} %get-tuple-element.98.refs_0_, bf16[768,512]{1,0:T(8,128)(2,1)S(1)} %collective-permute-done.25.refs_1_, bf16[16,32,1728]{2,1,0:T(8,128)(2,1)} %shard_map.192.refs_2_.refs_1_, bf16[16,32,1728]{2,1,0:T(8,128)(2,1)S(1)} %collective-permute-done.26.refs_3_), custom_call_target="tpu_custom_call" | custom-call | flops 500000000 | bytes 1000 | tf_op jit(solution)/shard_map/pallas_call | solution.py:50
  157.6 8.4 %shard_map.194 = (bf16[16,32,1728]{2,1,0:T(8,128)(2,1)}, bf16[16,32,1728]{2,1,0:T(8,128)(2,1)}) custom-call(bf16[512,1536]{1,0:T(8,128)(2,1)S(1)} %get-tuple-element.96.refs_0_, bf16[2,1536,1728]{2,1,0:T(8,128)(2,1)} %shard_map.189.refs_5_.refs_1_.refs_2_.refs_3_, f32[512,1728]{1,0:T(8,128)} %get-tuple-element.97.refs_2_, f32[512,1728]{1,0:T(8,128)S(1)} %copy-done.2, ...), custom_call_target="tpu_custom_call" | custom-call | flops 700000000 | bytes 1000 | tf_op jit(solution)/shard_map/pallas_call | solution.py:50
  166.7 10.3 %shard_map.195 = (bf16[128,1536]{1,0:T(8,128)(2,1)}, bf16[128,1536]{1,0:T(8,128)(2,1)}, bf16[128,1536]{1,0:T(8,128)(2,1)}, bf16[128,1536]{1,0:T(8,128)(2,1)}) custom-call(bf16[16,32,1728]{2,1,0:T(8,128)(2,1)} %get-tuple-element.104.refs_0_.refs_4_, bf16[16,32,1728]{2,1,0:T(8,128)(2,1)} %shard_map.192.refs_2_.refs_1_, ...), custom_call_target="tpu_custom_call" | custom-call | flops 700000000 | bytes 1000 | tf_op jit(solution)/shard_map/pallas_call | solution.py:50
  177.0 11.5 %shard_map.196.refs_2_ = bf16[4,192,3456]{2,1,0:T(8,128)(2,1)} custom-call(bf16[768,512]{1,0:T(8,128)(2,1)S(1)} %copy-done.21, bf16[768,512]{1,0:T(8,128)(2,1)S(1)} %collective-permute-done.25.refs_1_, bf16[768,512]{1,0:T(8,128)(2,1)S(1)} %copy-done.41, bf16[768,512]{1,0:T(8,128)(2,1)S(1)} %collective-permute-done.27.refs_3_, ...), custom_call_target="tpu_custom_call" | custom-call | flops 1000000000 | bytes 1000 | tf_op jit(solution)/shard_map/pallas_call | solution.py:50
  192.3 8.6 %collective-permute-done.33.refs_1_ = bf16[128,1536]{1,0:T(8,128)(2,1)S(1)} collective-permute-done((bf16[128,1536]{1,0:T(8,128)(2,1)}, bf16[128,1536]{1,0:T(8,128)(2,1)S(1)}, u32[]{:S(2)}, u32[]{:S(2)}) %collective-permute-start.33) | collective-permute-done | bytes 393248 | tf_op jit(solution)/shard_map/ppermute | solution.py:72
  200.9 9.0 %collective-permute-done.34.refs_2_ = bf16[128,1536]{1,0:T(8,128)(2,1)S(1)} collective-permute-done((bf16[128,1536]{1,0:T(8,128)(2,1)}, bf16[128,1536]{1,0:T(8,128)(2,1)S(1)}, u32[]{:S(2)}, u32[]{:S(2)}) %collective-permute-start.34) | collective-permute-done | bytes 393248 | tf_op jit(solution)/shard_map/ppermute | solution.py:72
  219.8 5.4 %collective-permute-done.36.refs_1_ = bf16[128,1536]{1,0:T(8,128)(2,1)S(1)} collective-permute-done((bf16[128,1536]{1,0:T(8,128)(2,1)S(1)}, bf16[128,1536]{1,0:T(8,128)(2,1)S(1)}, u32[]{:S(2)}, u32[]{:S(2)}) %collective-permute-start.36) | collective-permute-done | bytes 393248 | tf_op jit(solution)/shard_map/ppermute | solution.py:72
  226.6 8.0 %collective-permute-done.37.refs_2_ = bf16[128,1536]{1,0:T(8,128)(2,1)S(1)} collective-permute-done((bf16[128,1536]{1,0:T(8,128)(2,1)S(1)}, bf16[128,1536]{1,0:T(8,128)(2,1)S(1)}, u32[]{:S(2)}, u32[]{:S(2)}) %collective-permute-start.37) | collective-permute-done | bytes 393248 | tf_op jit(solution)/shard_map/ppermute | solution.py:72
  239.4 6.0 %collective-permute-done.39.refs_2_ = f32[32,384]{1,0:T(8,128)S(1)} collective-permute-done((f32[32,384]{1,0:T(8,128)S(1)}, f32[32,384]{1,0:T(8,128)S(1)}, u32[]{:S(2)}, u32[]{:S(2)}) %collective-permute-start.39) | collective-permute-done | bytes 49184 | tf_op jit(solution)/shard_map/ppermute | solution.py:78
  245.4 3.7 %shard_map.201 = (bf16[512,1152]{1,0:T(8,128)(2,1)S(1)}, bf16[4,192,1152]{2,1,0:T(8,128)(2,1)}, bf16[192,1536]{1,0:T(8,128)(2,1)}) custom-call(s32[3]{0:T(128)S(1)} %pad_add_fusion.refs_0_, f32[512,384]{1,0:T(8,128)S(1)} %get-tuple-element.117.refs_1_, f32[32,384]{1,0:T(8,128)S(1)} %collective-permute-done.39.refs_2_, ...), custom_call_target="tpu_custom_call" | custom-call | flops 300000000 | bytes 1000 | tf_op jit(solution)/shard_map/pallas_call | solution.py:50
  250.7 5.6 %shard_map.202 = (bf16[128,1536]{1,0:T(8,128)(2,1)}, bf16[128,1536]{1,0:T(8,128)(2,1)}, bf16[128,1536]{1,0:T(8,128)(2,1)}, bf16[128,1536]{1,0:T(8,128)(2,1)}) custom-call(bf16[512,1152]{1,0:T(8,128)(2,1)} %copy-done.12, bf16[1536,1152]{1,0:T(8,128)(2,1)} %bitcast.81), custom_call_target="tpu_custom_call" | custom-call | flops 400000000 | bytes 1000 | tf_op jit(solution)/shard_map/pallas_call | solution.py:50
  263.8 3.5 collective-permute-start.50
  267.8 9.0 %collective-permute-done.48.refs_2_ = bf16[4,48,1152]{2,1,0:T(8,128)(2,1)S(1)} collective-permute-done((bf16[4,48,1152]{2,1,0:T(8,128)(2,1)S(1)}, bf16[4,48,1152]{2,1,0:T(8,128)(2,1)S(1)}, u32[]{:S(2)}, u32[]{:S(2)}) %collective-permute-start.48) | collective-permute-done | bytes 442400 | tf_op jit(solution)/shard_map/ppermute | solution.py:72
  276.8 6.7 %shard_map.204 = (bf16[128,1536]{1,0:T(8,128)(2,1)}, bf16[128,1536]{1,0:T(8,128)(2,1)}, bf16[128,1536]{1,0:T(8,128)(2,1)}, bf16[128,1536]{1,0:T(8,128)(2,1)}) custom-call(bf16[16,32,1728]{2,1,0:T(8,128)(2,1)} %get-tuple-element.101.refs_6_.refs_0_, bf16[1728,1536]{1,0:T(8,128)(2,1)} %refs_1_.5, bf16[4,192,1152]{2,1,0:T(8,128)(2,1)S(1)} %get-tuple-element.126.refs_2_), custom_call_target="tpu_custom_call" | custom-call | flops 400000000 | bytes 1000 | tf_op jit(solution)/shard_map/pallas_call | solution.py:50
  294.9 8.6 %collective-permute-done.46.refs_2_ = bf16[128,1536]{1,0:T(8,128)(2,1)} collective-permute-done((bf16[128,1536]{1,0:T(8,128)(2,1)}, bf16[128,1536]{1,0:T(8,128)(2,1)}, u32[]{:S(2)}, u32[]{:S(2)}) %collective-permute-start.46) | collective-permute-done | bytes 393248 | tf_op jit(solution)/shard_map/ppermute | solution.py:72
  321.9 9.1 %collective-permute-done.43.refs_1_ = bf16[128,1536]{1,0:T(8,128)(2,1)S(1)} collective-permute-done((bf16[128,1536]{1,0:T(8,128)(2,1)}, bf16[128,1536]{1,0:T(8,128)(2,1)S(1)}, u32[]{:S(2)}, u32[]{:S(2)}) %collective-permute-start.43) | collective-permute-done | bytes 393248 | tf_op jit(solution)/shard_map/ppermute | solution.py:72
  335.4 3.7 collective-permute-start.57
  340.9 3.4 collective-permute-done.56
  355.1 5.9 %reduce-scatter.8.cloned.1.call-done = bf16[1,48,6144]{2,1,0:T(8,128)(2,1)} async-done(((bf16[4,48,6144]{2,1,0:T(8,128)(2,1)}), bf16[1,48,6144]{2,1,0:T(8,128)(2,1)}) %reduce-scatter.8.cloned.1.call-update) | async-done | bytes 589840 | tf_op jit(solution)/shard_map/reduce_scatter | solution.py:842
  (293 shorter events, 130.9 us)
Async XLA Ops:
  7.2 299.3 %reduce-scatter.6.cloned.1.call-start = ((), (), s32[]{:S(2)}) async-start(), calls=%async_computation.4 | async-start | bytes 3440640 | tf_op jit(solution)/shard_map/reduce_scatter | solution.py:535
  25.9 30.8 %collective-permute-start.8 = (bf16[2,96,1728]{2,1,0:T(8,128)(2,1)S(1)}, bf16[2,96,1728]{2,1,0:T(8,128)(2,1)S(1)}, u32[]{:S(2)}, u32[]{:S(2)}) collective-permute-start(bf16[2,96,1728]{2,1,0:T(8,128)(2,1)S(1)} %get-tuple-element.83), channel_id=1, source_target_pairs={{0,2},{1,3},{2,0},{3,1},{4,6},{5,7},{6,4},{7,5},{8,10},{9,11},{10,... | collective-permute-start | bytes 1990664 | tf_op jit(solution)/shard_map/ppermute | solution.py:72
  26.5 30.2 %collective-permute-start.9 = (bf16[2,96,1728]{2,1,0:T(8,128)(2,1)S(1)}, bf16[2,96,1728]{2,1,0:T(8,128)(2,1)S(1)}, u32[]{:S(2)}, u32[]{:S(2)}) collective-permute-start(bf16[2,96,1728]{2,1,0:T(8,128)(2,1)S(1)} %get-tuple-element.84), channel_id=1, source_target_pairs={{0,3},{1,2},{2,1},{3,0},{4,7},{5,6},{6,5},{7,4},{8,11},{9,10},{10,... | collective-permute-start | bytes 1990664 | tf_op jit(solution)/shard_map/ppermute | solution.py:72
  29.7 27.0 %collective-permute-start.10 = (bf16[3,96,1152]{2,1,0:T(8,128)(2,1)}, bf16[3,96,1152]{2,1,0:T(8,128)(2,1)S(1)}, u32[]{:S(2)}, u32[]{:S(2)}) collective-permute-start(bf16[3,96,1152]{2,1,0:T(8,128)(2,1)} %shard_map.180), channel_id=1, source_target_pairs={{0,4},{4,0},{8,12},{12,8},{1,5},{5,1},{9,13},{13,9},{2,6},{6,2},{1... | collective-permute-start | bytes 1990664 | tf_op jit(solution)/shard_map/ppermute | solution.py:72
  57.5 55.8 %collective-permute-start.22 = (bf16[3,2,96,1728]{3,2,1,0:T(8,128)(2,1)S(1)}, bf16[3,2,96,1728]{3,2,1,0:T(8,128)(2,1)}, u32[]{:S(2)}, u32[]{:S(2)}) collective-permute-start(bf16[3,2,96,1728]{3,2,1,0:T(8,128)(2,1)S(1)} %shard_map.181.refs_5_.refs_6_.refs_1_.refs_2_), channel_id=1, source_target_pairs={{0,4},{4,0},{8,12},{12,8},{1,5},{5,1},{9,13},{13,9},{2,6},{6,2},{1... | collective-permute-start | bytes 5971976 | tf_op jit(solution)/shard_map/ppermute | solution.py:72
  59.6 18.8 %collective-permute-start.2 = (bf16[144,1536]{1,0:T(8,128)(2,1)S(1)}, bf16[144,1536]{1,0:T(8,128)(2,1)S(1)}, u32[]{:S(2)}, u32[]{:S(2)}) collective-permute-start(bf16[144,1536]{1,0:T(8,128)(2,1)S(1)} %shard_map.177.refs_3_.refs_1_), channel_id=1, source_target_pairs={{0,2},{1,3},{2,0},{3,1},{4,6},{5,7},{6,4},{7,5},{8,10},{9,11},{10,... | collective-permute-start | bytes 1327112 | tf_op jit(solution)/shard_map/ppermute | solution.py:72
  60.8 19.0 %collective-permute-start.3 = (bf16[144,1536]{1,0:T(8,128)(2,1)S(1)}, bf16[144,1536]{1,0:T(8,128)(2,1)S(1)}, u32[]{:S(2)}, u32[]{:S(2)}) collective-permute-start(bf16[144,1536]{1,0:T(8,128)(2,1)S(1)} %shard_map.177.refs_3_.refs_1_), channel_id=1, source_target_pairs={{0,3},{1,2},{2,1},{3,0},{4,7},{5,6},{6,5},{7,4},{8,11},{9,10},{10,... | collective-permute-start | bytes 1327112 | tf_op jit(solution)/shard_map/ppermute | solution.py:72
  62.6 22.2 %collective-permute-start.11 = (bf16[3,96,1152]{2,1,0:T(8,128)(2,1)}, bf16[3,96,1152]{2,1,0:T(8,128)(2,1)}, u32[]{:S(2)}, u32[]{:S(2)}) collective-permute-start(bf16[3,96,1152]{2,1,0:T(8,128)(2,1)} %shard_map.180), channel_id=1, source_target_pairs={{0,16},{16,0},{1,17},{17,1},{2,18},{18,2},{3,19},{19,3},{4,20},{20... | collective-permute-start | bytes 1990664 | tf_op jit(solution)/shard_map/ppermute | solution.py:72
  78.5 19.4 %collective-permute-start.16 = (bf16[128,1536]{1,0:T(8,128)(2,1)}, bf16[128,1536]{1,0:T(8,128)(2,1)}, u32[]{:S(2)}, u32[]{:S(2)}) collective-permute-start(bf16[128,1536]{1,0:T(8,128)(2,1)} %shard_map.184.refs_5_.refs_1_), channel_id=1, source_target_pairs={{0,1},{1,0},{2,3},{3,2},{4,5},{5,4},{6,7},{7,6},{8,9},{9,8},{10,11... | collective-permute-start | bytes 1179656 | tf_op jit(solution)/shard_map/ppermute | solution.py:72
  80.6 19.1 %collective-permute-start.17 = (bf16[128,1536]{1,0:T(8,128)(2,1)}, bf16[128,1536]{1,0:T(8,128)(2,1)}, u32[]{:S(2)}, u32[]{:S(2)}) collective-permute-start(bf16[128,1536]{1,0:T(8,128)(2,1)} %shard_map.184.refs_5_.refs_1_), channel_id=1, source_target_pairs={{0,2},{1,3},{2,0},{3,1},{4,6},{5,7},{6,4},{7,5},{8,10},{9,11},{10,... | collective-permute-start | bytes 1179656 | tf_op jit(solution)/shard_map/ppermute | solution.py:72
  101.0 20.0 %collective-permute-start.23 = (bf16[3,2,96,1728]{3,2,1,0:T(8,128)(2,1)S(1)}, bf16[3,2,96,1728]{3,2,1,0:T(8,128)(2,1)}, u32[]{:S(2)}, u32[]{:S(2)}) collective-permute-start(bf16[3,2,96,1728]{3,2,1,0:T(8,128)(2,1)S(1)} %shard_map.181.refs_5_.refs_6_.refs_1_.refs_2_), channel_id=1, source_target_pairs={{0,16},{16,0},{1,17},{17,1},{2,18},{18,2},{3,19},{19,3},{4,20},{20... | collective-permute-start | bytes 5971976 | tf_op jit(solution)/shard_map/ppermute | solution.py:72
  116.0 19.9 %collective-permute-start.20 = (bf16[128,1536]{1,0:T(8,128)(2,1)}, bf16[128,1536]{1,0:T(8,128)(2,1)S(1)}, u32[]{:S(2)}, u32[]{:S(2)}) collective-permute-start(bf16[128,1536]{1,0:T(8,128)(2,1)} %copy-done.18), channel_id=1, source_target_pairs={{0,2},{1,3},{2,0},{3,1},{4,6},{5,7},{6,4},{7,5},{8,10},{9,11},{10,... | collective-permute-start | bytes 1179656 | tf_op jit(solution)/shard_map/ppermute | solution.py:72
  117.2 18.6 %collective-permute-start.21 = (bf16[128,1536]{1,0:T(8,128)(2,1)}, bf16[128,1536]{1,0:T(8,128)(2,1)S(1)}, u32[]{:S(2)}, u32[]{:S(2)}) collective-permute-start(bf16[128,1536]{1,0:T(8,128)(2,1)} %copy-done.18), channel_id=1, source_target_pairs={{0,3},{1,2},{2,1},{3,0},{4,7},{5,6},{6,5},{7,4},{8,11},{9,10},{10,... | collective-permute-start | bytes 1179656 | tf_op jit(solution)/shard_map/ppermute | solution.py:72
  155.5 152.9 %reduce-scatter.4.cloned.1.call-start = ((), (), s32[]{:S(2)}) async-start(), calls=%async_computation.3 | async-start | bytes 6635520 | tf_op jit(solution)/shard_map/reduce_scatter | solution.py:624
  188.6 172.3 %reduce-scatter.8.cloned.1.call-start = ((), (), s32[]{:S(2)}) async-start(), calls=%async_computation.5 | async-start | bytes 2949120 | tf_op jit(solution)/shard_map/reduce_scatter | solution.py:842
  190.2 19.7 %collective-permute-start.34 = (bf16[128,1536]{1,0:T(8,128)(2,1)}, bf16[128,1536]{1,0:T(8,128)(2,1)S(1)}, u32[]{:S(2)}, u32[]{:S(2)}) collective-permute-start(bf16[128,1536]{1,0:T(8,128)(2,1)} %get-tuple-element.111), channel_id=1, source_target_pairs={{0,2},{1,3},{2,0},{3,1},{4,6},{5,7},{6,4},{7,5},{8,10},{9,11},{10,... | collective-permute-start | bytes 1179656 | tf_op jit(solution)/shard_map/ppermute | solution.py:72
  191.0 18.9 %collective-permute-start.35 = (bf16[128,1536]{1,0:T(8,128)(2,1)S(1)}, bf16[128,1536]{1,0:T(8,128)(2,1)S(1)}, u32[]{:S(2)}, u32[]{:S(2)}) collective-permute-start(bf16[128,1536]{1,0:T(8,128)(2,1)S(1)} %copy-done.64), channel_id=1, source_target_pairs={{0,3},{1,2},{2,1},{3,0},{4,7},{5,6},{6,5},{7,4},{8,11},{9,10},{10,... | collective-permute-start | bytes 1179656 | tf_op jit(solution)/shard_map/ppermute | solution.py:72
  213.7 20.9 %collective-permute-start.37 = (bf16[128,1536]{1,0:T(8,128)(2,1)S(1)}, bf16[128,1536]{1,0:T(8,128)(2,1)S(1)}, u32[]{:S(2)}, u32[]{:S(2)}) collective-permute-start(bf16[128,1536]{1,0:T(8,128)(2,1)S(1)} %get-tuple-element.113.refs_6_.refs_0_), channel_id=1, source_target_pairs={{0,2},{1,3},{2,0},{3,1},{4,6},{5,7},{6,4},{7,5},{8,10},{9,11},{10,... | collective-permute-start | bytes 1179656 | tf_op jit(solution)/shard_map/ppermute | solution.py:72
  215.1 19.5 %collective-permute-start.38 = (bf16[128,1536]{1,0:T(8,128)(2,1)S(1)}, bf16[128,1536]{1,0:T(8,128)(2,1)S(1)}, u32[]{:S(2)}, u32[]{:S(2)}) collective-permute-start(bf16[128,1536]{1,0:T(8,128)(2,1)S(1)} %get-tuple-element.113.refs_6_.refs_0_), channel_id=1, source_target_pairs={{0,3},{1,2},{2,1},{3,0},{4,7},{5,6},{6,5},{7,4},{8,11},{9,10},{10,... | collective-permute-start | bytes 1179656 | tf_op jit(solution)/shard_map/ppermute | solution.py:72
  217.7 20.0 %collective-permute-start.30 = (bf16[512,96]{1,0:T(8,128)(2,1)S(1)}, bf16[512,96]{1,0:T(8,128)(2,1)S(1)}, u32[]{:S(2)}, u32[]{:S(2)}) collective-permute-start(bf16[512,96]{1,0:T(8,128)(2,1)S(1)} %get-tuple-element.107), channel_id=1, source_target_pairs={{0,1},{1,0},{2,3},{3,2},{4,5},{5,4},{6,7},{7,6},{8,9},{9,8},{10,11... | collective-permute-start | bytes 294920 | tf_op jit(solution)/shard_map/ppermute | solution.py:72
  218.3 19.6 %collective-permute-start.31 = (bf16[512,96]{1,0:T(8,128)(2,1)S(1)}, bf16[512,96]{1,0:T(8,128)(2,1)S(1)}, u32[]{:S(2)}, u32[]{:S(2)}) collective-permute-start(bf16[512,96]{1,0:T(8,128)(2,1)S(1)} %get-tuple-element.108), channel_id=1, source_target_pairs={{0,2},{1,3},{2,0},{3,1},{4,6},{5,7},{6,4},{7,5},{8,10},{9,11},{10,... | collective-permute-start | bytes 294920 | tf_op jit(solution)/shard_map/ppermute | solution.py:72
  263.8 22.8 %collective-permute-start.49 = (bf16[4,48,1152]{2,1,0:T(8,128)(2,1)}, bf16[4,48,1152]{2,1,0:T(8,128)(2,1)}, u32[]{:S(2)}, u32[]{:S(2)}) collective-permute-start(bf16[4,48,1152]{2,1,0:T(8,128)(2,1)} %get-tuple-element.155), channel_id=1, source_target_pairs={{0,2},{1,3},{2,0},{3,1},{4,6},{5,7},{6,4},{7,5},{8,10},{9,11},{10,... | collective-permute-start | bytes 1327112 | tf_op jit(solution)/shard_map/ppermute | solution.py:72
  263.8 24.9 %collective-permute-start.50 = (bf16[4,48,1152]{2,1,0:T(8,128)(2,1)}, bf16[4,48,1152]{2,1,0:T(8,128)(2,1)}, u32[]{:S(2)}, u32[]{:S(2)}) collective-permute-start(bf16[4,48,1152]{2,1,0:T(8,128)(2,1)} %get-tuple-element.154), channel_id=1, source_target_pairs={{0,3},{1,2},{2,1},{3,0},{4,7},{5,6},{6,5},{7,4},{8,11},{9,10},{10,... | collective-permute-start | bytes 1327112 | tf_op jit(solution)/shard_map/ppermute | solution.py:72
  267.2 27.6 %collective-permute-start.45 = (bf16[128,1536]{1,0:T(8,128)(2,1)}, bf16[128,1536]{1,0:T(8,128)(2,1)}, u32[]{:S(2)}, u32[]{:S(2)}) collective-permute-start(bf16[128,1536]{1,0:T(8,128)(2,1)} %get-tuple-element.131), channel_id=1, source_target_pairs={{0,1},{1,0},{2,3},{3,2},{4,5},{5,4},{6,7},{7,6},{8,9},{9,8},{10,11... | collective-permute-start | bytes 1179656 | tf_op jit(solution)/shard_map/ppermute | solution.py:72
  267.3 36.2 %collective-permute-start.46 = (bf16[128,1536]{1,0:T(8,128)(2,1)}, bf16[128,1536]{1,0:T(8,128)(2,1)}, u32[]{:S(2)}, u32[]{:S(2)}) collective-permute-start(bf16[128,1536]{1,0:T(8,128)(2,1)} %get-tuple-element.132), channel_id=1, source_target_pairs={{0,2},{1,3},{2,0},{3,1},{4,6},{5,7},{6,4},{7,5},{8,10},{9,11},{10,... | collective-permute-start | bytes 1179656 | tf_op jit(solution)/shard_map/ppermute | solution.py:72
  276.8 26.7 %collective-permute-start.47 = (bf16[128,1536]{1,0:T(8,128)(2,1)}, bf16[128,1536]{1,0:T(8,128)(2,1)}, u32[]{:S(2)}, u32[]{:S(2)}) collective-permute-start(bf16[128,1536]{1,0:T(8,128)(2,1)} %get-tuple-element.133), channel_id=1, source_target_pairs={{0,3},{1,2},{2,1},{3,0},{4,7},{5,6},{6,5},{7,4},{8,11},{9,10},{10,... | collective-permute-start | bytes 1179656 | tf_op jit(solution)/shard_map/ppermute | solution.py:72
  286.6 33.3 %collective-permute-start.42 = (bf16[128,1536]{1,0:T(8,128)(2,1)}, bf16[128,1536]{1,0:T(8,128)(2,1)S(1)}, u32[]{:S(2)}, u32[]{:S(2)}) collective-permute-start(bf16[128,1536]{1,0:T(8,128)(2,1)} %get-tuple-element.128), channel_id=1, source_target_pairs={{0,1},{1,0},{2,3},{3,2},{4,5},{5,4},{6,7},{7,6},{8,9},{9,8},{10,11... | collective-permute-start | bytes 1179656 | tf_op jit(solution)/shard_map/ppermute | solution.py:72
  288.7 42.3 %collective-permute-start.43 = (bf16[128,1536]{1,0:T(8,128)(2,1)}, bf16[128,1536]{1,0:T(8,128)(2,1)S(1)}, u32[]{:S(2)}, u32[]{:S(2)}) collective-permute-start(bf16[128,1536]{1,0:T(8,128)(2,1)} %get-tuple-element.129), channel_id=1, source_target_pairs={{0,2},{1,3},{2,0},{3,1},{4,6},{5,7},{6,4},{7,5},{8,10},{9,11},{10,... | collective-permute-start | bytes 1179656 | tf_op jit(solution)/shard_map/ppermute | solution.py:72
  294.8 39.0 %collective-permute-start.44 = (bf16[128,1536]{1,0:T(8,128)(2,1)}, bf16[128,1536]{1,0:T(8,128)(2,1)}, u32[]{:S(2)}, u32[]{:S(2)}) collective-permute-start(bf16[128,1536]{1,0:T(8,128)(2,1)} %get-tuple-element.130), channel_id=1, source_target_pairs={{0,3},{1,2},{2,1},{3,0},{4,7},{5,6},{6,5},{7,4},{8,11},{9,10},{10,... | collective-permute-start | bytes 1179656 | tf_op jit(solution)/shard_map/ppermute | solution.py:72
  313.1 32.1 %collective-permute-start.53 = (bf16[48,5184]{1,0:T(8,128)(2,1)}, bf16[48,5184]{1,0:T(8,128)(2,1)S(1)}, u32[]{:S(2)}, u32[]{:S(2)}) collective-permute-start(bf16[48,5184]{1,0:T(8,128)(2,1)} %pad_maximum_fusion.7), channel_id=1, source_target_pairs={{0,3},{1,2},{2,1},{3,0},{4,7},{5,6},{6,5},{7,4},{8,11},{9,10},{10,... | collective-permute-start | bytes 1493000 | tf_op jit(solution)/shard_map/ppermute | solution.py:72
  316.0 19.4 %collective-permute-start.55 = (f32[5,1536]{1,0:T(8,128)}, f32[5,1536]{1,0:T(8,128)}, u32[]{:S(2)}, u32[]{:S(2)}) collective-permute-start(f32[5,1536]{1,0:T(8,128)} %add.140), channel_id=1, source_target_pairs={{0,4},{4,0},{8,12},{12,8},{1,5},{5,1},{9,13},{13,9},{2,6},{6,2},{1... | collective-permute-start | bytes 92168 | tf_op jit(solution)/shard_map/ppermute | solution.py:72
  319.9 25.3 %collective-permute-start.52 = (bf16[48,5184]{1,0:T(8,128)(2,1)}, bf16[48,5184]{1,0:T(8,128)(2,1)S(1)}, u32[]{:S(2)}, u32[]{:S(2)}) collective-permute-start(bf16[48,5184]{1,0:T(8,128)(2,1)} %pad_maximum_fusion.6), channel_id=1, source_target_pairs={{0,2},{1,3},{2,0},{3,1},{4,6},{5,7},{6,4},{7,5},{8,10},{9,11},{10,... | collective-permute-start | bytes 1493000 | tf_op jit(solution)/shard_map/ppermute | solution.py:72
  (97 other events, 898.3 us)
Sparse Core Ops, SparseCore 0:
  155.6 53.2 reduce-scatter.5
  211.2 95.5 reduce-scatter.3
  309.2 51.6 reduce-scatter.7

commit v3 on v2

--- a/solution.py
+++ b/solution.py
@@ -221,7 +221,7 @@
             limit=6,
         )[0]
 
-    def assemble(own, parts, after=(), out=shape, out_spec=VMEM, limit=14):
+    def assemble(own, parts, after=(), out=shape, out_spec=VMEM, in_spec=ANY, limit=14):
         planes, columns = parts[0][0].shape[1], parts[0][0].shape[3]
         count = len(others)
         arrays = [p for p, _ in parts]
@@ -255,7 +255,7 @@
             body,
             [out((planes, width, columns))],
             [starts, own, *arrays],
-            in_specs=[SMEM] + [VMEM] * (1 + len(arrays)),
+            in_specs=[SMEM] + [in_spec] * (1 + len(arrays)),
             out_specs=[out_spec],
             scratch=[pltpu.SemaphoreType.DMA((planes * (4 + len(arrays) * count),))],
             after=after,
@@ -392,7 +392,7 @@
         mixer_body,
         [
             far((group, 3 * part), f32),
-            shape((shards * edge, part), f32),
+            far((shards * edge, part), f32),
             shape((group, part)),
         ]
         + [shape((rows, width))] * shards,
@@ -466,6 +466,7 @@
         (normed_two,),
         out=far,
         out_spec=ANY,
+        in_spec=VMEM,
         limit=20,
     )
     w_both = in_far(w_both)
@@ -488,6 +489,8 @@
 
     bundle = 32
     units = (group // bundle, bundle, hidden)
+    wide = 896
+    wide_units = tiles((group // bundle, bundle, wide), 2)
     unit_tiles = tiles((group // bundle, bundle, tile), 2)
     def gate_body(all_ref, w_ref, dh_ref, g_ref, du_ref):
         gate_ = mm(all_ref[...], w_ref[...])
@@ -499,15 +502,15 @@
         gate_body,
         [far((group, hidden), f32), far(units)],
         [two_all, w_both, d_hidden],
-        grid=(h_steps,),
+        grid=(pl.cdiv(hidden, wide),),
         in_specs=[
             whole(two_all),
-            pl.BlockSpec((None, width, tile), lambda step: (0, 0, step)),
-            tiles((group, tile), 1),
+            pl.BlockSpec((None, width, wide), lambda step: (0, 0, step)),
+            tiles((group, wide), 1),
         ],
-        out_specs=[tiles((group, tile), 1), unit_tiles],
+        out_specs=[tiles((group, wide), 1), wide_units],
         us=6,
-        limit=16,
+        limit=18,
     )
     gate = in_far(gate)
     d_up = wait_for(d_up, two_come, keep=True)
@@ -516,21 +519,33 @@
     def flat(ref):
         return ref[...].reshape(group, ref.shape[2])
 
-    def up_sum_body(own_ref, come_ref, du_ref, duc_ref, out_ref):
-        total = mm(own_ref[...], flat(du_ref)) + mm(come_ref[...], flat(duc_ref))
-        out_ref[...] = total.astype(bf16).reshape(blocks, chunk, tile)
+    def up_own_body(own_ref, du_ref, out_ref):
+        out_ref[...] = mm(own_ref[...], flat(du_ref)).astype(bf16)
+
+    (up_own,) = run(
+        up_own_body,
+        [shape((half, hidden))],
+        [two_keep, in_far(d_up)],
+        grid=(pl.cdiv(hidden, wide),),
+        in_specs=[whole(turned), wide_units],
+        out_specs=[tiles((half, wide), 1)],
+        us=3,
+        limit=8,
+    )
+
+    def up_sum_body(term_ref, come_ref, duc_ref, out_ref):
+        total = term_ref[...].astype(f32) + mm(come_ref[...], flat(duc_ref))
+        out_ref[...] = total.astype(bf16).reshape(blocks, chunk, wide)
 
     (up_both,) = run(
         up_sum_body,
-        [shape((blocks, chunk, hidden))],
-        [two_keep, two_come, d_up, d_up_come],
-        grid=(h_steps,),
-        in_specs=[whole(turned), whole(turned), unit_tiles, unit_tiles],
-        out_specs=[tiles((blocks, chunk, tile), 2)],
+        [far((blocks, chunk, hidden))],
+        [up_own, two_come, d_up_come],
+        grid=(pl.cdiv(hidden, wide),),
+        in_specs=[tiles((half, wide), 1), whole(turned), wide_units],
+        out_specs=[tiles((blocks, chunk, wide), 2)],
         us=5,
-        limit=14,
-        hbm=True,
-        near=(0, 1, 3),
+        limit=11,
     )
     up_sum = lax.psum_scatter(up_both, "seq", scatter_dimension=0, tiled=True).reshape(chunk, hidden)
 

time: 371 us -> 370 us (level)
  Pallas kernels: 115 us -> 111 us
    pallas_call x36 -> x37, Pallas kernels: 115 us -> 111 us  [run(): pl.pallas_call(kernel, out_shape=tuple(outs), grid=grid, in_specs=list(in...]
  transfers between devices with their start and end apart: 64 -> 64, of which waited for: 23 -> 25; matrix products, arithmetic and copies ran while one was open for 5% -> 5% of each run, Pallas kernels for 28% -> 28%
where the time goes in v3:
time: 370 us; the launch traced here: 368 us
  waiting for transfers between devices  138 us (37%)
  Pallas kernels  111 us (30%)
  starting transfers between devices  66.8 us (18%)
  local copies, waits for them, and re-layouts  30.9 us (8%)
  between operations  14.5 us (4%)
  other arithmetic  6.61 us (2%)
    ppermute x59, waiting for transfers between devices, swap(): lax.ppermute(value, axis, [(i, i ^ k) for i in range(lax.axis_size(axis))])  125 us
    pallas_call x37, Pallas kernels, run(): pl.pallas_call(kernel, out_shape=tuple(outs), grid=grid, in_specs=list(in...  111 us
    ppermute x59, starting transfers between devices, swap(): lax.ppermute(value, axis, [(i, i ^ k) for i in range(lax.axis_size(axis))])  60.3 us
    unnamed x130, local copies, waits for them, and re-layouts  18.5 us
    reduce_scatter x1, waiting for transfers between devices, on_device(): lax.psum_scatter(mix_both, 'seq', scatter_dimension=0, tiled=True)  9.05 us
  transfers between devices with their start and end apart: 64, of which 25 were waited for; matrix products, arithmetic and copies ran while one was open for 5% of the time, Pallas kernels for 28%

profile of v3, /device:TPU:0, one launch (start us, length us, event | category | flops | bytes accessed | tf_op | source)
XLA Modules:
  0.0 368.4 jit_solution(12619852681483164910)
XLA Ops:
  8.0 4.9 %collective-permute-start = (bf16[16,1536]{1,0:T(8,128)(2,1)S(1)}, bf16[16,1536]{1,0:T(8,128)(2,1)S(1)}, u32[]{:S(2)}, u32[]{:S(2)}) collective-permute-start(bf16[16,1536]{1,0:T(8,128)(2,1)S(1)} %slice_bitcast_fusion), channel_id=1, source_target_pairs={{0,4},{4,8},{8,12},{1,5},{5,9},{9,13},{2,6},{6,10},{10,14},{3,7},{... | collective-permute-start | bytes 147464 | tf_op jit(solution)/shard_map/ppermute | solution.py:78
  23.3 4.5 %collective-permute-done.5.refs_4_.refs_1_ = bf16[96,1152]{1,0:T(8,128)(2,1)S(1)} collective-permute-done((bf16[96,1152]{1,0:T(8,128)(2,1)S(1)}, bf16[96,1152]{1,0:T(8,128)(2,1)S(1)}, u32[]{:S(2)}, u32[]{:S(2)}) %collective-permute-start.5) | collective-permute-done | bytes 221216 | tf_op jit(solution)/shard_map/ppermute | solution.py:72
  34.6 11.5 %collective-permute-done.7.refs_0_ = bf16[2,96,1728]{2,1,0:T(8,128)(2,1)S(1)} collective-permute-done((bf16[2,96,1728]{2,1,0:T(8,128)(2,1)S(1)}, bf16[2,96,1728]{2,1,0:T(8,128)(2,1)S(1)}, u32[]{:S(2)}, u32[]{:S(2)}) %collective-permute-start.7) | collective-permute-done | bytes 663584 | tf_op jit(solution)/shard_map/ppermute | solution.py:72
  46.1 13.3 %collective-permute-done.8.refs_1_ = bf16[2,96,1728]{2,1,0:T(8,128)(2,1)S(1)} collective-permute-done((bf16[2,96,1728]{2,1,0:T(8,128)(2,1)S(1)}, bf16[2,96,1728]{2,1,0:T(8,128)(2,1)S(1)}, u32[]{:S(2)}, u32[]{:S(2)}) %collective-permute-start.8) | collective-permute-done | bytes 663584 | tf_op jit(solution)/shard_map/ppermute | solution.py:72
  65.4 9.1 %collective-permute-done.1.refs_2_ = bf16[144,1536]{1,0:T(8,128)(2,1)S(1)} collective-permute-done((bf16[144,1536]{1,0:T(8,128)(2,1)S(1)}, bf16[144,1536]{1,0:T(8,128)(2,1)S(1)}, u32[]{:S(2)}, u32[]{:S(2)}) %collective-permute-start.1) | collective-permute-done | bytes 442400 | tf_op jit(solution)/shard_map/ppermute | solution.py:72
  76.0 4.8 %collective-permute-done.2.refs_3_ = bf16[144,1536]{1,0:T(8,128)(2,1)S(1)} collective-permute-done((bf16[144,1536]{1,0:T(8,128)(2,1)S(1)}, bf16[144,1536]{1,0:T(8,128)(2,1)S(1)}, u32[]{:S(2)}, u32[]{:S(2)}) %collective-permute-start.2) | collective-permute-done | bytes 442400 | tf_op jit(solution)/shard_map/ppermute | solution.py:72
  91.3 4.9 %shard_map.185 = (f32[512,1152]{1,0:T(8,128)}, f32[64,384]{1,0:T(8,128)}, bf16[512,384]{1,0:T(8,128)(2,1)S(1)}, bf16[128,1536]{1,0:T(8,128)(2,1)S(1)}, bf16[128,...) custom-call(bf16[512,1536]{1,0:T(8,128)(2,1)S(1)} %get-tuple-element.85.refs_0_.refs_1_, ...), custom_call_target="tpu_custom_call" | custom-call | flops 550000000 | bytes 1000 | tf_op jit(solution)/shard_map/pallas_call | solution.py:50
  98.6 3.7 %collective-permute-start.15 = (bf16[128,1536]{1,0:T(8,128)(2,1)S(1)}, bf16[128,1536]{1,0:T(8,128)(2,1)S(1)}, u32[]{:S(2)}, u32[]{:S(2)}) collective-permute-start(bf16[128,1536]{1,0:T(8,128)(2,1)S(1)} %get-tuple-element.90), channel_id=1, source_target_pairs={{0,3},{1,2},{2,1},{3,0},{4,7},{5,6},{6,5},{7,4},{8,11},{9,10},{10,... | collective-permute-start | bytes 1179656 | tf_op jit(solution)/shard_map/ppermute | solution.py:72
  102.3 8.4 %shard_map.186 = (f32[512,1728]{1,0:T(8,128)S(1)}, bf16[768,512]{1,0:T(8,128)(2,1)}, bf16[768,512]{1,0:T(8,128)(2,1)}) custom-call(s32[3]{0:T(128)S(1)} %pad_add_fusion.refs_0_, bf16[128,1536]{1,0:T(8,128)(2,1)} %shard_map.184.refs_5_.refs_1_, bf16[128,1536]{1,0:T(8,128)(2,1)} %collective-permute-done.16.refs_2_, ...), custom_call_target="tpu_custom_call" | custom-call | flops 500000000 | bytes 1000 | tf_op jit(solution)/shard_map/pallas_call | solution.py:50
  110.8 3.9 %collective-permute-done.14.refs_2_ = bf16[128,1536]{1,0:T(8,128)(2,1)S(1)} collective-permute-done((bf16[128,1536]{1,0:T(8,128)(2,1)S(1)}, bf16[128,1536]{1,0:T(8,128)(2,1)S(1)}, u32[]{:S(2)}, u32[]{:S(2)}) %collective-permute-start.14) | collective-permute-done | bytes 393248 | tf_op jit(solution)/shard_map/ppermute | solution.py:72
  123.7 7.2 %shard_map.189.refs_5_.refs_1_.refs_2_.refs_3_ = bf16[2,1536,1728]{2,1,0:T(8,128)(2,1)} custom-call(s32[5]{0:T(128)S(1)} %stack.87.refs_0_, bf16[2,384,1728]{2,1,0:T(8,128)(2,1)S(1)} %pad_maximum_fusion.refs_1_, bf16[3,2,96,1728]{3,2,1,0:T(8,128)(2,1)S(1)} %shard_map.181.refs_5_.refs_6_.refs_1_.refs_2_, bf16[3,2,96,1728]{3,2,1,0:T(8,128)(2,1)} %shard_map.188.refs_3_, ...), custom_call_target="tpu_custom_call" | custom-call | flops 100000000 | bytes 1000 | tf_op jit(solution)/shard_map/pallas_call | solution.py:50
  130.9 7.1 %collective-permute-done.20.refs_3_ = bf16[128,1536]{1,0:T(8,128)(2,1)S(1)} collective-permute-done((bf16[128,1536]{1,0:T(8,128)(2,1)}, bf16[128,1536]{1,0:T(8,128)(2,1)S(1)}, u32[]{:S(2)}, u32[]{:S(2)}) %collective-permute-start.20) | collective-permute-done | bytes 393248 | tf_op jit(solution)/shard_map/ppermute | solution.py:72
  140.0 7.0 %shard_map.191 = (f32[512,1728]{1,0:T(8,128)}, bf16[16,32,1728]{2,1,0:T(8,128)(2,1)}) custom-call(bf16[512,1536]{1,0:T(8,128)(2,1)S(1)} %get-tuple-element.96.refs_0_, bf16[2,1536,1728]{2,1,0:T(8,128)(2,1)} %shard_map.189.refs_5_.refs_1_.refs_2_.refs_3_, f32[512,1728]{1,0:T(8,128)S(1)} %copy-done.1), custom_call_target="tpu_custom_call" | custom-call | flops 600000000 | bytes 1000 | tf_op jit(solution)/shard_map/pallas_call | solution.py:50
  147.1 3.4 shard_map.193.refs_0_
  151.0 3.5 shard_map.194.refs_4_
  156.6 8.4 %shard_map.195 = (bf16[16,32,1728]{2,1,0:T(8,128)(2,1)}, bf16[16,32,1728]{2,1,0:T(8,128)(2,1)}) custom-call(bf16[512,1536]{1,0:T(8,128)(2,1)S(1)} %get-tuple-element.96.refs_0_, bf16[2,1536,1728]{2,1,0:T(8,128)(2,1)} %shard_map.189.refs_5_.refs_1_.refs_2_.refs_3_, f32[512,1728]{1,0:T(8,128)} %get-tuple-element.97.refs_2_, f32[512,1728]{1,0:T(8,128)S(1)} %copy-done.2, ...), custom_call_target="tpu_custom_call" | custom-call | flops 700000000 | bytes 1000 | tf_op jit(solution)/shard_map/pallas_call | solution.py:50
  165.7 10.3 %shard_map.196 = (bf16[128,1536]{1,0:T(8,128)(2,1)}, bf16[128,1536]{1,0:T(8,128)(2,1)}, bf16[128,1536]{1,0:T(8,128)(2,1)}, bf16[128,1536]{1,0:T(8,128)(2,1)}) custom-call(bf16[16,32,1728]{2,1,0:T(8,128)(2,1)} %get-tuple-element.104.refs_0_.refs_4_, bf16[16,32,1728]{2,1,0:T(8,128)(2,1)} %shard_map.192.refs_1_, ...), custom_call_target="tpu_custom_call" | custom-call | flops 700000000 | bytes 1000 | tf_op jit(solution)/shard_map/pallas_call | solution.py:50
  176.1 11.5 %shard_map.197.refs_2_ = bf16[4,192,3456]{2,1,0:T(8,128)(2,1)} custom-call(bf16[768,512]{1,0:T(8,128)(2,1)S(1)} %copy-done.21, bf16[768,512]{1,0:T(8,128)(2,1)S(1)} %collective-permute-done.25.refs_1_, bf16[768,512]{1,0:T(8,128)(2,1)S(1)} %copy-done.41, bf16[768,512]{1,0:T(8,128)(2,1)S(1)} %collective-permute-done.27.refs_3_, ...), custom_call_target="tpu_custom_call" | custom-call | flops 1000000000 | bytes 1000 | tf_op jit(solution)/shard_map/pallas_call | solution.py:50
  191.3 8.6 %collective-permute-done.33.refs_1_ = bf16[128,1536]{1,0:T(8,128)(2,1)S(1)} collective-permute-done((bf16[128,1536]{1,0:T(8,128)(2,1)}, bf16[128,1536]{1,0:T(8,128)(2,1)S(1)}, u32[]{:S(2)}, u32[]{:S(2)}) %collective-permute-start.33) | collective-permute-done | bytes 393248 | tf_op jit(solution)/shard_map/ppermute | solution.py:72
  200.0 9.0 %collective-permute-done.34.refs_2_ = bf16[128,1536]{1,0:T(8,128)(2,1)S(1)} collective-permute-done((bf16[128,1536]{1,0:T(8,128)(2,1)}, bf16[128,1536]{1,0:T(8,128)(2,1)S(1)}, u32[]{:S(2)}, u32[]{:S(2)}) %collective-permute-start.34) | collective-permute-done | bytes 393248 | tf_op jit(solution)/shard_map/ppermute | solution.py:72
  218.9 5.3 %collective-permute-done.36.refs_1_ = bf16[128,1536]{1,0:T(8,128)(2,1)S(1)} collective-permute-done((bf16[128,1536]{1,0:T(8,128)(2,1)S(1)}, bf16[128,1536]{1,0:T(8,128)(2,1)S(1)}, u32[]{:S(2)}, u32[]{:S(2)}) %collective-permute-start.36) | collective-permute-done | bytes 393248 | tf_op jit(solution)/shard_map/ppermute | solution.py:72
  225.7 7.9 %collective-permute-done.37.refs_2_ = bf16[128,1536]{1,0:T(8,128)(2,1)S(1)} collective-permute-done((bf16[128,1536]{1,0:T(8,128)(2,1)S(1)}, bf16[128,1536]{1,0:T(8,128)(2,1)S(1)}, u32[]{:S(2)}, u32[]{:S(2)}) %collective-permute-start.37) | collective-permute-done | bytes 393248 | tf_op jit(solution)/shard_map/ppermute | solution.py:72
  238.4 4.0 %collective-permute-done.39.refs_2_ = f32[32,384]{1,0:T(8,128)S(1)} collective-permute-done((f32[32,384]{1,0:T(8,128)S(1)}, f32[32,384]{1,0:T(8,128)S(1)}, u32[]{:S(2)}, u32[]{:S(2)}) %collective-permute-start.39) | collective-permute-done | bytes 49184 | tf_op jit(solution)/shard_map/ppermute | solution.py:78
  242.4 3.7 %shard_map.202 = (bf16[512,1152]{1,0:T(8,128)(2,1)S(1)}, bf16[4,192,1152]{2,1,0:T(8,128)(2,1)}, bf16[192,1536]{1,0:T(8,128)(2,1)}) custom-call(s32[3]{0:T(128)S(1)} %pad_add_fusion.refs_0_, f32[512,384]{1,0:T(8,128)S(1)} %get-tuple-element.117.refs_1_, f32[32,384]{1,0:T(8,128)S(1)} %collective-permute-done.39.refs_2_, ...), custom_call_target="tpu_custom_call" | custom-call | flops 300000000 | bytes 1000 | tf_op jit(solution)/shard_map/pallas_call | solution.py:50
  247.7 5.6 %shard_map.203 = (bf16[128,1536]{1,0:T(8,128)(2,1)}, bf16[128,1536]{1,0:T(8,128)(2,1)}, bf16[128,1536]{1,0:T(8,128)(2,1)}, bf16[128,1536]{1,0:T(8,128)(2,1)}) custom-call(bf16[512,1152]{1,0:T(8,128)(2,1)} %copy-done.12, bf16[1536,1152]{1,0:T(8,128)(2,1)} %bitcast.81), custom_call_target="tpu_custom_call" | custom-call | flops 400000000 | bytes 1000 | tf_op jit(solution)/shard_map/pallas_call | solution.py:50
  265.7 8.1 %collective-permute-done.48.refs_2_ = bf16[4,48,1152]{2,1,0:T(8,128)(2,1)S(1)} collective-permute-done((bf16[4,48,1152]{2,1,0:T(8,128)(2,1)S(1)}, bf16[4,48,1152]{2,1,0:T(8,128)(2,1)S(1)}, u32[]{:S(2)}, u32[]{:S(2)}) %collective-permute-start.48) | collective-permute-done | bytes 442400 | tf_op jit(solution)/shard_map/ppermute | solution.py:72
  274.5 6.7 %shard_map.205 = (bf16[128,1536]{1,0:T(8,128)(2,1)}, bf16[128,1536]{1,0:T(8,128)(2,1)}, bf16[128,1536]{1,0:T(8,128)(2,1)}, bf16[128,1536]{1,0:T(8,128)(2,1)}) custom-call(bf16[16,32,1728]{2,1,0:T(8,128)(2,1)} %get-tuple-element.101.refs_6_.refs_0_, bf16[1728,1536]{1,0:T(8,128)(2,1)} %refs_1_.5, bf16[4,192,1152]{2,1,0:T(8,128)(2,1)S(1)} %get-tuple-element.126.refs_2_), custom_call_target="tpu_custom_call" | custom-call | flops 400000000 | bytes 1000 | tf_op jit(solution)/shard_map/pallas_call | solution.py:50
  281.1 3.9 %collective-permute-done.49.refs_3_ = bf16[4,48,1152]{2,1,0:T(8,128)(2,1)} collective-permute-done((bf16[4,48,1152]{2,1,0:T(8,128)(2,1)}, bf16[4,48,1152]{2,1,0:T(8,128)(2,1)}, u32[]{:S(2)}, u32[]{:S(2)}) %collective-permute-start.49) | collective-permute-done | bytes 442400 | tf_op jit(solution)/shard_map/ppermute | solution.py:72
  292.5 9.4 %collective-permute-done.46.refs_2_ = bf16[128,1536]{1,0:T(8,128)(2,1)} collective-permute-done((bf16[128,1536]{1,0:T(8,128)(2,1)}, bf16[128,1536]{1,0:T(8,128)(2,1)}, u32[]{:S(2)}, u32[]{:S(2)}) %collective-permute-start.46) | collective-permute-done | bytes 393248 | tf_op jit(solution)/shard_map/ppermute | solution.py:72
  320.0 4.7 %collective-permute-start.56 = (f32[5,1536]{1,0:T(8,128)}, f32[5,1536]{1,0:T(8,128)S(1)}, u32[]{:S(2)}, u32[]{:S(2)}) collective-permute-start(f32[5,1536]{1,0:T(8,128)} %add.140), channel_id=1, source_target_pairs={{0,8},{4,12},{8,0},{12,4},{1,9},{5,13},{9,1},{13,5},{2,10},{6,14},... | collective-permute-start | bytes 92168 | tf_op jit(solution)/shard_map/ppermute | solution.py:72
  332.0 9.0 %collective-permute-done.52.refs_3_.refs_2_ = bf16[48,5184]{1,0:T(8,128)(2,1)S(1)} collective-permute-done((bf16[48,5184]{1,0:T(8,128)(2,1)}, bf16[48,5184]{1,0:T(8,128)(2,1)S(1)}, u32[]{:S(2)}, u32[]{:S(2)}) %collective-permute-start.52) | collective-permute-done | bytes 497696 | tf_op jit(solution)/shard_map/ppermute | solution.py:72
  350.7 9.1 %reduce-scatter.8.cloned.1.call-done = bf16[1,48,6144]{2,1,0:T(8,128)(2,1)} async-done(((bf16[4,48,6144]{2,1,0:T(8,128)(2,1)}), bf16[1,48,6144]{2,1,0:T(8,128)(2,1)}) %reduce-scatter.8.cloned.1.call-update) | async-done | bytes 589840 | tf_op jit(solution)/shard_map/reduce_scatter | solution.py:857
  (294 shorter events, 131.5 us)
Async XLA Ops:
  7.2 297.7 %reduce-scatter.6.cloned.1.call-start = ((), (), s32[]{:S(2)}) async-start(), calls=%async_computation.4 | async-start | bytes 3440640 | tf_op jit(solution)/shard_map/reduce_scatter | solution.py:550
  27.8 18.4 %collective-permute-start.7 = (bf16[2,96,1728]{2,1,0:T(8,128)(2,1)S(1)}, bf16[2,96,1728]{2,1,0:T(8,128)(2,1)S(1)}, u32[]{:S(2)}, u32[]{:S(2)}) collective-permute-start(bf16[2,96,1728]{2,1,0:T(8,128)(2,1)S(1)} %get-tuple-element.82), channel_id=1, source_target_pairs={{0,1},{1,0},{2,3},{3,2},{4,5},{5,4},{6,7},{7,6},{8,9},{9,8},{10,11... | collective-permute-start | bytes 1990664 | tf_op jit(solution)/shard_map/ppermute | solution.py:72
  29.0 30.5 %collective-permute-start.8 = (bf16[2,96,1728]{2,1,0:T(8,128)(2,1)S(1)}, bf16[2,96,1728]{2,1,0:T(8,128)(2,1)S(1)}, u32[]{:S(2)}, u32[]{:S(2)}) collective-permute-start(bf16[2,96,1728]{2,1,0:T(8,128)(2,1)S(1)} %get-tuple-element.83), channel_id=1, source_target_pairs={{0,2},{1,3},{2,0},{3,1},{4,6},{5,7},{6,4},{7,5},{8,10},{9,11},{10,... | collective-permute-start | bytes 1990664 | tf_op jit(solution)/shard_map/ppermute | solution.py:72
  29.8 29.6 %collective-permute-start.9 = (bf16[2,96,1728]{2,1,0:T(8,128)(2,1)S(1)}, bf16[2,96,1728]{2,1,0:T(8,128)(2,1)S(1)}, u32[]{:S(2)}, u32[]{:S(2)}) collective-permute-start(bf16[2,96,1728]{2,1,0:T(8,128)(2,1)S(1)} %get-tuple-element.84), channel_id=1, source_target_pairs={{0,3},{1,2},{2,1},{3,0},{4,7},{5,6},{6,5},{7,4},{8,11},{9,10},{10,... | collective-permute-start | bytes 1990664 | tf_op jit(solution)/shard_map/ppermute | solution.py:72
  33.0 26.5 %collective-permute-start.10 = (bf16[3,96,1152]{2,1,0:T(8,128)(2,1)}, bf16[3,96,1152]{2,1,0:T(8,128)(2,1)S(1)}, u32[]{:S(2)}, u32[]{:S(2)}) collective-permute-start(bf16[3,96,1152]{2,1,0:T(8,128)(2,1)} %shard_map.180), channel_id=1, source_target_pairs={{0,4},{4,0},{8,12},{12,8},{1,5},{5,1},{9,13},{13,9},{2,6},{6,2},{1... | collective-permute-start | bytes 1990664 | tf_op jit(solution)/shard_map/ppermute | solution.py:72
  60.2 54.9 %collective-permute-start.22 = (bf16[3,2,96,1728]{3,2,1,0:T(8,128)(2,1)S(1)}, bf16[3,2,96,1728]{3,2,1,0:T(8,128)(2,1)}, u32[]{:S(2)}, u32[]{:S(2)}) collective-permute-start(bf16[3,2,96,1728]{3,2,1,0:T(8,128)(2,1)S(1)} %shard_map.181.refs_5_.refs_6_.refs_1_.refs_2_), channel_id=1, source_target_pairs={{0,4},{4,0},{8,12},{12,8},{1,5},{5,1},{9,13},{13,9},{2,6},{6,2},{1... | collective-permute-start | bytes 5971976 | tf_op jit(solution)/shard_map/ppermute | solution.py:72
  62.5 18.3 %collective-permute-start.2 = (bf16[144,1536]{1,0:T(8,128)(2,1)S(1)}, bf16[144,1536]{1,0:T(8,128)(2,1)S(1)}, u32[]{:S(2)}, u32[]{:S(2)}) collective-permute-start(bf16[144,1536]{1,0:T(8,128)(2,1)S(1)} %shard_map.177.refs_3_.refs_1_), channel_id=1, source_target_pairs={{0,2},{1,3},{2,0},{3,1},{4,6},{5,7},{6,4},{7,5},{8,10},{9,11},{10,... | collective-permute-start | bytes 1327112 | tf_op jit(solution)/shard_map/ppermute | solution.py:72
  63.6 18.1 %collective-permute-start.3 = (bf16[144,1536]{1,0:T(8,128)(2,1)S(1)}, bf16[144,1536]{1,0:T(8,128)(2,1)S(1)}, u32[]{:S(2)}, u32[]{:S(2)}) collective-permute-start(bf16[144,1536]{1,0:T(8,128)(2,1)S(1)} %shard_map.177.refs_3_.refs_1_), channel_id=1, source_target_pairs={{0,3},{1,2},{2,1},{3,0},{4,7},{5,6},{6,5},{7,4},{8,11},{9,10},{10,... | collective-permute-start | bytes 1327112 | tf_op jit(solution)/shard_map/ppermute | solution.py:72
  65.4 21.7 %collective-permute-start.11 = (bf16[3,96,1152]{2,1,0:T(8,128)(2,1)}, bf16[3,96,1152]{2,1,0:T(8,128)(2,1)}, u32[]{:S(2)}, u32[]{:S(2)}) collective-permute-start(bf16[3,96,1152]{2,1,0:T(8,128)(2,1)} %shard_map.180), channel_id=1, source_target_pairs={{0,16},{16,0},{1,17},{17,1},{2,18},{18,2},{3,19},{19,3},{4,20},{20... | collective-permute-start | bytes 1990664 | tf_op jit(solution)/shard_map/ppermute | solution.py:72
  96.6 18.1 %collective-permute-start.14 = (bf16[128,1536]{1,0:T(8,128)(2,1)S(1)}, bf16[128,1536]{1,0:T(8,128)(2,1)S(1)}, u32[]{:S(2)}, u32[]{:S(2)}) collective-permute-start(bf16[128,1536]{1,0:T(8,128)(2,1)S(1)} %get-tuple-element.89), channel_id=1, source_target_pairs={{0,2},{1,3},{2,0},{3,1},{4,6},{5,7},{6,4},{7,5},{8,10},{9,11},{10,... | collective-permute-start | bytes 1179656 | tf_op jit(solution)/shard_map/ppermute | solution.py:72
  102.3 20.6 %collective-permute-start.23 = (bf16[3,2,96,1728]{3,2,1,0:T(8,128)(2,1)S(1)}, bf16[3,2,96,1728]{3,2,1,0:T(8,128)(2,1)}, u32[]{:S(2)}, u32[]{:S(2)}) collective-permute-start(bf16[3,2,96,1728]{3,2,1,0:T(8,128)(2,1)S(1)} %shard_map.181.refs_5_.refs_6_.refs_1_.refs_2_), channel_id=1, source_target_pairs={{0,16},{16,0},{1,17},{17,1},{2,18},{18,2},{3,19},{19,3},{4,20},{20... | collective-permute-start | bytes 5971976 | tf_op jit(solution)/shard_map/ppermute | solution.py:72
  118.1 19.9 %collective-permute-start.20 = (bf16[128,1536]{1,0:T(8,128)(2,1)}, bf16[128,1536]{1,0:T(8,128)(2,1)S(1)}, u32[]{:S(2)}, u32[]{:S(2)}) collective-permute-start(bf16[128,1536]{1,0:T(8,128)(2,1)} %copy-done.18), channel_id=1, source_target_pairs={{0,2},{1,3},{2,0},{3,1},{4,6},{5,7},{6,4},{7,5},{8,10},{9,11},{10,... | collective-permute-start | bytes 1179656 | tf_op jit(solution)/shard_map/ppermute | solution.py:72
  119.5 18.5 %collective-permute-start.21 = (bf16[128,1536]{1,0:T(8,128)(2,1)}, bf16[128,1536]{1,0:T(8,128)(2,1)S(1)}, u32[]{:S(2)}, u32[]{:S(2)}) collective-permute-start(bf16[128,1536]{1,0:T(8,128)(2,1)} %copy-done.18), channel_id=1, source_target_pairs={{0,3},{1,2},{2,1},{3,0},{4,7},{5,6},{6,5},{7,4},{8,11},{9,10},{10,... | collective-permute-start | bytes 1179656 | tf_op jit(solution)/shard_map/ppermute | solution.py:72
  154.5 152.4 %reduce-scatter.4.cloned.1.call-start = ((), (), s32[]{:S(2)}) async-start(), calls=%async_computation.3 | async-start | bytes 6635520 | tf_op jit(solution)/shard_map/reduce_scatter | solution.py:639
  187.7 172.1 %reduce-scatter.8.cloned.1.call-start = ((), (), s32[]{:S(2)}) async-start(), calls=%async_computation.5 | async-start | bytes 2949120 | tf_op jit(solution)/shard_map/reduce_scatter | solution.py:857
  189.2 19.7 %collective-permute-start.34 = (bf16[128,1536]{1,0:T(8,128)(2,1)}, bf16[128,1536]{1,0:T(8,128)(2,1)S(1)}, u32[]{:S(2)}, u32[]{:S(2)}) collective-permute-start(bf16[128,1536]{1,0:T(8,128)(2,1)} %get-tuple-element.111), channel_id=1, source_target_pairs={{0,2},{1,3},{2,0},{3,1},{4,6},{5,7},{6,4},{7,5},{8,10},{9,11},{10,... | collective-permute-start | bytes 1179656 | tf_op jit(solution)/shard_map/ppermute | solution.py:72
  190.1 18.8 %collective-permute-start.35 = (bf16[128,1536]{1,0:T(8,128)(2,1)S(1)}, bf16[128,1536]{1,0:T(8,128)(2,1)S(1)}, u32[]{:S(2)}, u32[]{:S(2)}) collective-permute-start(bf16[128,1536]{1,0:T(8,128)(2,1)S(1)} %copy-done.64), channel_id=1, source_target_pairs={{0,3},{1,2},{2,1},{3,0},{4,7},{5,6},{6,5},{7,4},{8,11},{9,10},{10,... | collective-permute-start | bytes 1179656 | tf_op jit(solution)/shard_map/ppermute | solution.py:72
  212.7 20.9 %collective-permute-start.37 = (bf16[128,1536]{1,0:T(8,128)(2,1)S(1)}, bf16[128,1536]{1,0:T(8,128)(2,1)S(1)}, u32[]{:S(2)}, u32[]{:S(2)}) collective-permute-start(bf16[128,1536]{1,0:T(8,128)(2,1)S(1)} %get-tuple-element.113.refs_6_.refs_0_), channel_id=1, source_target_pairs={{0,2},{1,3},{2,0},{3,1},{4,6},{5,7},{6,4},{7,5},{8,10},{9,11},{10,... | collective-permute-start | bytes 1179656 | tf_op jit(solution)/shard_map/ppermute | solution.py:72
  214.2 19.4 %collective-permute-start.38 = (bf16[128,1536]{1,0:T(8,128)(2,1)S(1)}, bf16[128,1536]{1,0:T(8,128)(2,1)S(1)}, u32[]{:S(2)}, u32[]{:S(2)}) collective-permute-start(bf16[128,1536]{1,0:T(8,128)(2,1)S(1)} %get-tuple-element.113.refs_6_.refs_0_), channel_id=1, source_target_pairs={{0,3},{1,2},{2,1},{3,0},{4,7},{5,6},{6,5},{7,4},{8,11},{9,10},{10,... | collective-permute-start | bytes 1179656 | tf_op jit(solution)/shard_map/ppermute | solution.py:72
  216.7 20.0 %collective-permute-start.30 = (bf16[512,96]{1,0:T(8,128)(2,1)S(1)}, bf16[512,96]{1,0:T(8,128)(2,1)S(1)}, u32[]{:S(2)}, u32[]{:S(2)}) collective-permute-start(bf16[512,96]{1,0:T(8,128)(2,1)S(1)} %get-tuple-element.107), channel_id=1, source_target_pairs={{0,1},{1,0},{2,3},{3,2},{4,5},{5,4},{6,7},{7,6},{8,9},{9,8},{10,11... | collective-permute-start | bytes 294920 | tf_op jit(solution)/shard_map/ppermute | solution.py:72
  217.4 19.6 %collective-permute-start.31 = (bf16[512,96]{1,0:T(8,128)(2,1)S(1)}, bf16[512,96]{1,0:T(8,128)(2,1)S(1)}, u32[]{:S(2)}, u32[]{:S(2)}) collective-permute-start(bf16[512,96]{1,0:T(8,128)(2,1)S(1)} %get-tuple-element.108), channel_id=1, source_target_pairs={{0,2},{1,3},{2,0},{3,1},{4,6},{5,7},{6,4},{7,5},{8,10},{9,11},{10,... | collective-permute-start | bytes 294920 | tf_op jit(solution)/shard_map/ppermute | solution.py:72
  262.2 22.9 %collective-permute-start.49 = (bf16[4,48,1152]{2,1,0:T(8,128)(2,1)}, bf16[4,48,1152]{2,1,0:T(8,128)(2,1)}, u32[]{:S(2)}, u32[]{:S(2)}) collective-permute-start(bf16[4,48,1152]{2,1,0:T(8,128)(2,1)} %get-tuple-element.155), channel_id=1, source_target_pairs={{0,2},{1,3},{2,0},{3,1},{4,6},{5,7},{6,4},{7,5},{8,10},{9,11},{10,... | collective-permute-start | bytes 1327112 | tf_op jit(solution)/shard_map/ppermute | solution.py:72
  262.2 23.5 %collective-permute-start.50 = (bf16[4,48,1152]{2,1,0:T(8,128)(2,1)}, bf16[4,48,1152]{2,1,0:T(8,128)(2,1)}, u32[]{:S(2)}, u32[]{:S(2)}) collective-permute-start(bf16[4,48,1152]{2,1,0:T(8,128)(2,1)} %get-tuple-element.154), channel_id=1, source_target_pairs={{0,3},{1,2},{2,1},{3,0},{4,7},{5,6},{6,5},{7,4},{8,11},{9,10},{10,... | collective-permute-start | bytes 1327112 | tf_op jit(solution)/shard_map/ppermute | solution.py:72
  264.2 27.6 %collective-permute-start.45 = (bf16[128,1536]{1,0:T(8,128)(2,1)}, bf16[128,1536]{1,0:T(8,128)(2,1)}, u32[]{:S(2)}, u32[]{:S(2)}) collective-permute-start(bf16[128,1536]{1,0:T(8,128)(2,1)} %get-tuple-element.131), channel_id=1, source_target_pairs={{0,1},{1,0},{2,3},{3,2},{4,5},{5,4},{6,7},{7,6},{8,9},{9,8},{10,11... | collective-permute-start | bytes 1179656 | tf_op jit(solution)/shard_map/ppermute | solution.py:72
  265.7 36.2 %collective-permute-start.46 = (bf16[128,1536]{1,0:T(8,128)(2,1)}, bf16[128,1536]{1,0:T(8,128)(2,1)}, u32[]{:S(2)}, u32[]{:S(2)}) collective-permute-start(bf16[128,1536]{1,0:T(8,128)(2,1)} %get-tuple-element.132), channel_id=1, source_target_pairs={{0,2},{1,3},{2,0},{3,1},{4,6},{5,7},{6,4},{7,5},{8,10},{9,11},{10,... | collective-permute-start | bytes 1179656 | tf_op jit(solution)/shard_map/ppermute | solution.py:72
  273.8 28.1 %collective-permute-start.47 = (bf16[128,1536]{1,0:T(8,128)(2,1)}, bf16[128,1536]{1,0:T(8,128)(2,1)}, u32[]{:S(2)}, u32[]{:S(2)}) collective-permute-start(bf16[128,1536]{1,0:T(8,128)(2,1)} %get-tuple-element.133), channel_id=1, source_target_pairs={{0,3},{1,2},{2,1},{3,0},{4,7},{5,6},{6,5},{7,4},{8,11},{9,10},{10,... | collective-permute-start | bytes 1179656 | tf_op jit(solution)/shard_map/ppermute | solution.py:72
  285.0 31.7 %collective-permute-start.42 = (bf16[128,1536]{1,0:T(8,128)(2,1)}, bf16[128,1536]{1,0:T(8,128)(2,1)S(1)}, u32[]{:S(2)}, u32[]{:S(2)}) collective-permute-start(bf16[128,1536]{1,0:T(8,128)(2,1)} %get-tuple-element.128), channel_id=1, source_target_pairs={{0,1},{1,0},{2,3},{3,2},{4,5},{5,4},{6,7},{7,6},{8,9},{9,8},{10,11... | collective-permute-start | bytes 1179656 | tf_op jit(solution)/shard_map/ppermute | solution.py:72
  285.7 32.5 %collective-permute-start.43 = (bf16[128,1536]{1,0:T(8,128)(2,1)}, bf16[128,1536]{1,0:T(8,128)(2,1)S(1)}, u32[]{:S(2)}, u32[]{:S(2)}) collective-permute-start(bf16[128,1536]{1,0:T(8,128)(2,1)} %get-tuple-element.129), channel_id=1, source_target_pairs={{0,2},{1,3},{2,0},{3,1},{4,6},{5,7},{6,4},{7,5},{8,10},{9,11},{10,... | collective-permute-start | bytes 1179656 | tf_op jit(solution)/shard_map/ppermute | solution.py:72
  291.8 28.1 %collective-permute-start.44 = (bf16[128,1536]{1,0:T(8,128)(2,1)}, bf16[128,1536]{1,0:T(8,128)(2,1)}, u32[]{:S(2)}, u32[]{:S(2)}) collective-permute-start(bf16[128,1536]{1,0:T(8,128)(2,1)} %get-tuple-element.130), channel_id=1, source_target_pairs={{0,3},{1,2},{2,1},{3,0},{4,7},{5,6},{6,5},{7,4},{8,11},{9,10},{10,... | collective-permute-start | bytes 1179656 | tf_op jit(solution)/shard_map/ppermute | solution.py:72
  311.5 20.4 %collective-permute-start.51 = (bf16[48,5184]{1,0:T(8,128)(2,1)}, bf16[48,5184]{1,0:T(8,128)(2,1)S(1)}, u32[]{:S(2)}, u32[]{:S(2)}) collective-permute-start(bf16[48,5184]{1,0:T(8,128)(2,1)} %pad_maximum_fusion.5), channel_id=1, source_target_pairs={{0,1},{1,0},{2,3},{3,2},{4,5},{5,4},{6,7},{7,6},{8,9},{9,8},{10,11... | collective-permute-start | bytes 1493000 | tf_op jit(solution)/shard_map/ppermute | solution.py:72
  316.7 24.3 %collective-permute-start.52 = (bf16[48,5184]{1,0:T(8,128)(2,1)}, bf16[48,5184]{1,0:T(8,128)(2,1)S(1)}, u32[]{:S(2)}, u32[]{:S(2)}) collective-permute-start(bf16[48,5184]{1,0:T(8,128)(2,1)} %pad_maximum_fusion.6), channel_id=1, source_target_pairs={{0,2},{1,3},{2,0},{3,1},{4,6},{5,7},{6,4},{7,5},{8,10},{9,11},{10,... | collective-permute-start | bytes 1493000 | tf_op jit(solution)/shard_map/ppermute | solution.py:72
  318.9 22.0 %collective-permute-start.53 = (bf16[48,5184]{1,0:T(8,128)(2,1)}, bf16[48,5184]{1,0:T(8,128)(2,1)S(1)}, u32[]{:S(2)}, u32[]{:S(2)}) collective-permute-start(bf16[48,5184]{1,0:T(8,128)(2,1)} %pad_maximum_fusion.7), channel_id=1, source_target_pairs={{0,3},{1,2},{2,1},{3,0},{4,7},{5,6},{6,5},{7,4},{8,11},{9,10},{10,... | collective-permute-start | bytes 1493000 | tf_op jit(solution)/shard_map/ppermute | solution.py:72
  (97 other events, 896.9 us)
Sparse Core Ops, SparseCore 0:
  154.7 53.1 reduce-scatter.5
  210.2 95.6 reduce-scatter.3
  308.3 51.4 reduce-scatter.7

commit v4 on v3

--- a/solution.py
+++ b/solution.py
@@ -292,7 +292,8 @@
 
     x_local = block_input.reshape(rows, width)
     cot_local = out_cotangent.reshape(rows, width)
-    tail = shifted(x_local[rows - edge :], "seq", 1)
+    in_mine = pack(in_got)
+    tail = shifted(wait_for(x_local[rows - edge :], in_mine), "seq", 1)
     small = jnp.concatenate([norm_one[None], norm_two[None], conv_kernel], axis=0)
     small = jnp.pad(small, ((0, edge - taps - 2), (0, 0)))
 
@@ -306,7 +307,6 @@
     messages = [message] + send_tokens(message)
     taps_own = conv_kernel.astype(f32)
 
-    in_mine = pack(in_got, (message,))
     in_next = swap(in_mine, "seq", 1)
 
     def both_piece(j, start, size):
@@ -318,7 +318,7 @@
     both_sent = wait_all(both_sent, *in_got)
     both_got = [swap(piece, "fsdp", k) for piece, k in zip(both_sent, others)]
 
-    both_mine = pack(both_got, (in_next,))
+    both_mine = pack(both_got, (in_next, message))
     both_next = swap(both_mine, "seq", 1)
 
     def norm_body(place_ref, *refs):

time: 370 us -> 366 us (0.989)
  local copies, waits for them, and re-layouts: 30.9 us -> 27.1 us
    ppermute x59, waiting for transfers between devices: 125 us -> 114 us  [swap(): lax.ppermute(value, axis, [(i, i ^ k) for i in range(lax.axis_size(axis))])]
    ppermute x2, waiting for transfers between devices: 4.01 us -> 14.8 us  [shifted(): return lax.ppermute(block, axis, route)]
    unnamed x130 -> x110, local copies, waits for them, and re-layouts: 18.5 us -> 15.5 us
    pallas_call x37 -> x38, Pallas kernels: 111 us -> 111 us  [run(): pl.pallas_call(kernel, out_shape=tuple(outs), grid=grid, in_specs=list(in...]
  transfers between devices with their start and end apart: 64 -> 64, of which waited for: 25 -> 26; matrix products, arithmetic and copies ran while one was open for 5% -> 5% of each run, Pallas kernels for 28% -> 28%
where the time goes in v4:
time: 366 us; the launch traced here: 365 us
  waiting for transfers between devices  139 us (38%)
  Pallas kernels  111 us (30%)
  starting transfers between devices  67 us (18%)
  local copies, waits for them, and re-layouts  27.1 us (7%)
  between operations  14.5 us (4%)
  other arithmetic  6.61 us (2%)
    ppermute x59, waiting for transfers between devices, swap(): lax.ppermute(value, axis, [(i, i ^ k) for i in range(lax.axis_size(axis))])  114 us
    pallas_call x38, Pallas kernels, run(): pl.pallas_call(kernel, out_shape=tuple(outs), grid=grid, in_specs=list(in...  111 us
    ppermute x59, starting transfers between devices, swap(): lax.ppermute(value, axis, [(i, i ^ k) for i in range(lax.axis_size(axis))])  63 us
    unnamed x110, local copies, waits for them, and re-layouts  15.5 us
    ppermute x2, waiting for transfers between devices, shifted(): return lax.ppermute(block, axis, route)  14.8 us
    reduce_scatter x1, waiting for transfers between devices, on_device(): lax.psum_scatter(mix_both, 'seq', scatter_dimension=0, tiled=True)  9.1 us
  transfers between devices with their start and end apart: 64, of which 26 were waited for; matrix products, arithmetic and copies ran while one was open for 5% of the time, Pallas kernels for 28%

profile of v4, /device:TPU:0, one launch (start us, length us, event | category | flops | bytes accessed | tf_op | source)
XLA Modules:
  0.0 365.0 jit_solution(8426571794844891644)
XLA Ops:
  18.4 5.4 %collective-permute-done.1.refs_1_.refs_4_ = bf16[96,1152]{1,0:T(8,128)(2,1)S(1)} collective-permute-done((bf16[96,1152]{1,0:T(8,128)(2,1)S(1)}, bf16[96,1152]{1,0:T(8,128)(2,1)S(1)}, u32[]{:S(2)}, u32[]{:S(2)}) %collective-permute-start.1) | collective-permute-done | bytes 221216 | tf_op jit(solution)/shard_map/ppermute | solution.py:72
  32.2 10.8 %collective-permute-done.3.refs_1_ = bf16[16,1536]{1,0:T(8,128)(2,1)S(1)} collective-permute-done((bf16[16,1536]{1,0:T(8,128)(2,1)S(1)}, bf16[16,1536]{1,0:T(8,128)(2,1)S(1)}, u32[]{:S(2)}, u32[]{:S(2)}) %collective-permute-start.3) | collective-permute-done | bytes 49184 | tf_op jit(solution)/shard_map/ppermute | solution.py:78
  43.1 12.6 %collective-permute-done.8.refs_1_ = bf16[2,96,1728]{2,1,0:T(8,128)(2,1)S(1)} collective-permute-done((bf16[2,96,1728]{2,1,0:T(8,128)(2,1)S(1)}, bf16[2,96,1728]{2,1,0:T(8,128)(2,1)S(1)}, u32[]{:S(2)}, u32[]{:S(2)}) %collective-permute-start.8) | collective-permute-done | bytes 663584 | tf_op jit(solution)/shard_map/ppermute | solution.py:72
  61.7 9.4 %collective-permute-done.4.refs_2_ = bf16[144,1536]{1,0:T(8,128)(2,1)S(1)} collective-permute-done((bf16[144,1536]{1,0:T(8,128)(2,1)S(1)}, bf16[144,1536]{1,0:T(8,128)(2,1)S(1)}, u32[]{:S(2)}, u32[]{:S(2)}) %collective-permute-start.4) | collective-permute-done | bytes 442400 | tf_op jit(solution)/shard_map/ppermute | solution.py:72
  72.6 4.3 %collective-permute-done.5.refs_3_ = bf16[144,1536]{1,0:T(8,128)(2,1)S(1)} collective-permute-done((bf16[144,1536]{1,0:T(8,128)(2,1)S(1)}, bf16[144,1536]{1,0:T(8,128)(2,1)S(1)}, u32[]{:S(2)}, u32[]{:S(2)}) %collective-permute-start.5) | collective-permute-done | bytes 442400 | tf_op jit(solution)/shard_map/ppermute | solution.py:72
  84.4 3.1 shard_map.184
  87.6 4.9 %shard_map.186 = (f32[512,1152]{1,0:T(8,128)}, f32[64,384]{1,0:T(8,128)}, bf16[512,384]{1,0:T(8,128)(2,1)S(1)}, bf16[128,1536]{1,0:T(8,128)(2,1)S(1)}, bf16[128,...) custom-call(bf16[512,1536]{1,0:T(8,128)(2,1)S(1)} %get-tuple-element.85.refs_0_.refs_1_, ...), custom_call_target="tpu_custom_call" | custom-call | flops 550000000 | bytes 1000 | tf_op jit(solution)/shard_map/pallas_call | solution.py:50
  94.9 4.0 %collective-permute-start.15 = (bf16[128,1536]{1,0:T(8,128)(2,1)S(1)}, bf16[128,1536]{1,0:T(8,128)(2,1)S(1)}, u32[]{:S(2)}, u32[]{:S(2)}) collective-permute-start(bf16[128,1536]{1,0:T(8,128)(2,1)S(1)} %get-tuple-element.90), channel_id=1, source_target_pairs={{0,3},{1,2},{2,1},{3,0},{4,7},{5,6},{6,5},{7,4},{8,11},{9,10},{10,... | collective-permute-start | bytes 1179656 | tf_op jit(solution)/shard_map/ppermute | solution.py:72
  98.9 8.3 %shard_map.187 = (f32[512,1728]{1,0:T(8,128)S(1)}, bf16[768,512]{1,0:T(8,128)(2,1)}, bf16[768,512]{1,0:T(8,128)(2,1)}) custom-call(s32[3]{0:T(128)S(1)} %pad_add_fusion.refs_0_, bf16[128,1536]{1,0:T(8,128)(2,1)} %shard_map.185.refs_5_.refs_1_, bf16[128,1536]{1,0:T(8,128)(2,1)} %collective-permute-done.16.refs_2_, ...), custom_call_target="tpu_custom_call" | custom-call | flops 500000000 | bytes 1000 | tf_op jit(solution)/shard_map/pallas_call | solution.py:50
  107.3 4.1 %collective-permute-done.14.refs_2_ = bf16[128,1536]{1,0:T(8,128)(2,1)S(1)} collective-permute-done((bf16[128,1536]{1,0:T(8,128)(2,1)S(1)}, bf16[128,1536]{1,0:T(8,128)(2,1)S(1)}, u32[]{:S(2)}, u32[]{:S(2)}) %collective-permute-start.14) | collective-permute-done | bytes 393248 | tf_op jit(solution)/shard_map/ppermute | solution.py:72
  119.5 7.2 %shard_map.190.refs_5_.refs_1_.refs_2_.refs_3_ = bf16[2,1536,1728]{2,1,0:T(8,128)(2,1)} custom-call(s32[5]{0:T(128)S(1)} %stack.87.refs_0_, bf16[2,384,1728]{2,1,0:T(8,128)(2,1)S(1)} %pad_maximum_fusion.refs_1_, bf16[3,2,96,1728]{3,2,1,0:T(8,128)(2,1)S(1)} %shard_map.182.refs_5_.refs_6_.refs_1_.refs_2_, bf16[3,2,96,1728]{3,2,1,0:T(8,128)(2,1)} %shard_map.189.refs_3_, ...), custom_call_target="tpu_custom_call" | custom-call | flops 100000000 | bytes 1000 | tf_op jit(solution)/shard_map/pallas_call | solution.py:50
  126.7 7.6 %collective-permute-done.20.refs_3_ = bf16[128,1536]{1,0:T(8,128)(2,1)S(1)} collective-permute-done((bf16[128,1536]{1,0:T(8,128)(2,1)S(1)}, bf16[128,1536]{1,0:T(8,128)(2,1)S(1)}, u32[]{:S(2)}, u32[]{:S(2)}) %collective-permute-start.20) | collective-permute-done | bytes 393248 | tf_op jit(solution)/shard_map/ppermute | solution.py:72
  136.3 7.0 %shard_map.192 = (f32[512,1728]{1,0:T(8,128)}, bf16[16,32,1728]{2,1,0:T(8,128)(2,1)}) custom-call(bf16[512,1536]{1,0:T(8,128)(2,1)S(1)} %get-tuple-element.96.refs_0_, bf16[2,1536,1728]{2,1,0:T(8,128)(2,1)} %shard_map.190.refs_5_.refs_1_.refs_2_.refs_3_, f32[512,1728]{1,0:T(8,128)S(1)} %copy-done.1), custom_call_target="tpu_custom_call" | custom-call | flops 600000000 | bytes 1000 | tf_op jit(solution)/shard_map/pallas_call | solution.py:50
  143.3 3.4 shard_map.194.refs_0_
  147.3 3.5 shard_map.195.refs_4_
  152.9 8.4 %shard_map.196 = (bf16[16,32,1728]{2,1,0:T(8,128)(2,1)}, bf16[16,32,1728]{2,1,0:T(8,128)(2,1)}) custom-call(bf16[512,1536]{1,0:T(8,128)(2,1)S(1)} %get-tuple-element.96.refs_0_, bf16[2,1536,1728]{2,1,0:T(8,128)(2,1)} %shard_map.190.refs_5_.refs_1_.refs_2_.refs_3_, f32[512,1728]{1,0:T(8,128)} %get-tuple-element.97.refs_2_, f32[512,1728]{1,0:T(8,128)S(1)} %copy-done.2, ...), custom_call_target="tpu_custom_call" | custom-call | flops 700000000 | bytes 1000 | tf_op jit(solution)/shard_map/pallas_call | solution.py:50
  162.0 10.3 %shard_map.197 = (bf16[128,1536]{1,0:T(8,128)(2,1)}, bf16[128,1536]{1,0:T(8,128)(2,1)}, bf16[128,1536]{1,0:T(8,128)(2,1)}, bf16[128,1536]{1,0:T(8,128)(2,1)}) custom-call(bf16[16,32,1728]{2,1,0:T(8,128)(2,1)} %get-tuple-element.104.refs_0_.refs_4_, bf16[16,32,1728]{2,1,0:T(8,128)(2,1)} %shard_map.193.refs_1_, ...), custom_call_target="tpu_custom_call" | custom-call | flops 700000000 | bytes 1000 | tf_op jit(solution)/shard_map/pallas_call | solution.py:50
  172.4 11.6 %shard_map.198.refs_2_ = bf16[4,192,3456]{2,1,0:T(8,128)(2,1)} custom-call(bf16[768,512]{1,0:T(8,128)(2,1)S(1)} %get-tuple-element.98.refs_0_, bf16[768,512]{1,0:T(8,128)(2,1)S(1)} %collective-permute-done.25.refs_1_, bf16[768,512]{1,0:T(8,128)(2,1)S(1)} %copy-done.36, bf16[768,512]{1,0:T(8,128)(2,1)S(1)} %collective-permute-done.27.refs_3_, ...), custom_call_target="tpu_custom_call" | custom-call | flops 1000000000 | bytes 1000 | tf_op jit(solution)/shard_map/pallas_call | solution.py:50
  187.6 8.7 %collective-permute-done.33.refs_1_ = bf16[128,1536]{1,0:T(8,128)(2,1)S(1)} collective-permute-done((bf16[128,1536]{1,0:T(8,128)(2,1)}, bf16[128,1536]{1,0:T(8,128)(2,1)S(1)}, u32[]{:S(2)}, u32[]{:S(2)}) %collective-permute-start.33) | collective-permute-done | bytes 393248 | tf_op jit(solution)/shard_map/ppermute | solution.py:72
  196.3 9.0 %collective-permute-done.34.refs_2_ = bf16[128,1536]{1,0:T(8,128)(2,1)S(1)} collective-permute-done((bf16[128,1536]{1,0:T(8,128)(2,1)}, bf16[128,1536]{1,0:T(8,128)(2,1)S(1)}, u32[]{:S(2)}, u32[]{:S(2)}) %collective-permute-start.34) | collective-permute-done | bytes 393248 | tf_op jit(solution)/shard_map/ppermute | solution.py:72
  213.8 5.3 %collective-permute-done.36.refs_1_ = bf16[128,1536]{1,0:T(8,128)(2,1)S(1)} collective-permute-done((bf16[128,1536]{1,0:T(8,128)(2,1)S(1)}, bf16[128,1536]{1,0:T(8,128)(2,1)S(1)}, u32[]{:S(2)}, u32[]{:S(2)}) %collective-permute-start.36) | collective-permute-done | bytes 393248 | tf_op jit(solution)/shard_map/ppermute | solution.py:72
  220.6 8.5 %collective-permute-done.37.refs_2_ = bf16[128,1536]{1,0:T(8,128)(2,1)S(1)} collective-permute-done((bf16[128,1536]{1,0:T(8,128)(2,1)S(1)}, bf16[128,1536]{1,0:T(8,128)(2,1)S(1)}, u32[]{:S(2)}, u32[]{:S(2)}) %collective-permute-start.37) | collective-permute-done | bytes 393248 | tf_op jit(solution)/shard_map/ppermute | solution.py:72
  233.7 4.0 %collective-permute-done.39.refs_2_ = f32[32,384]{1,0:T(8,128)S(1)} collective-permute-done((f32[32,384]{1,0:T(8,128)S(1)}, f32[32,384]{1,0:T(8,128)S(1)}, u32[]{:S(2)}, u32[]{:S(2)}) %collective-permute-start.39) | collective-permute-done | bytes 49184 | tf_op jit(solution)/shard_map/ppermute | solution.py:78
  237.7 3.7 %shard_map.203 = (bf16[512,1152]{1,0:T(8,128)(2,1)S(1)}, bf16[4,192,1152]{2,1,0:T(8,128)(2,1)}, bf16[192,1536]{1,0:T(8,128)(2,1)}) custom-call(s32[3]{0:T(128)S(1)} %pad_add_fusion.refs_0_, f32[512,384]{1,0:T(8,128)S(1)} %get-tuple-element.117.refs_1_, f32[32,384]{1,0:T(8,128)S(1)} %collective-permute-done.39.refs_2_, ...), custom_call_target="tpu_custom_call" | custom-call | flops 300000000 | bytes 1000 | tf_op jit(solution)/shard_map/pallas_call | solution.py:50
  243.0 5.7 %shard_map.204 = (bf16[128,1536]{1,0:T(8,128)(2,1)}, bf16[128,1536]{1,0:T(8,128)(2,1)}, bf16[128,1536]{1,0:T(8,128)(2,1)}, bf16[128,1536]{1,0:T(8,128)(2,1)}) custom-call(bf16[512,1152]{1,0:T(8,128)(2,1)} %copy-done.13, bf16[1536,1152]{1,0:T(8,128)(2,1)} %bitcast.81), custom_call_target="tpu_custom_call" | custom-call | flops 400000000 | bytes 1000 | tf_op jit(solution)/shard_map/pallas_call | solution.py:50
  261.2 7.9 %collective-permute-done.48.refs_2_ = bf16[4,48,1152]{2,1,0:T(8,128)(2,1)S(1)} collective-permute-done((bf16[4,48,1152]{2,1,0:T(8,128)(2,1)S(1)}, bf16[4,48,1152]{2,1,0:T(8,128)(2,1)S(1)}, u32[]{:S(2)}, u32[]{:S(2)}) %collective-permute-start.48) | collective-permute-done | bytes 442400 | tf_op jit(solution)/shard_map/ppermute | solution.py:72
  270.2 6.7 %shard_map.206 = (bf16[128,1536]{1,0:T(8,128)(2,1)}, bf16[128,1536]{1,0:T(8,128)(2,1)}, bf16[128,1536]{1,0:T(8,128)(2,1)}, bf16[128,1536]{1,0:T(8,128)(2,1)}) custom-call(bf16[16,32,1728]{2,1,0:T(8,128)(2,1)} %get-tuple-element.101.refs_6_.refs_0_, bf16[1728,1536]{1,0:T(8,128)(2,1)} %refs_1_.5, bf16[4,192,1152]{2,1,0:T(8,128)(2,1)S(1)} %get-tuple-element.126.refs_2_), custom_call_target="tpu_custom_call" | custom-call | flops 400000000 | bytes 1000 | tf_op jit(solution)/shard_map/pallas_call | solution.py:50
  288.2 8.1 %collective-permute-done.46.refs_2_ = bf16[128,1536]{1,0:T(8,128)(2,1)} collective-permute-done((bf16[128,1536]{1,0:T(8,128)(2,1)}, bf16[128,1536]{1,0:T(8,128)(2,1)}, u32[]{:S(2)}, u32[]{:S(2)}) %collective-permute-start.46) | collective-permute-done | bytes 393248 | tf_op jit(solution)/shard_map/ppermute | solution.py:72
  317.7 3.5 collective-permute-start.55
  327.5 9.9 %collective-permute-done.52.refs_3_.refs_2_ = bf16[48,5184]{1,0:T(8,128)(2,1)S(1)} collective-permute-done((bf16[48,5184]{1,0:T(8,128)(2,1)}, bf16[48,5184]{1,0:T(8,128)(2,1)S(1)}, u32[]{:S(2)}, u32[]{:S(2)}) %collective-permute-start.52) | collective-permute-done | bytes 497696 | tf_op jit(solution)/shard_map/ppermute | solution.py:72
  342.9 3.1 shard_map.211
  347.2 9.1 %reduce-scatter.8.cloned.1.call-done = bf16[1,48,6144]{2,1,0:T(8,128)(2,1)} async-done(((bf16[4,48,6144]{2,1,0:T(8,128)(2,1)}), bf16[1,48,6144]{2,1,0:T(8,128)(2,1)}) %reduce-scatter.8.cloned.1.call-update) | async-done | bytes 589840 | tf_op jit(solution)/shard_map/reduce_scatter | solution.py:857
  (275 shorter events, 131.4 us)
Async XLA Ops:
  7.2 292.1 %reduce-scatter.6.cloned.1.call-start = ((), (), s32[]{:S(2)}) async-start(), calls=%async_computation.4 | async-start | bytes 3440640 | tf_op jit(solution)/shard_map/reduce_scatter | solution.py:550
  23.8 19.3 %collective-permute-start.7 = (bf16[2,96,1728]{2,1,0:T(8,128)(2,1)S(1)}, bf16[2,96,1728]{2,1,0:T(8,128)(2,1)S(1)}, u32[]{:S(2)}, u32[]{:S(2)}) collective-permute-start(bf16[2,96,1728]{2,1,0:T(8,128)(2,1)S(1)} %get-tuple-element.82), channel_id=1, source_target_pairs={{0,1},{1,0},{2,3},{3,2},{4,5},{5,4},{6,7},{7,6},{8,9},{9,8},{10,11... | collective-permute-start | bytes 1990664 | tf_op jit(solution)/shard_map/ppermute | solution.py:72
  25.0 30.8 %collective-permute-start.8 = (bf16[2,96,1728]{2,1,0:T(8,128)(2,1)S(1)}, bf16[2,96,1728]{2,1,0:T(8,128)(2,1)S(1)}, u32[]{:S(2)}, u32[]{:S(2)}) collective-permute-start(bf16[2,96,1728]{2,1,0:T(8,128)(2,1)S(1)} %get-tuple-element.83), channel_id=1, source_target_pairs={{0,2},{1,3},{2,0},{3,1},{4,6},{5,7},{6,4},{7,5},{8,10},{9,11},{10,... | collective-permute-start | bytes 1990664 | tf_op jit(solution)/shard_map/ppermute | solution.py:72
  25.8 29.9 %collective-permute-start.9 = (bf16[2,96,1728]{2,1,0:T(8,128)(2,1)S(1)}, bf16[2,96,1728]{2,1,0:T(8,128)(2,1)S(1)}, u32[]{:S(2)}, u32[]{:S(2)}) collective-permute-start(bf16[2,96,1728]{2,1,0:T(8,128)(2,1)S(1)} %get-tuple-element.84), channel_id=1, source_target_pairs={{0,3},{1,2},{2,1},{3,0},{4,7},{5,6},{6,5},{7,4},{8,11},{9,10},{10,... | collective-permute-start | bytes 1990664 | tf_op jit(solution)/shard_map/ppermute | solution.py:72
  28.1 27.7 %collective-permute-start.10 = (bf16[3,96,1152]{2,1,0:T(8,128)(2,1)S(1)}, bf16[3,96,1152]{2,1,0:T(8,128)(2,1)}, u32[]{:S(2)}, u32[]{:S(2)}) collective-permute-start(bf16[3,96,1152]{2,1,0:T(8,128)(2,1)S(1)} %shard_map.178.refs_1_), channel_id=1, source_target_pairs={{0,4},{4,0},{8,12},{12,8},{1,5},{5,1},{9,13},{13,9},{2,6},{6,2},{1... | collective-permute-start | bytes 1990664 | tf_op jit(solution)/shard_map/ppermute | solution.py:72
  56.6 55.3 %collective-permute-start.22 = (bf16[3,2,96,1728]{3,2,1,0:T(8,128)(2,1)S(1)}, bf16[3,2,96,1728]{3,2,1,0:T(8,128)(2,1)}, u32[]{:S(2)}, u32[]{:S(2)}) collective-permute-start(bf16[3,2,96,1728]{3,2,1,0:T(8,128)(2,1)S(1)} %shard_map.182.refs_5_.refs_6_.refs_1_.refs_2_), channel_id=1, source_target_pairs={{0,4},{4,0},{8,12},{12,8},{1,5},{5,1},{9,13},{13,9},{2,6},{6,2},{1... | collective-permute-start | bytes 5971976 | tf_op jit(solution)/shard_map/ppermute | solution.py:72
  58.8 18.2 %collective-permute-start.5 = (bf16[144,1536]{1,0:T(8,128)(2,1)S(1)}, bf16[144,1536]{1,0:T(8,128)(2,1)S(1)}, u32[]{:S(2)}, u32[]{:S(2)}) collective-permute-start(bf16[144,1536]{1,0:T(8,128)(2,1)S(1)} %shard_map.180.refs_4_.refs_1_), channel_id=1, source_target_pairs={{0,2},{1,3},{2,0},{3,1},{4,6},{5,7},{6,4},{7,5},{8,10},{9,11},{10,... | collective-permute-start | bytes 1327112 | tf_op jit(solution)/shard_map/ppermute | solution.py:72
  59.9 18.0 %collective-permute-start.6 = (bf16[144,1536]{1,0:T(8,128)(2,1)S(1)}, bf16[144,1536]{1,0:T(8,128)(2,1)S(1)}, u32[]{:S(2)}, u32[]{:S(2)}) collective-permute-start(bf16[144,1536]{1,0:T(8,128)(2,1)S(1)} %shard_map.180.refs_4_.refs_1_), channel_id=1, source_target_pairs={{0,3},{1,2},{2,1},{3,0},{4,7},{5,6},{6,5},{7,4},{8,11},{9,10},{10,... | collective-permute-start | bytes 1327112 | tf_op jit(solution)/shard_map/ppermute | solution.py:72
  61.7 21.5 %collective-permute-start.11 = (bf16[3,96,1152]{2,1,0:T(8,128)(2,1)S(1)}, bf16[3,96,1152]{2,1,0:T(8,128)(2,1)}, u32[]{:S(2)}, u32[]{:S(2)}) collective-permute-start(bf16[3,96,1152]{2,1,0:T(8,128)(2,1)S(1)} %shard_map.178.refs_1_), channel_id=1, source_target_pairs={{0,16},{16,0},{1,17},{17,1},{2,18},{18,2},{3,19},{19,3},{4,20},{20... | collective-permute-start | bytes 1990664 | tf_op jit(solution)/shard_map/ppermute | solution.py:72
  92.9 18.5 %collective-permute-start.14 = (bf16[128,1536]{1,0:T(8,128)(2,1)S(1)}, bf16[128,1536]{1,0:T(8,128)(2,1)S(1)}, u32[]{:S(2)}, u32[]{:S(2)}) collective-permute-start(bf16[128,1536]{1,0:T(8,128)(2,1)S(1)} %get-tuple-element.89), channel_id=1, source_target_pairs={{0,2},{1,3},{2,0},{3,1},{4,6},{5,7},{6,4},{7,5},{8,10},{9,11},{10,... | collective-permute-start | bytes 1179656 | tf_op jit(solution)/shard_map/ppermute | solution.py:72
  98.9 20.6 %collective-permute-start.23 = (bf16[3,2,96,1728]{3,2,1,0:T(8,128)(2,1)S(1)}, bf16[3,2,96,1728]{3,2,1,0:T(8,128)(2,1)}, u32[]{:S(2)}, u32[]{:S(2)}) collective-permute-start(bf16[3,2,96,1728]{3,2,1,0:T(8,128)(2,1)S(1)} %shard_map.182.refs_5_.refs_6_.refs_1_.refs_2_), channel_id=1, source_target_pairs={{0,16},{16,0},{1,17},{17,1},{2,18},{18,2},{3,19},{19,3},{4,20},{20... | collective-permute-start | bytes 5971976 | tf_op jit(solution)/shard_map/ppermute | solution.py:72
  114.6 19.7 %collective-permute-start.20 = (bf16[128,1536]{1,0:T(8,128)(2,1)S(1)}, bf16[128,1536]{1,0:T(8,128)(2,1)S(1)}, u32[]{:S(2)}, u32[]{:S(2)}) collective-permute-start(bf16[128,1536]{1,0:T(8,128)(2,1)S(1)} %get-tuple-element.95.refs_1_.refs_6_), channel_id=1, source_target_pairs={{0,2},{1,3},{2,0},{3,1},{4,6},{5,7},{6,4},{7,5},{8,10},{9,11},{10,... | collective-permute-start | bytes 1179656 | tf_op jit(solution)/shard_map/ppermute | solution.py:72
  116.0 18.3 %collective-permute-start.21 = (bf16[128,1536]{1,0:T(8,128)(2,1)S(1)}, bf16[128,1536]{1,0:T(8,128)(2,1)S(1)}, u32[]{:S(2)}, u32[]{:S(2)}) collective-permute-start(bf16[128,1536]{1,0:T(8,128)(2,1)S(1)} %get-tuple-element.95.refs_1_.refs_6_), channel_id=1, source_target_pairs={{0,3},{1,2},{2,1},{3,0},{4,7},{5,6},{6,5},{7,4},{8,11},{9,10},{10,... | collective-permute-start | bytes 1179656 | tf_op jit(solution)/shard_map/ppermute | solution.py:72
  150.9 151.5 %reduce-scatter.4.cloned.1.call-start = ((), (), s32[]{:S(2)}) async-start(), calls=%async_computation.3 | async-start | bytes 6635520 | tf_op jit(solution)/shard_map/reduce_scatter | solution.py:639
  184.0 172.3 %reduce-scatter.8.cloned.1.call-start = ((), (), s32[]{:S(2)}) async-start(), calls=%async_computation.5 | async-start | bytes 2949120 | tf_op jit(solution)/shard_map/reduce_scatter | solution.py:857
  185.6 19.6 %collective-permute-start.34 = (bf16[128,1536]{1,0:T(8,128)(2,1)}, bf16[128,1536]{1,0:T(8,128)(2,1)S(1)}, u32[]{:S(2)}, u32[]{:S(2)}) collective-permute-start(bf16[128,1536]{1,0:T(8,128)(2,1)} %get-tuple-element.111), channel_id=1, source_target_pairs={{0,2},{1,3},{2,0},{3,1},{4,6},{5,7},{6,4},{7,5},{8,10},{9,11},{10,... | collective-permute-start | bytes 1179656 | tf_op jit(solution)/shard_map/ppermute | solution.py:72
  186.4 18.9 %collective-permute-start.35 = (bf16[128,1536]{1,0:T(8,128)(2,1)S(1)}, bf16[128,1536]{1,0:T(8,128)(2,1)S(1)}, u32[]{:S(2)}, u32[]{:S(2)}) collective-permute-start(bf16[128,1536]{1,0:T(8,128)(2,1)S(1)} %copy-done.54), channel_id=1, source_target_pairs={{0,3},{1,2},{2,1},{3,0},{4,7},{5,6},{6,5},{7,4},{8,11},{9,10},{10,... | collective-permute-start | bytes 1179656 | tf_op jit(solution)/shard_map/ppermute | solution.py:72
  207.6 21.5 %collective-permute-start.37 = (bf16[128,1536]{1,0:T(8,128)(2,1)S(1)}, bf16[128,1536]{1,0:T(8,128)(2,1)S(1)}, u32[]{:S(2)}, u32[]{:S(2)}) collective-permute-start(bf16[128,1536]{1,0:T(8,128)(2,1)S(1)} %get-tuple-element.113.refs_6_.refs_0_), channel_id=1, source_target_pairs={{0,2},{1,3},{2,0},{3,1},{4,6},{5,7},{6,4},{7,5},{8,10},{9,11},{10,... | collective-permute-start | bytes 1179656 | tf_op jit(solution)/shard_map/ppermute | solution.py:72
  209.1 20.0 %collective-permute-start.38 = (bf16[128,1536]{1,0:T(8,128)(2,1)S(1)}, bf16[128,1536]{1,0:T(8,128)(2,1)S(1)}, u32[]{:S(2)}, u32[]{:S(2)}) collective-permute-start(bf16[128,1536]{1,0:T(8,128)(2,1)S(1)} %get-tuple-element.113.refs_6_.refs_0_), channel_id=1, source_target_pairs={{0,3},{1,2},{2,1},{3,0},{4,7},{5,6},{6,5},{7,4},{8,11},{9,10},{10,... | collective-permute-start | bytes 1179656 | tf_op jit(solution)/shard_map/ppermute | solution.py:72
  211.7 20.6 %collective-permute-start.30 = (bf16[512,96]{1,0:T(8,128)(2,1)S(1)}, bf16[512,96]{1,0:T(8,128)(2,1)S(1)}, u32[]{:S(2)}, u32[]{:S(2)}) collective-permute-start(bf16[512,96]{1,0:T(8,128)(2,1)S(1)} %get-tuple-element.107), channel_id=1, source_target_pairs={{0,1},{1,0},{2,3},{3,2},{4,5},{5,4},{6,7},{7,6},{8,9},{9,8},{10,11... | collective-permute-start | bytes 294920 | tf_op jit(solution)/shard_map/ppermute | solution.py:72
  212.3 19.9 %collective-permute-start.31 = (bf16[512,96]{1,0:T(8,128)(2,1)S(1)}, bf16[512,96]{1,0:T(8,128)(2,1)S(1)}, u32[]{:S(2)}, u32[]{:S(2)}) collective-permute-start(bf16[512,96]{1,0:T(8,128)(2,1)S(1)} %get-tuple-element.108), channel_id=1, source_target_pairs={{0,2},{1,3},{2,0},{3,1},{4,6},{5,7},{6,4},{7,5},{8,10},{9,11},{10,... | collective-permute-start | bytes 294920 | tf_op jit(solution)/shard_map/ppermute | solution.py:72
  256.6 22.9 %collective-permute-start.49 = (bf16[4,48,1152]{2,1,0:T(8,128)(2,1)}, bf16[4,48,1152]{2,1,0:T(8,128)(2,1)}, u32[]{:S(2)}, u32[]{:S(2)}) collective-permute-start(bf16[4,48,1152]{2,1,0:T(8,128)(2,1)} %get-tuple-element.155), channel_id=1, source_target_pairs={{0,2},{1,3},{2,0},{3,1},{4,6},{5,7},{6,4},{7,5},{8,10},{9,11},{10,... | collective-permute-start | bytes 1327112 | tf_op jit(solution)/shard_map/ppermute | solution.py:72
  257.7 23.2 %collective-permute-start.50 = (bf16[4,48,1152]{2,1,0:T(8,128)(2,1)}, bf16[4,48,1152]{2,1,0:T(8,128)(2,1)}, u32[]{:S(2)}, u32[]{:S(2)}) collective-permute-start(bf16[4,48,1152]{2,1,0:T(8,128)(2,1)} %get-tuple-element.154), channel_id=1, source_target_pairs={{0,3},{1,2},{2,1},{3,0},{4,7},{5,6},{6,5},{7,4},{8,11},{9,10},{10,... | collective-permute-start | bytes 1327112 | tf_op jit(solution)/shard_map/ppermute | solution.py:72
  259.5 27.6 %collective-permute-start.45 = (bf16[128,1536]{1,0:T(8,128)(2,1)}, bf16[128,1536]{1,0:T(8,128)(2,1)}, u32[]{:S(2)}, u32[]{:S(2)}) collective-permute-start(bf16[128,1536]{1,0:T(8,128)(2,1)} %get-tuple-element.131), channel_id=1, source_target_pairs={{0,1},{1,0},{2,3},{3,2},{4,5},{5,4},{6,7},{7,6},{8,9},{9,8},{10,11... | collective-permute-start | bytes 1179656 | tf_op jit(solution)/shard_map/ppermute | solution.py:72
  260.1 36.2 %collective-permute-start.46 = (bf16[128,1536]{1,0:T(8,128)(2,1)}, bf16[128,1536]{1,0:T(8,128)(2,1)}, u32[]{:S(2)}, u32[]{:S(2)}) collective-permute-start(bf16[128,1536]{1,0:T(8,128)(2,1)} %get-tuple-element.132), channel_id=1, source_target_pairs={{0,2},{1,3},{2,0},{3,1},{4,6},{5,7},{6,4},{7,5},{8,10},{9,11},{10,... | collective-permute-start | bytes 1179656 | tf_op jit(solution)/shard_map/ppermute | solution.py:72
  269.1 27.3 %collective-permute-start.47 = (bf16[128,1536]{1,0:T(8,128)(2,1)}, bf16[128,1536]{1,0:T(8,128)(2,1)}, u32[]{:S(2)}, u32[]{:S(2)}) collective-permute-start(bf16[128,1536]{1,0:T(8,128)(2,1)} %get-tuple-element.133), channel_id=1, source_target_pairs={{0,3},{1,2},{2,1},{3,0},{4,7},{5,6},{6,5},{7,4},{8,11},{9,10},{10,... | collective-permute-start | bytes 1179656 | tf_op jit(solution)/shard_map/ppermute | solution.py:72
  279.5 33.7 %collective-permute-start.42 = (bf16[128,1536]{1,0:T(8,128)(2,1)}, bf16[128,1536]{1,0:T(8,128)(2,1)S(1)}, u32[]{:S(2)}, u32[]{:S(2)}) collective-permute-start(bf16[128,1536]{1,0:T(8,128)(2,1)} %get-tuple-element.128), channel_id=1, source_target_pairs={{0,1},{1,0},{2,3},{3,2},{4,5},{5,4},{6,7},{7,6},{8,9},{9,8},{10,11... | collective-permute-start | bytes 1179656 | tf_op jit(solution)/shard_map/ppermute | solution.py:72
  280.9 33.7 %collective-permute-start.43 = (bf16[128,1536]{1,0:T(8,128)(2,1)}, bf16[128,1536]{1,0:T(8,128)(2,1)S(1)}, u32[]{:S(2)}, u32[]{:S(2)}) collective-permute-start(bf16[128,1536]{1,0:T(8,128)(2,1)} %get-tuple-element.129), channel_id=1, source_target_pairs={{0,2},{1,3},{2,0},{3,1},{4,6},{5,7},{6,4},{7,5},{8,10},{9,11},{10,... | collective-permute-start | bytes 1179656 | tf_op jit(solution)/shard_map/ppermute | solution.py:72
  287.1 28.8 %collective-permute-start.44 = (bf16[128,1536]{1,0:T(8,128)(2,1)}, bf16[128,1536]{1,0:T(8,128)(2,1)}, u32[]{:S(2)}, u32[]{:S(2)}) collective-permute-start(bf16[128,1536]{1,0:T(8,128)(2,1)} %get-tuple-element.130), channel_id=1, source_target_pairs={{0,3},{1,2},{2,1},{3,0},{4,7},{5,6},{6,5},{7,4},{8,11},{9,10},{10,... | collective-permute-start | bytes 1179656 | tf_op jit(solution)/shard_map/ppermute | solution.py:72
  306.9 20.6 %collective-permute-start.51 = (bf16[48,5184]{1,0:T(8,128)(2,1)}, bf16[48,5184]{1,0:T(8,128)(2,1)S(1)}, u32[]{:S(2)}, u32[]{:S(2)}) collective-permute-start(bf16[48,5184]{1,0:T(8,128)(2,1)} %pad_maximum_fusion.5), channel_id=1, source_target_pairs={{0,1},{1,0},{2,3},{3,2},{4,5},{5,4},{6,7},{7,6},{8,9},{9,8},{10,11... | collective-permute-start | bytes 1493000 | tf_op jit(solution)/shard_map/ppermute | solution.py:72
  313.2 24.3 %collective-permute-start.52 = (bf16[48,5184]{1,0:T(8,128)(2,1)}, bf16[48,5184]{1,0:T(8,128)(2,1)S(1)}, u32[]{:S(2)}, u32[]{:S(2)}) collective-permute-start(bf16[48,5184]{1,0:T(8,128)(2,1)} %pad_maximum_fusion.6), channel_id=1, source_target_pairs={{0,2},{1,3},{2,0},{3,1},{4,6},{5,7},{6,4},{7,5},{8,10},{9,11},{10,... | collective-permute-start | bytes 1493000 | tf_op jit(solution)/shard_map/ppermute | solution.py:72
  315.4 22.0 %collective-permute-start.53 = (bf16[48,5184]{1,0:T(8,128)(2,1)}, bf16[48,5184]{1,0:T(8,128)(2,1)S(1)}, u32[]{:S(2)}, u32[]{:S(2)}) collective-permute-start(bf16[48,5184]{1,0:T(8,128)(2,1)} %pad_maximum_fusion.7), channel_id=1, source_target_pairs={{0,3},{1,2},{2,1},{3,0},{4,7},{5,6},{6,5},{7,4},{8,11},{9,10},{10,... | collective-permute-start | bytes 1493000 | tf_op jit(solution)/shard_map/ppermute | solution.py:72
  (87 other events, 876.2 us)
Sparse Core Ops, SparseCore 0:
  151.0 53.3 reduce-scatter.5
  206.6 95.6 reduce-scatter.3
  304.7 51.5 reduce-scatter.7
